TPU v7x, 32 devices: a whole 2x2x4 slice. The times are simulated.
32 devices in a mesh: dp: 32 (over z, y, x, core).
Axes of the slice: x: 2, y: 2, z: 4, core: 2. Of those that a mesh axis runs over, the one named last changes fastest.
Arguments:
- tokens: bfloat16 [40960, 768], P('dp'), may hold values from -6 to 6
- cotangent: bfloat16 [40960, 768], P('dp'), may hold values from -6 to 6
- loss_mask: int32 [40960], P('dp'), may hold values from 0 to 1, as said below
- bucket_perm: int32 [32], replicated, may hold values from 0 to 31, as said below
- short_lengths: int32 [24, 3], replicated, may hold values from 1 to 512, 1024 in all within a row
- row_owner: int32 [40960], P('dp'), may hold values from 0 to 31, as said below
- row_slot: int32 [40960], P('dp'), may hold values from 0 to 2047, as said below
- first_gain: float32 [768], P('dp'), may hold values from 0.25 to 1.75
- first_shift: float32 [768], P('dp'), may hold values from -1.25 to 1.25
- second_gain: float32 [768], P('dp'), may hold values from 0.25 to 1.75
- second_shift: float32 [768], P('dp'), may hold values from -1.25 to 1.25
- project_weight: float32 [768, 2304], P('dp'), may hold values from -0.21875 to 0.21875
- project_bias: float32 [2304], P('dp'), may hold values from -1.25 to 1.25
- output_weight: float32 [768, 768], P('dp'), may hold values from -0.875 to 0.875
- output_bias: float32 [768], P('dp'), may hold values from -1.25 to 1.25
- up_weight: float32 [768, 3072], P('dp'), may hold values from -0.21875 to 0.21875
- up_bias: float32 [3072], P('dp'), may hold values from -1.25 to 1.25
- down_weight: float32 [3072, 768], P('dp'), may hold values from -0.109375 to 0.109375
- down_bias: float32 [768], P('dp'), may hold values from -1.25 to 1.25
Outputs:
- block_out: bfloat16 [40960, 768], P('dp')
- tokens_grad: bfloat16 [40960, 768], P('dp')
- first_gain_grad: float32 [768], P('dp')
- first_shift_grad: float32 [768], P('dp')
- second_gain_grad: float32 [768], P('dp')
- second_shift_grad: float32 [768], P('dp')
- project_weight_grad: float32 [768, 2304], P('dp')
- project_bias_grad: float32 [2304], P('dp')
- output_weight_grad: float32 [768, 768], P('dp')
- output_bias_grad: float32 [768], P('dp')
- up_weight_grad: float32 [768, 3072], P('dp')
- up_bias_grad: float32 [3072], P('dp')
- down_weight_grad: float32 [3072, 768], P('dp')
- down_bias_grad: float32 [768], P('dp')
Inputs may be any that keep to these rules, and one draw needn't show every extreme that they name: `bucket_perm`: each device owns exactly one bucket. `row_owner`: the tokens of one device go to every device: exactly 64 to the owner of each long bucket and 32 to the owner of each short bucket. `row_slot`: with row_owner, each place 0 to 2047 of a long bucket and 0 to 1023 of a short bucket is named by exactly one token. `loss_mask`: the first token of each device carries loss.
All inputs are finite; a program needn't handle non-finite values.
Results may differ from a plain program's by a relative error of at most 0.012.
The roundings to bfloat16 on the way count: a program that leaves them out, or rounds other values in their place, can miss the bound.
Values may be sent and summed in bfloat16 or wider, within the bound.
No kernel may reach another device: no remote copies, remote signals or barrier semaphores. Data moves between devices by JAX's collectives and lax.ppermute only.
A program may use at most 320 MiB of HBM per device.

v0:
```python
import jax
import jax.numpy as jnp
from jax import lax
from jax.sharding import PartitionSpec as P

D = 768
HEADS = 12
HEAD_DIM = 64
ROT = 16
LONG = 2048
QBLK = 512


epsilon = 1e-05
bfloat = jnp.bfloat16
single = jnp.float32


def over_rows(left, right):
    return lax.dot_general(left, right, (((0,), (0,)), ((), ())), preferred_element_type=single)


def against(left, right):
    return lax.dot_general(left, right, (((1,), (1,)), ((), ())), preferred_element_type=single)


def norm_parts(values, gain, shift):
    mean = jnp.mean(values, -1, keepdims=True)
    centred = values - mean
    spread = jnp.mean(centred * centred, -1, keepdims=True)
    factor = lax.rsqrt(spread + epsilon)
    scaled = centred * factor
    return (scaled * gain + shift, scaled, factor)


def norm_back(upper, scaled, factor, gain):
    gain_grad = jnp.sum(upper * scaled, 0)
    shift_grad = jnp.sum(upper, 0)
    inner = upper * gain
    lower = factor * (
        inner
        - jnp.mean(inner, -1, keepdims=True)
        - scaled * jnp.mean(inner * scaled, -1, keepdims=True)
    )
    return (lower, gain_grad, shift_grad)


def exact_gelu(values):
    return jax.nn.gelu(values, approximate=False)


def angles(position):
    freq = 10000.0 ** (-2.0 * jnp.arange(ROT // 2).astype(single) / ROT)
    phase = position.astype(single)[:, None] * freq[None, :]
    return (jnp.cos(phase), jnp.sin(phase))


def turn(values, cosine, sine, sign):
    count = values.shape[0]
    heads = values.reshape(count, HEADS, HEAD_DIM)
    half = ROT // 2
    first = heads[..., :half]
    second = heads[..., half:ROT]
    cosine = cosine[:, None]
    sine = sign * sine[:, None]
    turned = jnp.concatenate(
        [first * cosine - second * sine, second * cosine + first * sine, heads[..., ROT:]], -1
    )
    return turned.reshape(count, values.shape[1])


def bucket_of(owners, bucket_perm, short_lengths, devices):
    spread = jnp.arange(devices, dtype=jnp.int32)
    bucket = jnp.sum(jnp.where(bucket_perm[None, :] == owners[:, None], spread[None, :], 0), -1)
    long_count = devices // 4
    is_long = bucket < long_count
    picks = (
        bucket[:, None] - long_count == jnp.arange(short_lengths.shape[0], dtype=jnp.int32)[None, :]
    ).astype(jnp.int32)
    return (is_long, jnp.dot(picks, short_lengths))


def layout_of(slots, is_long, lengths):
    ends = jnp.cumsum(lengths, -1)
    docs = jnp.sum((slots[:, None] >= ends).astype(jnp.int32), -1)
    starts = ends - lengths
    offsets = jnp.sum(
        jnp.where(
            docs[:, None] == jnp.arange(lengths.shape[-1], dtype=jnp.int32)[None, :], starts, 0
        ),
        -1,
    )
    return (jnp.where(is_long, 0, docs), jnp.where(is_long, slots, slots - offsets))


def split_heads(part):
    return part.reshape(part.shape[0], HEADS, HEAD_DIM).transpose(1, 0, 2)


def join_heads(part):
    return part.transpose(1, 0, 2).reshape(part.shape[1], D)


def attend(mixed, docs):
    count = mixed.shape[0]
    queries = split_heads(mixed[:, :D])
    keys = split_heads(mixed[:, D : 2 * D])
    values = split_heads(mixed[:, 2 * D :])
    spots = jnp.arange(count, dtype=jnp.int32)
    score_scale = HEAD_DIM ** (-0.5)
    context_parts = []
    logsum_parts = []
    for block in range(count // QBLK):
        low_edge = block * QBLK
        top = low_edge + QBLK
        allowed = (docs[low_edge:top, None] == docs[None, :top]) & (
            spots[low_edge:top, None] >= spots[None, :top]
        )

        def one_head(parts):
            head_q, head_k, head_v = parts
            score = (
                jnp.einsum("qd,kd->qk", head_q, head_k, preferred_element_type=single) * score_scale
            )
            score = jnp.where(allowed, score, -jnp.inf)
            peak = jnp.max(score, -1, keepdims=True)
            expo = jnp.exp(score - peak)
            total = jnp.sum(expo, -1, keepdims=True)
            probs = (expo / total).astype(bfloat)
            return (
                jnp.einsum("qk,kd->qd", probs, head_v, preferred_element_type=single),
                peak[:, 0] + jnp.log(total[:, 0]),
            )

        part_context, part_logsum = lax.map(
            one_head, (queries[:, low_edge:top], keys[:, :top], values[:, :top])
        )
        context_parts.append(part_context)
        logsum_parts.append(part_logsum)
    context = join_heads(jnp.concatenate(context_parts, 1)).astype(bfloat)
    return (context, jnp.concatenate(logsum_parts, 1))


def attend_back(mixed, docs, logsum, dcontext, cosine, sine):
    count = mixed.shape[0]
    queries = split_heads(mixed[:, :D])
    keys = split_heads(mixed[:, D : 2 * D])
    values = split_heads(mixed[:, 2 * D :])
    upper = split_heads(dcontext)
    spots = jnp.arange(count, dtype=jnp.int32)
    score_scale = HEAD_DIM ** (-0.5)
    query_parts = []
    key_grad = jnp.zeros((HEADS, count, HEAD_DIM), single)
    value_grad = jnp.zeros((HEADS, count, HEAD_DIM), single)
    for block in range(count // QBLK):
        low_edge = block * QBLK
        top = low_edge + QBLK
        allowed = (docs[low_edge:top, None] == docs[None, :top]) & (
            spots[low_edge:top, None] >= spots[None, :top]
        )

        def one_head(parts):
            head_q, head_k, head_v, head_up, head_sum = parts
            score = (
                jnp.einsum("qd,kd->qk", head_q, head_k, preferred_element_type=single) * score_scale
            )
            probs = jnp.exp(jnp.where(allowed, score - head_sum[:, None], -jnp.inf))
            dprob = jnp.einsum("qd,kd->qk", head_up, head_v, preferred_element_type=single)
            delta = jnp.sum(probs * dprob, -1, keepdims=True)
            dscore = (probs * (dprob - delta)).astype(bfloat)
            grad_q = (
                jnp.einsum("qk,kd->qd", dscore, head_k, preferred_element_type=single) * score_scale
            )
            grad_k = (
                jnp.einsum("qk,qd->kd", dscore, head_q, preferred_element_type=single) * score_scale
            )
            grad_v = jnp.einsum(
                "qk,qd->kd", probs.astype(bfloat), head_up, preferred_element_type=single
            )
            return (grad_q, grad_k, grad_v)

        part_q, part_k, part_v = lax.map(
            one_head,
            (
                queries[:, low_edge:top],
                keys[:, :top],
                values[:, :top],
                upper[:, low_edge:top],
                logsum[:, low_edge:top],
            ),
        )
        query_parts.append(part_q)
        key_grad = key_grad.at[:, :top].add(part_k)
        value_grad = value_grad.at[:, :top].add(part_v)
    query_rows = turn(join_heads(jnp.concatenate(query_parts, 1)), cosine, sine, -1.0)
    key_rows = turn(join_heads(key_grad), cosine, sine, -1.0)
    return jnp.concatenate([query_rows, key_rows, join_heads(value_grad)], -1).astype(bfloat)


def scatter_rows(values, place, total, fill):
    return jnp.full((total,) + values.shape[1:], fill, values.dtype).at[place].set(values)


def body(
    tokens,
    cotangent,
    loss_mask,
    bucket_perm,
    short_lengths,
    row_owner,
    row_slot,
    first_gain,
    first_shift,
    second_gain,
    second_shift,
    project_weight,
    project_bias,
    output_weight,
    output_bias,
    up_weight,
    up_bias,
    down_weight,
    down_bias,
):
    devices = lax.axis_size("dp")
    position_self = lax.axis_index("dp")
    capacity = LONG
    pair = capacity // devices
    gathered = (
        lax.all_gather(first_gain.astype(bfloat), "dp", axis=0, tiled=True),
        lax.all_gather(first_shift.astype(bfloat), "dp", axis=0, tiled=True),
        lax.all_gather(second_gain.astype(bfloat), "dp", axis=0, tiled=True),
        lax.all_gather(second_shift.astype(bfloat), "dp", axis=0, tiled=True),
        lax.all_gather(project_weight.astype(bfloat), "dp", axis=0, tiled=True),
        lax.all_gather(project_bias.astype(bfloat), "dp", axis=0, tiled=True),
        lax.all_gather(output_weight.astype(bfloat), "dp", axis=0, tiled=True),
        lax.all_gather(output_bias.astype(bfloat), "dp", axis=0, tiled=True),
        lax.all_gather(up_weight.astype(bfloat), "dp", axis=0, tiled=True),
        lax.all_gather(up_bias.astype(bfloat), "dp", axis=0, tiled=True),
        lax.all_gather(down_weight.astype(bfloat), "dp", axis=0, tiled=True),
        lax.all_gather(down_bias.astype(bfloat), "dp", axis=0, tiled=True),
    )
    gain_one = gathered[0].astype(single)
    shift_one = gathered[1].astype(single)
    gain_two = gathered[2].astype(single)
    shift_two = gathered[3].astype(single)
    project_full = gathered[4]
    project_add = gathered[5].astype(single)
    output_full = gathered[6]
    output_add = gathered[7].astype(single)
    up_full = gathered[8]
    up_add = gathered[9].astype(single)
    down_full = gathered[10]
    down_add = gathered[11].astype(single)
    total_count = lax.psum(jnp.sum(loss_mask.astype(single)), "dp")
    scale = lax.rsqrt(total_count)
    tangent = cotangent * loss_mask.astype(bfloat)[:, None]
    owner_hot = (row_owner[:, None] == jnp.arange(devices, dtype=jnp.int32)[None, :]).astype(
        jnp.int32
    )
    order_rank = jnp.sum((jnp.cumsum(owner_hot, 0) - owner_hot) * owner_hot, -1)
    place = row_owner * pair + order_rank
    slot_send = scatter_rows(row_slot, place, capacity, capacity)
    self_long, self_lengths = bucket_of(
        jnp.reshape(position_self, (1,)), bucket_perm, short_lengths, devices
    )
    own_docs, own_position = layout_of(
        jnp.arange(capacity, dtype=jnp.int32), self_long, self_lengths
    )
    own_cos, own_sin = angles(own_position)

    def settle(received, slots):
        return (
            jnp.zeros((capacity,) + received.shape[1:], received.dtype)
            .at[slots]
            .set(received, mode="drop")
        )

    def collect(values, slots):
        return values[jnp.minimum(slots, capacity - 1)]

    moved = (
        lax.all_to_all(
            scatter_rows(tokens, place, capacity, 0), "dp", split_axis=0, concat_axis=0, tiled=True
        ),
        lax.all_to_all(
            scatter_rows(tangent, place, capacity, 0), "dp", split_axis=0, concat_axis=0, tiled=True
        ),
        lax.all_to_all(slot_send, "dp", split_axis=0, concat_axis=0, tiled=True),
    )
    slot_recv = moved[2]
    rows = settle(moved[0], slot_recv).astype(single)
    tangent_own = settle(moved[1], slot_recv)
    normed, scaled, factor = norm_parts(rows, gain_one, shift_one)
    normed_b = normed.astype(bfloat)
    mixed = jnp.dot(normed_b, project_full, preferred_element_type=single) + project_add
    queries = turn(mixed[:, :D], own_cos, own_sin, 1.0)
    keys = turn(mixed[:, D : 2 * D], own_cos, own_sin, 1.0)
    mixed_b = jnp.concatenate([queries, keys, mixed[:, 2 * D :]], -1).astype(bfloat)
    mixed_b, front_saved = (mixed_b, (normed_b, scaled, factor))
    context_b, logsum = attend(mixed_b, own_docs)
    attended = jnp.dot(context_b, output_full, preferred_element_type=single) + output_add
    normed, scaled, factor = norm_parts(rows, gain_two, shift_two)
    normed_b = normed.astype(bfloat)
    hidden = jnp.dot(normed_b, up_full, preferred_element_type=single) + up_add
    active_b = exact_gelu(hidden).astype(bfloat)
    result = jnp.dot(active_b, down_full, preferred_element_type=single) + down_add
    feed = result
    out_own = (rows + attended + feed).astype(bfloat)
    normed_two, scaled_two, factor_two, hidden, active_b = (
        normed_b,
        scaled,
        factor,
        hidden,
        active_b,
    )
    down_grad = over_rows(active_b, tangent_own)
    bias_grad = jnp.sum(tangent_own.astype(single), 0)
    output_grad = over_rows(context_b, tangent_own)
    above = against(tangent_own, down_full)
    slope = jax.vjp(exact_gelu, hidden)[1](above)[0].astype(bfloat)
    up_grad = over_rows(normed_two, slope)
    up_add_grad = jnp.sum(slope.astype(single), 0)
    lower_two, gain_two_grad, shift_two_grad = norm_back(
        against(slope, up_full), scaled_two, factor_two, gain_two
    )
    feed = (gain_two_grad, shift_two_grad, up_grad, up_add_grad, down_grad, bias_grad)
    dcontext_b = against(tangent_own, output_full).astype(bfloat)
    lower_two, feed_grads, output_grad, bias_grad, dcontext_b = (
        lower_two,
        feed,
        output_grad,
        bias_grad,
        dcontext_b,
    )
    dmixed_b = attend_back(mixed_b, own_docs, logsum, dcontext_b, own_cos, own_sin)
    normed_one, scaled_one, factor_one = front_saved
    project_grad = over_rows(normed_one, dmixed_b)
    project_add_grad = jnp.sum(dmixed_b.astype(single), 0)
    lower_one, gain_one_grad, shift_one_grad = norm_back(
        against(dmixed_b, project_full), scaled_one, factor_one, gain_one
    )
    lower_one, gain_one_grad, shift_one_grad, project_grad, project_add_grad = (
        lower_one,
        gain_one_grad,
        shift_one_grad,
        project_grad,
        project_add_grad,
    )
    grad_own = (tangent_own.astype(single) + lower_one + lower_two).astype(bfloat)
    returned = (
        lax.all_to_all(collect(out_own, slot_recv), "dp", split_axis=0, concat_axis=0, tiled=True),
        lax.all_to_all(collect(grad_own, slot_recv), "dp", split_axis=0, concat_axis=0, tiled=True),
    )
    block_out = returned[0][place]
    tokens_grad = returned[1][place]
    shards = (
        lax.psum_scatter(gain_one_grad, "dp", scatter_dimension=0, tiled=True),
        lax.psum_scatter(shift_one_grad, "dp", scatter_dimension=0, tiled=True),
        lax.psum_scatter(feed_grads[0], "dp", scatter_dimension=0, tiled=True),
        lax.psum_scatter(feed_grads[1], "dp", scatter_dimension=0, tiled=True),
        lax.psum_scatter(project_grad, "dp", scatter_dimension=0, tiled=True),
        lax.psum_scatter(project_add_grad, "dp", scatter_dimension=0, tiled=True),
        lax.psum_scatter(output_grad, "dp", scatter_dimension=0, tiled=True),
        lax.psum_scatter(bias_grad, "dp", scatter_dimension=0, tiled=True),
        lax.psum_scatter(feed_grads[2], "dp", scatter_dimension=0, tiled=True),
        lax.psum_scatter(feed_grads[3], "dp", scatter_dimension=0, tiled=True),
        lax.psum_scatter(feed_grads[4], "dp", scatter_dimension=0, tiled=True),
        lax.psum_scatter(feed_grads[5], "dp", scatter_dimension=0, tiled=True),
    )
    return (
        block_out,
        tokens_grad,
        shards[0] * scale,
        shards[1] * scale,
        shards[2] * scale,
        shards[3] * scale,
        shards[4] * scale,
        shards[5] * scale,
        shards[6] * scale,
        shards[7] * scale,
        shards[8] * scale,
        shards[9] * scale,
        shards[10] * scale,
        shards[11] * scale,
    )


def solution(mesh):
    placed = (
        P("dp", None),
        P("dp", None),
        P("dp"),
        P(),
        P(),
        P("dp"),
        P("dp"),
        P("dp"),
        P("dp"),
        P("dp"),
        P("dp"),
        P("dp", None),
        P("dp"),
        P("dp", None),
        P("dp"),
        P("dp", None),
        P("dp"),
        P("dp", None),
        P("dp"),
    )
    return jax.shard_map(
        body,
        mesh=mesh,
        in_specs=placed,
        out_specs=(
            P("dp", None),
            P("dp", None),
            P("dp"),
            P("dp"),
            P("dp"),
            P("dp"),
            P("dp", None),
            P("dp"),
            P("dp", None),
            P("dp"),
            P("dp", None),
            P("dp"),
            P("dp", None),
            P("dp"),
        ),
        check_vma=False,
    )
```

profile of v0, /device:TPU:0, one launch (start us, length us, event | category | flops | bytes accessed | tf_op | source)
XLA Modules:
  0.0 1732.3 jit_solution(8718023516212438470)
XLA Ops:
  54.1 15.4 scatter_custom_fusion.3
  69.6 66.0 %all-to-all-done.1 = bf16[32,64,768]{2,1,0:T(8,128)(2,1)S(1)} async-done(((bf16[32,64,768]{2,1,0:T(8,128)(2,1)}), bf16[32,64,768]{2,1,0:T(8,128)(2,1)S(1)}, u32[]{:S(2)}, u32[]{:S(2)}) %all-to-all-start.1) | async-done | bytes 3145760 | tf_op jit(solution)/shard_map/all_to_all | solution.py:283
  146.8 110.3 %all-reduce.18 = (bf16[2304]{0:T(1024)(128)(2,1)S(1)}, bf16[768]{0:T(1024)(128)(2,1)S(1)}, bf16[768]{0:T(1024)(128)(2,1)S(1)}, bf16[768]{0:T(1024)(128)(2,1)S(1)...) all-reduce(bf16[2304]{0:T(1024)(128)(2,1)S(1)} %dynamic-update-slic, ...), channel_id=1, replica_groups=mesh['dp'=32] {'dp'}, use_global_device_ids=true, to_apply=%add.4 | all-reduce | flops 9984 | bytes 39936
  278.9 12.2 scatter_custom_fusion.4
  297.7 14.9 copy.124
  408.2 49.6 %while.122 = (s32[]{:T(128)}, bf16[12,512,64]{1,2,0:T(8,128)(2,1)S(1)}, f32[12,512]{1,0:T(8,128)}, bf16[12,512,64]{2,1,0:T(8,128)(2,1)}, bf16[12,512,64]{2,1,0:T...) while((s32[]{:T(128)}, ...), condition=%wide.region_15.16_spmd.clone, body=%wide.region_12.15_spmd.clone.sunk | while | flops 69991936 | bytes 3700849 | solution.py:135
  467.1 46.1 %while.123 = (s32[]{:T(128)}, bf16[12,512,64]{1,2,0:T(8,128)(2,1)S(1)}, f32[12,512]{1,0:T(8,128)S(1)}, bf16[12,512,64]{2,1,0:T(8,128)(2,1)}, bf16[12,1024,64]{2,...) while((s32[]{:T(128)}, ...), condition=%wide.region_19.20_spmd.clone, body=%wide.region_16.19_spmd.clone.sunk | while | flops 139984384 | bytes 7112833 | solution.py:135
  514.6 116.6 %while.127 = (s32[]{:T(128)}, f32[12,512,64]{1,2,0:T(8,128)}, f32[12,1024,64]{1,2,0:T(8,128)}, f32[12,1024,64]{1,2,0:T(8,128)}, bf16[12,512,64]{2,1,0:T(8,128)(2...) while((s32[]{:T(128)}, f32[12,512,64]{1,2,0:T(8,128)}, ...), condition=%wide.region_35.36_spmd.clone, body=%wide.region_33.35_spmd.clone.sunk | while | flops 341933568 | bytes 17722512 | solution.py:182
  635.2 53.9 %while.124 = (s32[]{:T(128)}, bf16[12,512,64]{1,2,0:T(8,128)(2,1)S(1)}, f32[12,512]{1,0:T(8,128)S(1)}, bf16[12,512,64]{2,1,0:T(8,128)(2,1)}, bf16[12,1536,64]{2,...) while((s32[]{:T(128)}, ...), condition=%wide.region_23.24_spmd.clone, body=%wide.region_20.23_spmd.clone.sunk | while | flops 209976832 | bytes 10524801 | solution.py:135
  690.0 122.5 %while.128 = (s32[]{:T(128)}, f32[12,512,64]{1,2,0:T(8,128)S(1)}, f32[12,1536,64]{1,2,0:T(8,128)}, f32[12,1536,64]{1,2,0:T(8,128)}, bf16[12,512,64]{2,1,0:T(8,12...) while((s32[]{:T(128)}, f32[12,512,64]{1,2,0:T(8,128)S(1)}, ...), condition=%wide.region_38.39_spmd.clone, body=%wide.region_36.38_spmd.clone.sunk | while | flops 512884224 | bytes 26246288 | solution.py:182
  813.6 63.2 %while.125 = (s32[]{:T(128)}, bf16[12,512,64]{1,2,0:T(8,128)(2,1)S(1)}, f32[12,512]{1,0:T(8,128)S(1)}, bf16[12,512,64]{2,1,0:T(8,128)(2,1)}, bf16[12,2048,64]{2,...) while((s32[]{:T(128)}, ...), condition=%wide.region_27.28_spmd.clone, body=%wide.region_24.27_spmd.clone.sunk | while | flops 279969280 | bytes 13928569 | solution.py:135
  877.1 138.8 %while.129 = (s32[]{:T(128)}, f32[12,512,64]{1,2,0:T(8,128)S(1)}, f32[12,2048,64]{1,2,0:T(8,128)}, f32[12,2048,64]{1,2,0:T(8,128)}, bf16[12,512,64]{2,1,0:T(8,12...) while((s32[]{:T(128)}, f32[12,512,64]{1,2,0:T(8,128)S(1)}, ...), condition=%wide.region_41.42_spmd.clone, body=%wide.region_39.41_spmd.clone.sunk | while | flops 683834880 | bytes 34761864 | solution.py:182
  1020.1 111.7 %while.126 = (s32[]{:T(128)}, f32[12,512,64]{1,2,0:T(8,128)}, f32[12,512,64]{1,2,0:T(8,128)}, f32[12,512,64]{1,2,0:T(8,128)}, bf16[12,512,64]{2,1,0:T(8,128)(2,1...) while((s32[]{:T(128)}, f32[12,512,64]{1,2,0:T(8,128)}, ...), condition=%wide.region_32.33_spmd.clone, body=%wide.region_30.32_spmd.clone.sunk | while | flops 170982912 | bytes 9198721 | solution.py:182
  1173.6 15.5 fusion.237
  1189.8 70.3 %multiply_convert_fusion.4 = (bf16[2048,3072]{1,0:T(8,128)(2,1)}, f32[2048,3072]{1,0:T(8,128)}, f32[2048,3072]{1,0:T(8,128)}) fusion(f32[3072]{0:T(1024)S(1)} %copy-done.52, bf16[768,3072]{1,0:T(8,128)(2,1)} %all-gather.9.cloned.1.call-done, bf16[2048,768]{1,0:T(8,128)(2,1)S(1)} %copy-done.3, f32[768]{0:T(1024)S(1)} %copy-done.54, f32[768]{0:T(1024)S(1)} %copy-done.51, ...), kind=kOutput, calls=%fused_computation.229 | convolution fusion | flops 10088349696 | bytes 70813696 | tf_op jit(solution)/shard_map/dot_general | solution.py:305
  1260.1 35.1 %convert_reduce_fusion = (f32[3072]{0:T(1024)S(1)}, bf16[2048,3072]{1,0:T(8,128)(2,1)}) fusion(f32[2048,3072]{1,0:T(8,128)} %get-tuple-element.1187, bf16[2048,768]{1,0:T(8,128)(2,1)} %scatter_custom_fusion.4, bf16[3072,768]{1,0:T(8,128)(2,1)} %all-gather.11.cloned.1.call-done, f32[2048,3072]{1,0:T(8,128)} %get-tuple-element.1241, f32[3072]{0:T(1024)S(1)} %copy-done.52), kind=kOutput, calls=%fused_computation.227 | convolution fusion | flops 9770628096 | bytes 70803456 | tf_op jit(solution)/shard_map/dot_general | solution.py:24
  1295.2 16.7 fusion.233
  1318.3 14.5 fusion.208
  1346.7 15.7 fusion.254
  1362.5 16.2 fusion.252
  1378.6 17.7 %fusion.204 = (f32[768]{0:T(1024)S(1)}, f32[2048]{0:T(1024)S(1)}, f32[2048]{0:T(1024)S(1)}, f32[768]{0:T(1024)S(1)}, f32[768]{0:T(1024)S(1)}, /*index=5*/f32[204...) fusion(bf16[2048,768]{1,0:T(8,128)(2,1)S(1)} %copy-done.5, f32[2048]{0:T(1024)S(1)} %copy-done.42, ...), kind=kOutput, calls=%fused_computation.273 | convolution fusion | flops 7302795264 | bytes 28772352 | tf_op jit(solution)/shard_map/dot_general | solution.py:24
  1414.3 17.3 all-to-all-done.2
  1441.1 112.2 %all-reduce.17 = (f32[768]{0:T(1024)S(1)}, f32[]{:T(128)}, f32[768]{0:T(1024)S(1)}, f32[768]{0:T(1024)S(1)}, f32[768]{0:T(1024)S(1)}, /*index=5*/f32[2304]{0:T(1024)S(1)}, f32[768]{0:T(1024)S(1)}, f32[3072]{0:T(1024)S(1)}) all-reduce(f32[768]{0:T(1024)S(1)} %get-tuple-element.988, ...), channel_id=2, replica_groups=mesh['dp'=32] {'dp'}, use_global_device_ids=true, to_apply=%region_47.48.clone | all-reduce | flops 9217 | bytes 73736
  1583.2 139.8 %reduce-scatter.11.cloned.1.call-done = f32[96,768]{1,0:T(8,128)} async-done(((f32[3072,768]{1,0:T(8,128)}), f32[96,768]{1,0:T(8,128)}) %reduce-scatter.11.cloned.1.call-update) | async-done | bytes 294928 | tf_op jit(solution)/shard_map/reduce_scatter | solution.py:368
  (953 shorter events, 1022.4 us)
Async XLA Ops:
  7.2 137.4 %copy-start = (s32[24,3]{0,1:T(4,128)S(1)}, s32[24,3]{0,1:T(4,128)}, u32[]{:S(2)}) copy-start(s32[24,3]{0,1:T(4,128)} %param.59) | copy-start | bytes 868
  7.2 283.9 %all-gather.7.cloned.1.call-start = ((), (), s32[]{:S(2)}) async-start(), calls=%async_computation.10 | async-start | bytes 1216512 | tf_op jit(solution)/shard_map/all_gather | solution.py:236
  8.8 309.6 %all-gather.5.cloned.1.call-start = ((), (), s32[]{:S(2)}) async-start(), calls=%async_computation.9 | async-start | bytes 3649536 | tf_op jit(solution)/shard_map/all_gather | solution.py:234
  10.4 1178.8 %all-gather.9.cloned.1.call-start = ((), (), s32[]{:S(2)}) async-start(), calls=%async_computation.11 | async-start | bytes 4866048 | tf_op jit(solution)/shard_map/all_gather | solution.py:238
  30.1 18.1 %all-to-all-start = ((s32[32,64,1]{1,2,0:T(1,128)}), s32[32,64,1]{1,2,0:T(1,128)S(1)}, u32[]{:S(2)}, u32[]{:S(2)}) async-start(s32[32,64,1]{1,2,0:T(1,128)} %bitcast.3), calls=%async_computation | async-start | bytes 32768 | tf_op jit(solution)/shard_map/all_to_all | solution.py:289
  48.3 87.3 %all-to-all-start.1 = ((bf16[32,64,768]{2,1,0:T(8,128)(2,1)}), bf16[32,64,768]{2,1,0:T(8,128)(2,1)S(1)}, u32[]{:S(2)}, u32[]{:S(2)}) async-start(bf16[32,64,768]{2,1,0:T(8,128)(2,1)} %bitcast.5), calls=%async_computation.1 | async-start | bytes 6291456 | tf_op jit(solution)/shard_map/all_to_all | solution.py:283
  69.6 70.4 %copy-start.36 = (f32[96,768]{1,0:T(8,128)S(1)}, f32[96,768]{1,0:T(8,128)}, u32[]{:S(2)}) copy-start(f32[96,768]{1,0:T(8,128)} %param.72) | copy-start | bytes 884740
  135.6 143.3 %all-to-all-start.3 = ((bf16[32,64,768]{2,1,0:T(8,128)(2,1)}), bf16[32,64,768]{2,1,0:T(8,128)(2,1)}, u32[]{:S(2)}, u32[]{:S(2)}) async-start(bf16[32,64,768]{2,1,0:T(8,128)(2,1)} %bitcast.23), calls=%async_computation.3 | async-start | bytes 6291456 | tf_op jit(solution)/shard_map/all_to_all | solution.py:286
  139.9 1120.2 %all-gather.11.cloned.1.call-start = ((), (), s32[]{:S(2)}) async-start(), calls=%async_computation.12 | async-start | bytes 4866048 | tf_op jit(solution)/shard_map/all_gather | solution.py:240
  140.7 1416.9 %reduce-scatter.7.cloned.1.call-start = ((), (), s32[]{:S(2)}) async-start(), calls=%async_computation.14 | async-start | bytes 2433024 | tf_op jit(solution)/shard_map/reduce_scatter | solution.py:364
  257.1 61.3 %copy-start.48 = (f32[768]{0:T(1024)}, f32[768]{0:T(1024)S(1)}, u32[]{:S(2)}) copy-start(f32[768]{0:T(1024)S(1)} %convert_element_type.174) | copy-start | bytes 9220
  257.7 60.7 %copy-start.55 = (f32[768]{0:T(1024)}, f32[768]{0:T(1024)S(1)}, u32[]{:S(2)}) copy-start(f32[768]{0:T(1024)S(1)} %convert_element_type.176) | copy-start | bytes 9220
  514.6 116.6 %slice-start.2 = ((bf16[12,2048,64]{1,2,0:T(8,128)(2,1)}), bf16[12,1536,64]{1,2,0:T(8,128)(2,1)S(1)}, s32[]{:S(2)}) async-start(bf16[12,2048,64]{1,2,0:T(8,128)(2,1)} %copy-done.6), calls=%async_computation.19 | async-start | bytes 4718592 | tf_op jit(solution)/shard_map/slice | solution.py:136
  689.3 123.2 %copy-start.8 = (bf16[12,512,64]{1,2,0:T(8,128)(2,1)S(1)}, bf16[12,512,64]{1,2,0:T(8,128)(2,1)}, u32[]{:S(2)}) copy-start(bf16[12,512,64]{1,2,0:T(8,128)(2,1)} %copy-done.7) | copy-start | bytes 2359300
  689.3 123.2 %copy-start.62 = (s32[512]{0:T(512)S(1)}, s32[512]{0:T(512)}, u32[]{:S(2)}) copy-start(s32[512]{0:T(512)} %iota_add_fusion.2) | copy-start | bytes 6148
  689.3 123.2 %copy-start.67 = (s32[512]{0:T(512)S(1)}, s32[512]{0:T(512)}, u32[]{:S(2)}) copy-start(s32[512]{0:T(512)} %get-tuple-element.2068) | copy-start | bytes 6148
  1020.1 111.7 %copy-start.18 = (f32[12,512,64]{1,2,0:T(8,128)S(1)}, f32[12,512,64]{1,2,0:T(8,128)}, u32[]{:S(2)}) copy-start(f32[12,512,64]{1,2,0:T(8,128)} %get-tuple-element.501) | copy-start | bytes 4718596
  1159.1 412.9 %reduce-scatter.5.cloned.1.call-start = ((), (), s32[]{:S(2)}) async-start(), calls=%async_computation.13 | async-start | bytes 7299072 | tf_op jit(solution)/shard_map/reduce_scatter | solution.py:362
  1189.2 392.4 %reduce-scatter.9.cloned.1.call-start = ((), (), s32[]{:S(2)}) async-start(), calls=%async_computation.15 | async-start | bytes 9732096 | tf_op jit(solution)/shard_map/reduce_scatter | solution.py:366
  1342.2 89.3 %all-to-all-start.2 = ((bf16[32,64,768]{2,1,0:T(8,128)(2,1)}), bf16[32,64,768]{2,1,0:T(8,128)(2,1)}, u32[]{:S(2)}, u32[]{:S(2)}) async-start(bf16[32,64,768]{2,1,0:T(8,128)(2,1)} %bitcast.473), calls=%async_computation.2 | async-start | bytes 6291456 | tf_op jit(solution)/shard_map/all_to_all | solution.py:352
  1346.6 376.4 %reduce-scatter.11.cloned.1.call-start = ((), (), s32[]{:S(2)}) async-start(), calls=%async_computation.16 | async-start | bytes 9732096 | tf_op jit(solution)/shard_map/reduce_scatter | solution.py:368
  1431.6 135.6 %all-to-all-start.4 = ((bf16[32,64,768]{2,1,0:T(8,128)(2,1)}), bf16[32,64,768]{2,1,0:T(8,128)(2,1)S(1)}, u32[]{:S(2)}, u32[]{:S(2)}) async-start(bf16[32,64,768]{2,1,0:T(8,128)(2,1)} %bitcast.472), calls=%async_computation.4 | async-start | bytes 6291456 | tf_op jit(solution)/shard_map/all_to_all | solution.py:353
  1554.0 170.7 %copy-start.70 = (f32[24]{0:T(128)}, f32[24]{0:T(128)S(1)}, u32[]{:S(2)}) copy-start(f32[24]{0:T(128)S(1)} %dynamic-slice_multiply_fusion.1) | copy-start | bytes 292
  1567.2 158.1 %copy-start.1 = (s32[24,3]{0,1:T(4,128)S(1)}, s32[24,3]{0,1:T(4,128)}, u32[]{:S(2)}) copy-start(s32[24,3]{0,1:T(4,128)} %param.59) | copy-start | bytes 868
  (78 other events, 500.5 us)
Sparse Core Ops, SparseCore 0:
  11.5 63.2 all-gather.6
  78.3 74.2 all-gather.4
  156.1 81.9 all-gather.8
  241.4 62.7 all-gather.10
  1159.2 98.9 reduce-scatter.6
  1264.7 152.1 reduce-scatter.4
  1422.8 158.7 reduce-scatter.8
  1588.4 134.5 reduce-scatter.10
where the time goes:
time: 1750 us; the launch traced here: 1730 us
  matrix products  860 us (49%)
  local copies, waits for them, and re-layouts  237 us (14%)
  waiting for transfers between devices  231 us (13%)
  blocking collectives  223 us (13%)
  other arithmetic  136 us (8%)
  starting transfers between devices  26.1 us (1%)
  between operations  17.5 us (1%)
    unnamed x2, blocking collectives  223 us
    dot_general x96, matrix products, one_head(): jnp.einsum('qd,kd->qk', head_q, head_k, preferred_element_type=single)  196 us
    reduce_scatter x1, waiting for transfers between devices, body(): lax.psum_scatter(feed_grads[4], 'dp', scatter_dimension=0, tiled=True)  140 us
    dot_general x48, matrix products, one_head(): jnp.einsum('qk,qd->kd', probs.astype(bfloat), head_up, preferred_element_...  97.8 us
    dot_general x48, matrix products, one_head(): jnp.einsum('qk,qd->kd', dscore, head_q, preferred_element_type=single)  97.5 us
    dot_general x48, matrix products, one_head(): jnp.einsum('qk,kd->qd', dscore, head_k, preferred_element_type=single)  87.4 us
    dot_general x48, matrix products, one_head(): jnp.einsum('qk,kd->qd', probs, head_v, preferred_element_type=single)  80.6 us
    dot_general x4, matrix products, against(): lax.dot_general(left, right, (((1,), (1,)), ((), ())), preferred_element_...  75.5 us
  transfers between devices with their start and end apart: 13, of which 4 were waited for; matrix products, arithmetic and copies ran while one was open for 70% of the time, Pallas kernels for 0%

commit v1 on v0

v1 whole, which is shorter than its diff:
```python
import functools
import math

import jax
import jax.numpy as jnp
from jax import lax
from jax.experimental import pallas as pl
from jax.experimental.pallas import tpu as pltpu
from jax.sharding import PartitionSpec as P

D = 768
HEADS = 12
HEAD_DIM = 64
ROT = 16
FF = 3072
LONG = 2048
SHORT_TOK = 1024
TOTAL = 3 * SHORT_TOK
BLK = 256
NH = HEADS // 2
HW = NH * HEAD_DIM
PART = SHORT_TOK // 2
MIB = 2**20

epsilon = 1e-05
bfloat = jnp.bfloat16
single = jnp.float32


def dot(left, right):
    return jnp.dot(left, right, preferred_element_type=single)


def over_rows(left, right):
    return lax.dot_general(left, right, (((0,), (0,)), ((), ())), preferred_element_type=single)


def against(left, right):
    return lax.dot_general(left, right, (((1,), (1,)), ((), ())), preferred_element_type=single)


def norm_stats(values):
    mean = jnp.mean(values, -1, keepdims=True)
    centred = values - mean
    spread = jnp.mean(centred * centred, -1, keepdims=True)
    factor = lax.rsqrt(spread + epsilon)
    return (centred * factor, factor)


def norm_back(upper, scaled, factor, gain):
    gain_grad = jnp.sum(upper * scaled, 0)
    shift_grad = jnp.sum(upper, 0)
    inner = upper * gain
    lower = factor * (
        inner
        - jnp.mean(inner, -1, keepdims=True)
        - scaled * jnp.mean(inner * scaled, -1, keepdims=True)
    )
    return (lower, gain_grad, shift_grad)


def params(mib):
    return pltpu.CompilerParams(vmem_limit_bytes=mib * MIB)


def whole(shape):
    return pl.BlockSpec(shape, lambda *_: (0,) * len(shape))


def feed_kernel(
    tok, tan, gain, shift, up, up_add, down, feed, lower, g_up, g_up_add, g_down, normed, act, slope
):
    step = pl.program_id(0)
    rows = tok.shape[0]
    chunk = rows // 2
    root = 1.0 / math.sqrt(2.0)
    dens = 1.0 / math.sqrt(2.0 * math.pi)

    @pl.when(step == 0)
    def _():
        def one(i, carry):
            r = pl.ds(pl.multiple_of(i * BLK, BLK), BLK)
            scaled, _ = norm_stats(tok[r, :].astype(single))
            normed[r, :] = (scaled * gain[...] + shift[...]).astype(bfloat)
            return carry

        lax.fori_loop(0, rows // BLK, one, 0)

    bias_sum = jnp.zeros(g_up_add.shape, single)
    for i in range(2):
        r = pl.ds(i * chunk, chunk)
        hidden = dot(normed[r, :], up[...]) + up_add[...]
        above = against(tan[r, :], down[...])
        phi = 0.5 * (1.0 + lax.erf(hidden * root))
        active = (hidden * phi).astype(bfloat)
        sl = (above * (phi + hidden * (dens * jnp.exp(-0.5 * hidden * hidden)))).astype(bfloat)
        act[r, :] = active
        slope[r, :] = sl
        bias_sum = bias_sum + jnp.sum(sl.astype(single), 0, keepdims=True)
        part_feed = dot(active, down[...])
        part_lower = against(sl, up[...])

        @pl.when(step == 0)
        def _():
            feed[r, :] = part_feed
            lower[r, :] = part_lower

        @pl.when(step > 0)
        def _():
            feed[r, :] += part_feed
            lower[r, :] += part_lower

    g_up_add[...] = bias_sum
    g_up[...] = over_rows(normed[...], slope[...])
    g_down[...] = over_rows(act[...], tan[...])


def feed_forward(tok, tan, gain, shift, up, up_add, down):
    rows = tok.shape[0]
    width = 768
    cols = pl.BlockSpec((D, width), lambda j: (0, j))
    line = pl.BlockSpec((1, width), lambda j: (0, j))
    tall = pl.BlockSpec((width, D), lambda j: (j, 0))
    return pl.pallas_call(
        feed_kernel,
        grid=(FF // width,),
        in_specs=[whole((rows, D)), whole((rows, D)), whole((1, D)), whole((1, D)), cols, line, tall],
        out_specs=[whole((rows, D)), whole((rows, D)), cols, line, tall],
        out_shape=[
            jax.ShapeDtypeStruct((rows, D), single),
            jax.ShapeDtypeStruct((rows, D), single),
            jax.ShapeDtypeStruct((D, FF), single),
            jax.ShapeDtypeStruct((1, FF), single),
            jax.ShapeDtypeStruct((FF, D), single),
        ],
        scratch_shapes=[
            pltpu.VMEM((rows, D), bfloat),
            pltpu.VMEM((rows, width), bfloat),
            pltpu.VMEM((rows, width), bfloat),
        ],
        compiler_params=params(56),
        cost_estimate=pl.CostEstimate(
            flops=12 * rows * D * FF, bytes_accessed=50 * MIB, transcendentals=2 * rows * FF
        ),
        name="feed_forward",
    )(tok, tan, gain, shift, up, up_add, down)


def pick_rows(places, own, other, low, span, first):
    spot = lax.broadcasted_iota(jnp.int32, (BLK, PART), 0) + first

    def part(k):
        mine = jnp.where(places[k] == spot, 1.0, 0.0).astype(bfloat)
        theirs = jnp.where(places[k + 3] == spot, 1.0, 0.0).astype(bfloat)
        return dot(mine, own[k]) + dot(theirs, other[k])

    return part


def turn_lanes(values, cosine, sine):
    lane = lax.broadcasted_iota(jnp.int32, values.shape, 1)
    swapped = jnp.where(
        lax.rem(lane, ROT) < ROT // 2, pltpu.roll(values, 128 - ROT // 2, 1), pltpu.roll(values, ROT // 2, 1)
    )
    return values * cosine + swapped * sine


def front_kernel(
    meta, places, own, other, gain, shift, weight, add, cosine, sine, normed, q, k, kt, v, vt, rows
):
    i = pl.program_id(0)
    active = meta[2, i]

    @pl.when(active > 0)
    def _():
        part = pick_rows(places, own, other, None, None, i * BLK)
        low = meta[3, i]
        rows[...] = part(low)

        @pl.when(meta[4, i] > 1)
        def _():
            rows[...] += part(low + 1)

        scaled, _ = norm_stats(rows[...])
        n = (scaled * gain[...] + shift[...]).astype(bfloat)
        normed[...] = n
        for s in range(3):
            c = slice(s * HW, (s + 1) * HW)
            mixed = dot(n, weight[:, c]) + add[:, c]
            if s < 2:
                mixed = jnp.concatenate(
                    [
                        turn_lanes(mixed[:, p : p + 128], cosine[...], sine[...])
                        for p in range(0, HW, 128)
                    ],
                    1,
                )
            low_mixed = mixed.astype(bfloat)
            if s == 0:
                q[...] = low_mixed * HEAD_DIM ** (-0.5)
            elif s == 1:
                k[...] = low_mixed
                kt[...] = low_mixed.T
            else:
                v[...] = low_mixed
                vt[...] = low_mixed.T

    @pl.when(active == 0)
    def _():
        for ref in (normed, q, k, kt, v, vt):
            ref[...] = jnp.zeros_like(ref)


def front(meta, places, own, other, gain, shift, weight, add, cosine, sine):
    tall = lambda width: pl.BlockSpec((BLK, width), lambda i, m: (i, 0))
    flat = pl.BlockSpec((HW, BLK), lambda i, m: (0, i))
    out = lambda *shape: jax.ShapeDtypeStruct(shape, bfloat)
    return pl.pallas_call(
        front_kernel,
        grid_spec=pltpu.PrefetchScalarGridSpec(
            num_scalar_prefetch=1,
            grid=(TOTAL // BLK,),
            in_specs=[
                whole((6, 1, PART)),
                whole((3, PART, D)),
                whole((3, PART, D)),
                whole((1, D)),
                whole((1, D)),
                whole((D, 3 * HW)),
                whole((1, 3 * HW)),
                tall(128),
                tall(128),
            ],
            out_specs=[tall(D), tall(HW), tall(HW), flat, tall(HW), flat],
            scratch_shapes=[pltpu.VMEM((BLK, D), single)],
        ),
        out_shape=[
            out(TOTAL, D),
            out(TOTAL, HW),
            out(TOTAL, HW),
            out(HW, TOTAL),
            out(TOTAL, HW),
            out(HW, TOTAL),
        ],
        compiler_params=params(40),
        cost_estimate=pl.CostEstimate(
            flops=2 * TOTAL * D * (3 * HW + 1024), bytes_accessed=24 * MIB, transcendentals=0
        ),
        name="front",
    )(meta, places, own, other, gain, shift, weight, add, cosine, sine)


def settle_kernel(meta, places, own, other, out, rows):
    i = pl.program_id(0)

    @pl.when(meta[2, i] > 0)
    def _():
        part = pick_rows(places, own, other, None, None, i * BLK)
        low = meta[3, i]
        rows[...] = part(low)

        @pl.when(meta[4, i] > 1)
        def _():
            rows[...] += part(low + 1)

        out[...] = rows[...].astype(bfloat)

    @pl.when(meta[2, i] == 0)
    def _():
        out[...] = jnp.zeros_like(out)


def settle(meta, places, own, other):
    width = own.shape[-1]
    return pl.pallas_call(
        settle_kernel,
        grid_spec=pltpu.PrefetchScalarGridSpec(
            num_scalar_prefetch=1,
            grid=(TOTAL // BLK,),
            in_specs=[whole((6, 1, PART)), whole((3, PART, width)), whole((3, PART, width))],
            out_specs=pl.BlockSpec((BLK, width), lambda i, m: (i, 0)),
            scratch_shapes=[pltpu.VMEM((BLK, width), single)],
        ),
        out_shape=jax.ShapeDtypeStruct((TOTAL, width), bfloat),
        compiler_params=params(32),
        name="settle",
    )(meta, places, own, other)


def unsettle_kernel(meta, spots, values, out, acc):
    b = pl.program_id(0)
    low, high = meta[5, b], meta[6, b]
    acc[...] = jnp.zeros_like(acc)
    lane = lax.broadcasted_iota(jnp.int32, (PART, PART), 1)

    def one(c, carry):
        hot = jnp.where(spots[:, 0:1] == lane + c * PART, 1.0, 0.0).astype(bfloat)
        r = pl.ds(pl.multiple_of(c * PART, PART), PART)
        acc[...] += dot(hot, values[r, :].astype(bfloat))
        return carry

    lax.fori_loop(low, high, one, 0)
    out[0] = acc[...].astype(bfloat)


def unsettle(meta, spots, values):
    width = values.shape[-1]
    return pl.pallas_call(
        unsettle_kernel,
        grid_spec=pltpu.PrefetchScalarGridSpec(
            num_scalar_prefetch=1,
            grid=(6,),
            in_specs=[
                pl.BlockSpec((PART, 128), lambda b, m: (b, 0)),
                whole((TOTAL, width)),
            ],
            out_specs=pl.BlockSpec((1, PART, width), lambda b, m: (b, 0, 0)),
            scratch_shapes=[pltpu.VMEM((PART, width), single)],
        ),
        out_shape=jax.ShapeDtypeStruct((6, PART, width), bfloat),
        compiler_params=params(40),
        name="unsettle",
    )(meta, spots, values)


def of_head(values, h):
    lane = lax.broadcasted_iota(jnp.int32, values.shape, 1)
    return jnp.where((lane < HEAD_DIM) == (h % 2 == 0), values, jnp.zeros_like(values))


def lanes_of(h):
    return slice((h // 2) * 128, (h // 2) * 128 + 128)


def rows_of(h):
    return slice(h * HEAD_DIM, (h + 1) * HEAD_DIM)


def allowed_of(start, j, diagonal):
    row = lax.broadcasted_iota(jnp.int32, (BLK, BLK), 0)
    allowed = row + j * BLK >= start[...]
    if diagonal:
        allowed &= row <= lax.broadcasted_iota(jnp.int32, (BLK, BLK), 1)
    return allowed


def over_blocks(meta, i, step):
    def masked(j, carry):
        step(j, True, False)
        return carry

    def plain(j, carry):
        step(j, False, False)
        return carry

    lax.fori_loop(meta[0, i], meta[1, i], masked, 0)
    lax.fori_loop(meta[1, i], i, plain, 0)
    step(i, True, True)


def attend_kernel(meta, q, k, vt, start, context, logsum, score, peak, total, acc):
    i = pl.program_id(0)

    @pl.when(meta[2, i] > 0)
    def _():
        first = meta[0, i]
        queries = [of_head(q[:, lanes_of(h)], h) for h in range(NH)]
        peak[...] = jnp.full(peak.shape, -jnp.inf, single)

        def step(j, masked, diagonal):
            r = pl.ds(pl.multiple_of(j * BLK, BLK), BLK)
            o = pl.ds(pl.multiple_of((j - first) * BLK, BLK), BLK)
            if masked:
                allowed = allowed_of(start, j, diagonal)
            for h in range(NH):
                s = against(k[r, lanes_of(h)], queries[h])
                if masked:
                    s = jnp.where(allowed, s, -jnp.inf)
                score[h, o, :] = s
                peak[h] = jnp.maximum(peak[h], jnp.max(s.reshape(BLK // 8, 8, BLK), 0))

        over_blocks(meta, i, step)
        tops = [jnp.max(peak[h], 0, keepdims=True) for h in range(NH)]
        total[...] = jnp.zeros_like(total)
        acc[...] = jnp.zeros_like(acc)

        def add(j, carry):
            r = pl.ds(pl.multiple_of(j * BLK, BLK), BLK)
            o = pl.ds(pl.multiple_of((j - first) * BLK, BLK), BLK)
            for h in range(NH):
                p = jnp.exp(score[h, o, :] - tops[h])
                total[h] += jnp.sum(p.reshape(BLK // 8, 8, BLK), 0)
                acc[rows_of(h), :] += dot(vt[rows_of(h), r], p.astype(bfloat))
            return carry

        lax.fori_loop(first, i + 1, add, 0)
        for h in range(NH):
            whole_sum = jnp.sum(total[h], 0, keepdims=True)
            acc[rows_of(h), :] = acc[rows_of(h), :] / whole_sum
            logsum[h : h + 1, :] = tops[h] + jnp.log(whole_sum)
        context[...] = acc[...].T

    @pl.when(meta[2, i] == 0)
    def _():
        context[...] = jnp.zeros_like(context)
        logsum[...] = jnp.zeros_like(logsum)


def attend(meta, q, k, vt, start):
    block = pl.BlockSpec((BLK, HW), lambda i, m: (i, 0))
    line = lambda rows: pl.BlockSpec((rows, BLK), lambda i, m: (0, i))
    return pl.pallas_call(
        attend_kernel,
        grid_spec=pltpu.PrefetchScalarGridSpec(
            num_scalar_prefetch=1,
            grid=(TOTAL // BLK,),
            in_specs=[block, whole((TOTAL, HW)), whole((HW, TOTAL)), line(1)],
            out_specs=[block, line(8)],
            scratch_shapes=[
                pltpu.VMEM((NH, LONG, BLK), single),
                pltpu.VMEM((NH, 8, BLK), single),
                pltpu.VMEM((NH, 8, BLK), single),
                pltpu.VMEM((HW, BLK), single),
            ],
        ),
        out_shape=[
            jax.ShapeDtypeStruct((TOTAL, HW), single),
            jax.ShapeDtypeStruct((8, TOTAL), single),
        ],
        compiler_params=params(40),
        cost_estimate=pl.CostEstimate(
            flops=NH * LONG * LONG * 512, bytes_accessed=12 * MIB, transcendentals=NH * LONG * LONG // 2
        ),
        name="attend",
    )(meta, q, k, vt, start)


def attend_back_kernel(meta, q, k, kt, v, start, upper, context, logsum, dq, dk, dv, dqt, probs, slopes):
    i = pl.program_id(0)

    @pl.when(i == 0)
    def _():
        dk[...] = jnp.zeros_like(dk)
        dv[...] = jnp.zeros_like(dv)

    @pl.when(meta[2, i] > 0)
    def _():
        queries = [of_head(q[:, lanes_of(h)], h) for h in range(NH)]
        uppers = [of_head(upper[:, lanes_of(h)], h) for h in range(NH)]
        both = (upper[...].astype(single) * context[...]).T
        delta = [jnp.sum(both[rows_of(h), :], 0, keepdims=True) for h in range(NH)]
        dqt[...] = jnp.zeros_like(dqt)

        def step(j, masked, diagonal):
            r = pl.ds(pl.multiple_of(j * BLK, BLK), BLK)
            if masked:
                allowed = allowed_of(start, j, diagonal)
            for h in range(NH):
                s = against(k[r, lanes_of(h)], queries[h])
                p = jnp.exp(s - logsum[h : h + 1, :])
                if masked:
                    p = jnp.where(allowed, p, 0.0)
                dp = against(v[r, lanes_of(h)], uppers[h])
                c = slice((h % 2) * BLK, (h % 2) * BLK + BLK)
                probs[h // 2, :, c] = p.astype(bfloat)
                slopes[h // 2, :, c] = (p * (dp - delta[h])).astype(bfloat)
            for g in range(NH // 2):
                c = slice(g * 128, g * 128 + 128)
                dv[r, c] += dot(probs[g], jnp.concatenate(uppers[2 * g : 2 * g + 2], 0))
                dk[r, c] += dot(slopes[g], jnp.concatenate(queries[2 * g : 2 * g + 2], 0))
                for h in (2 * g, 2 * g + 1):
                    e = slice((h % 2) * BLK, (h % 2) * BLK + BLK)
                    dqt[rows_of(h), :] += dot(kt[rows_of(h), r], slopes[g, :, e])

        over_blocks(meta, i, step)
        dq[...] = dqt[...].T * HEAD_DIM ** (-0.5)

    @pl.when(meta[2, i] == 0)
    def _():
        dq[...] = jnp.zeros_like(dq)


def attend_back(meta, q, k, kt, v, start, upper, context, logsum):
    block = pl.BlockSpec((BLK, HW), lambda i, m: (i, 0))
    line = lambda rows: pl.BlockSpec((rows, BLK), lambda i, m: (0, i))
    full = whole((TOTAL, HW))
    return pl.pallas_call(
        attend_back_kernel,
        grid_spec=pltpu.PrefetchScalarGridSpec(
            num_scalar_prefetch=1,
            grid=(TOTAL // BLK,),
            in_specs=[block, full, whole((HW, TOTAL)), full, line(1), block, block, line(8)],
            out_specs=[block, full, full],
            scratch_shapes=[
                pltpu.VMEM((HW, BLK), single),
                pltpu.VMEM((NH // 2, BLK, 2 * BLK), bfloat),
                pltpu.VMEM((NH // 2, BLK, 2 * BLK), bfloat),
            ],
        ),
        out_shape=[jax.ShapeDtypeStruct((TOTAL, HW), single)] * 3,
        compiler_params=params(48),
        cost_estimate=pl.CostEstimate(
            flops=5 * NH * LONG * LONG * 256, bytes_accessed=24 * MIB, transcendentals=NH * LONG * LONG // 2
        ),
        name="attend_back",
    )(meta, q, k, kt, v, start, upper, context, logsum)


def back_kernel(meta, dq, dk, dv, normed, weight, cosine, sine, lower, g_weight, g_add):
    i = pl.program_id(0)

    @pl.when(i == 0)
    def _():
        g_weight[...] = jnp.zeros_like(g_weight)
        g_add[...] = jnp.zeros_like(g_add)

    @pl.when(meta[2, i] > 0)
    def _():
        turned = []
        for ref in (dq, dk):
            for p in range(0, HW, 128):
                turned.append(turn_lanes(ref[:, p : p + 128], cosine[...], -sine[...]))
        turned.append(dv[...])
        mixed = jnp.concatenate(turned, 1).astype(bfloat)
        g_add[...] += jnp.sum(mixed.astype(single), 0, keepdims=True)
        lower[...] = against(mixed, weight[...]).astype(bfloat)
        g_weight[...] += over_rows(normed[...], mixed)

    @pl.when(meta[2, i] == 0)
    def _():
        lower[...] = jnp.zeros_like(lower)


def back(meta, dq, dk, dv, normed, weight, cosine, sine):
    tall = lambda width: pl.BlockSpec((BLK, width), lambda i, m: (i, 0))
    return pl.pallas_call(
        back_kernel,
        grid_spec=pltpu.PrefetchScalarGridSpec(
            num_scalar_prefetch=1,
            grid=(TOTAL // BLK,),
            in_specs=[
                tall(HW),
                tall(HW),
                tall(HW),
                tall(D),
                whole((D, 3 * HW)),
                tall(128),
                tall(128),
            ],
            out_specs=[tall(D), whole((D, 3 * HW)), whole((1, 3 * HW))],
        ),
        out_shape=[
            jax.ShapeDtypeStruct((TOTAL, D), bfloat),
            jax.ShapeDtypeStruct((D, 3 * HW), single),
            jax.ShapeDtypeStruct((1, 3 * HW), single),
        ],
        compiler_params=params(40),
        cost_estimate=pl.CostEstimate(
            flops=4 * TOTAL * D * 3 * HW, bytes_accessed=32 * MIB, transcendentals=0
        ),
        name="back",
    )(meta, dq, dk, dv, normed, weight, cosine, sine)


def gather_all(x):
    return lax.all_gather(x, "dp", axis=0, tiled=True)


def scatter_sum(x):
    return lax.psum_scatter(x, "dp", scatter_dimension=0, tiled=True)


def body(
    tokens,
    cotangent,
    loss_mask,
    bucket_perm,
    short_lengths,
    row_owner,
    row_slot,
    first_gain,
    first_shift,
    second_gain,
    second_shift,
    project_weight,
    project_bias,
    output_weight,
    output_bias,
    up_weight,
    up_bias,
    down_weight,
    down_bias,
):
    devices = lax.axis_size("dp")
    me = lax.axis_index("dp")
    core = me % 2
    chip = me // 2
    rows = tokens.shape[0]
    share = LONG // devices // 4
    room = 3 * share
    long_count = devices // 4
    swap = [(i, i ^ 1) for i in range(devices)]

    def exchange(x):
        return lax.ppermute(x, "dp", swap)

    small = jnp.concatenate(
        [
            first_gain,
            first_shift,
            second_gain,
            second_shift,
            output_bias,
            down_bias,
            project_bias,
            up_bias,
        ]
    ).astype(bfloat)
    small_all = gather_all(small[None])
    project_full = gather_all(project_weight.astype(bfloat))
    output_full = gather_all(output_weight.astype(bfloat))
    up_full = gather_all(up_weight.astype(bfloat))
    down_full = gather_all(down_weight.astype(bfloat))
    piece = D // devices

    def vector(first, width):
        return small_all[:, first : first + width].astype(single).reshape(1, devices * width)

    gain_one, shift_one, gain_two, shift_two, output_add, down_add = (
        vector(i * piece, piece) for i in range(6)
    )
    project_add = vector(6 * piece, 3 * piece)
    up_add = vector(9 * piece, 4 * piece)
    project_half = lax.dynamic_index_in_dim(
        project_full.reshape(D, 3, 2, HW), core, 2, keepdims=False
    ).reshape(D, 3 * HW)
    project_add_half = lax.dynamic_index_in_dim(
        project_add.reshape(1, 3, 2, HW), core, 2, keepdims=False
    ).reshape(1, 3 * HW)

    spread = jnp.arange(devices, dtype=jnp.int32)
    bucket = jnp.sum(jnp.where(bucket_perm[None, :] == row_owner[:, None], spread[None, :], 0), -1)
    hot = (row_owner[:, None] == spread[None, :]).astype(bfloat)
    line = jnp.arange(rows, dtype=jnp.int32)
    before = (line[None, :] < line[:, None]).astype(bfloat)
    rank = jnp.sum(dot(before, hot) * hot.astype(single), -1).astype(jnp.int32)
    is_long = bucket < long_count
    short = bucket - long_count
    part = jnp.where(is_long, 0, short % 3)
    to_chip = jnp.where(is_long, 2 * bucket, 2 * (short // 3) + 1)
    held = jnp.where(is_long, 2 * share, share)
    to_core = rank // held
    place = (2 * to_chip + to_core) * room + part * share + rank % held
    slot = part * SHORT_TOK + row_slot
    spots = jnp.arange(devices * room, dtype=jnp.int32)
    slot_at = jnp.sum(
        jnp.where(place[None, :] == spots[:, None], slot[None, :] + 1, 0), -1
    ) - 1
    slot_send = slot_at.reshape(devices // 2, 1, 2 * room)
    slot_send = jnp.broadcast_to(slot_send, (devices // 2, 2, 2 * room)).reshape(devices, 2 * room)
    sender = (place[None, :] == spots[:, None]).astype(bfloat)
    keeper = (place[:, None] == spots[None, :]).astype(bfloat)

    def swap_all(x):
        return lax.all_to_all(x, "dp", split_axis=0, concat_axis=0, tiled=True)

    def dispatch(x):
        moved = swap_all(dot(sender, x).astype(bfloat).reshape(devices, room, D))
        return moved.reshape(devices, 3, share, D).transpose(1, 0, 2, 3).reshape(3, PART, D)

    def give_back(x):
        moved = x.reshape(3, devices, share, D).transpose(1, 0, 2, 3).reshape(devices, room, D)
        return dot(keeper, swap_all(moved).reshape(devices * room, D))

    slot_recv = swap_all(slot_send).reshape(devices, 2, 3, share).transpose(1, 2, 0, 3)
    slot_recv = slot_recv.reshape(2, 3, PART)
    slot_recv = jnp.where(core == 0, slot_recv, slot_recv[::-1])
    places = slot_recv.reshape(6, 1, PART)
    places_wide = jnp.broadcast_to(slot_recv.reshape(6 * PART, 1), (6 * PART, 128))

    self_long = chip % 2 == 0
    lengths = lax.dynamic_slice_in_dim(short_lengths, 3 * (chip // 2), 3, 0)
    ends = jnp.cumsum(lengths, -1)
    at = jnp.arange(TOTAL, dtype=jnp.int32).reshape(3, SHORT_TOK)
    inside = jnp.arange(SHORT_TOK, dtype=jnp.int32)
    begun = jnp.max(
        jnp.where(ends[:, None, :] <= inside[None, :, None], ends[:, None, :], 0), -1
    )
    start = jnp.where(self_long, 0, begun + at - inside[None, :]).reshape(TOTAL)
    position = jnp.arange(TOTAL, dtype=jnp.int32) - start
    blocks = jnp.arange(TOTAL // BLK, dtype=jnp.int32)
    low_start = start[::BLK] // BLK
    high_start = (start[BLK - 1 :: BLK] + BLK - 1) // BLK
    zero = jnp.zeros_like(blocks)
    meta = jnp.stack(
        [
            low_start,
            jnp.minimum(blocks, jnp.maximum(low_start, high_start)),
            jnp.where(self_long & (blocks >= LONG // BLK), 0, 1),
            jnp.where(self_long, 0, blocks // (SHORT_TOK // BLK)),
            jnp.where(self_long, 2, 1) + zero,
            jnp.where(self_long, 0, 2 * (blocks % 3)),
            jnp.where(self_long, jnp.where(blocks % 3 == 2, 0, 4), 2 * (blocks % 3) + 2),
        ]
    ).astype(jnp.int32)
    freq = 10000.0 ** (-2.0 * jnp.arange(ROT // 2).astype(single) / ROT)
    phase = position.astype(single)[:, None] * freq[None, :]
    cos8, sin8 = jnp.cos(phase), jnp.sin(phase)
    rest = HEAD_DIM - ROT
    cosine = jnp.tile(
        jnp.concatenate([cos8, cos8, jnp.ones((TOTAL, rest), single)], 1), (1, 2)
    )
    sine = jnp.tile(jnp.concatenate([-sin8, sin8, jnp.zeros((TOTAL, rest), single)], 1), (1, 2))
    starts = start.reshape(1, TOTAL)

    def half(x, which):
        return lax.dynamic_slice_in_dim(x, which * HW, HW, x.ndim - 1)

    tangent = cotangent * loss_mask.astype(bfloat)[:, None]
    own = dispatch(tokens)
    other = exchange(own)
    upper_rows = dispatch(against(tangent, output_full).astype(bfloat))
    upper_other = exchange(half(upper_rows, 1 - core))
    normed_one, q, k, kt, v, vt = front(
        meta, places, own, other, gain_one, shift_one, project_half, project_add_half, cosine, sine
    )
    context, logsum = attend(meta, q, k, vt, starts)
    context_rows = unsettle(meta, places_wide, context)
    mine, theirs = context_rows[:3], exchange(context_rows[3:])
    context_back = give_back(
        jnp.concatenate(
            [jnp.where(core == 0, mine, theirs), jnp.where(core == 0, theirs, mine)], -1
        )
    ).astype(bfloat)

    feed, lower_two_up, up_grad, up_add_grad, down_grad = feed_forward(
        tokens, tangent, gain_two, shift_two, up_full, up_add, down_full
    )

    upper = settle(meta, places, half(upper_rows, core), upper_other)
    dq, dk, dv = attend_back(meta, q, k, kt, v, starts, upper, context, logsum)
    lower_rows, project_grad_half, project_add_half_grad = back(
        meta, dq, dk, dv, normed_one, project_half, cosine, sine
    )
    lower_moved = unsettle(meta, places_wide, lower_rows)
    lower_sum = lower_moved[:3].astype(single) + exchange(lower_moved[3:]).astype(single)
    upper_one = give_back(lower_sum.astype(bfloat))

    rows_in = tokens.astype(single)
    scaled, factor = norm_stats(rows_in)
    block_out = (
        rows_in + (dot(context_back, output_full) + output_add) + (feed + down_add)
    ).astype(bfloat)
    lower_one, gain_one_grad, shift_one_grad = norm_back(upper_one, scaled, factor, gain_one)
    lower_two, gain_two_grad, shift_two_grad = norm_back(lower_two_up, scaled, factor, gain_two)
    tokens_grad = (tangent.astype(single) + lower_one + lower_two).astype(bfloat)
    output_grad = over_rows(context_back, tangent)
    bias_grad = jnp.sum(tangent.astype(single), 0)

    def spread_half(x):
        lead = x.shape[0]
        x = x.reshape(lead, 3, 1, HW)
        empty = jnp.zeros_like(x)
        pair = jnp.where(
            core == 0, jnp.concatenate([x, empty], 2), jnp.concatenate([empty, x], 2)
        )
        return pair.reshape(lead, 3 * D)

    scale = lax.rsqrt(lax.psum(jnp.sum(loss_mask.astype(single)), "dp"))
    vectors = jnp.concatenate(
        [
            x.reshape(devices, -1)
            for x in (
                gain_one_grad,
                shift_one_grad,
                gain_two_grad,
                shift_two_grad,
                bias_grad,
                spread_half(project_add_half_grad),
                up_add_grad,
            )
        ],
        1,
    )
    vector_sum = scatter_sum(vectors)[0] * scale
    gains = [vector_sum[i * piece : (i + 1) * piece] for i in range(5)]
    return (
        block_out,
        tokens_grad,
        gains[0],
        gains[1],
        gains[2],
        gains[3],
        scatter_sum(spread_half(project_grad_half)) * scale,
        vector_sum[5 * piece : 8 * piece],
        scatter_sum(output_grad) * scale,
        gains[4],
        scatter_sum(up_grad) * scale,
        vector_sum[8 * piece : 12 * piece],
        scatter_sum(down_grad) * scale,
        gains[4],
    )


def solution(mesh):
    tall, flat = P("dp", None), P("dp")
    return jax.shard_map(
        body,
        mesh=mesh,
        in_specs=(
            tall,
            tall,
            flat,
            P(),
            P(),
            flat,
            flat,
            flat,
            flat,
            flat,
            flat,
            tall,
            flat,
            tall,
            flat,
            tall,
            flat,
            tall,
            flat,
        ),
        out_specs=(
            tall,
            tall,
            flat,
            flat,
            flat,
            flat,
            tall,
            flat,
            tall,
            flat,
            tall,
            flat,
            tall,
            flat,
        ),
        check_vma=False,
    )
```

time: 1750 us -> 863 us (0.49)
  matrix products: 860 us -> 38.3 us
  Pallas kernels: 0 us -> 203 us
  local copies, waits for them, and re-layouts: 237 us -> 68.3 us
  waiting for transfers between devices: 231 us -> 347 us
  blocking collectives: 223 us -> 113 us
  other arithmetic: 136 us -> 33.1 us
    dot_general x345 -> x6, matrix products: 808 us -> 35.1 us  [dot(): return jnp.dot(left, right, preferred_element_type=single)]
    pallas_call x0 -> x8, Pallas kernels: none -> 203 us  [the longest x1 52 us: attend_back(): pl.pallas_call(attend_back_kernel, grid_spec=pltpu.PrefetchScalarGridSpec...]
    unnamed x2 -> x1, blocking collectives: 223 us -> 38 us
    all_gather x0 -> x1, blocking collectives: none -> 75.5 us  [gather_all(): return lax.all_gather(x, 'dp', axis=0, tiled=True)]
    reduce_scatter x4 -> x3, waiting for transfers between devices: 148 us -> 214 us  [scatter_sum(): return lax.psum_scatter(x, 'dp', scatter_dimension=0, tiled=True)]
    slice x22 -> x7, local copies, waits for them, and re-layouts: 53.3 us -> 2.22 us  [the longest x1 0.59 us: body(): gains = [vector_sum[i * piece:(i + 1) * piece] for i in range(5)]]
    dot_general x4 -> x1, matrix products: 52 us -> 3.19 us  [over_rows(): lax.dot_general(left, right, (((0,), (0,)), ((), ())), preferred_element_...]
    scatter x4 -> x0, local copies, waits for them, and re-layouts: 39.7 us -> none  [the longest x2 23.5 us: settle(): return jnp.zeros((capacity,) + received.shape[1:], received.dtype).at[slo...]
  transfers between devices with their start and end apart: 13 -> 17, of which waited for: 4 -> 7; matrix products, arithmetic and copies ran while one was open for 70% -> 14% of each run, Pallas kernels for 0% -> 24%
where the time goes in v1:
time: 863 us; the launch traced here: 855 us
  waiting for transfers between devices  347 us (40%)
  Pallas kernels  203 us (24%)
  blocking collectives  113 us (13%)
  local copies, waits for them, and re-layouts  68.3 us (8%)
  matrix products  38.3 us (4%)
  starting transfers between devices  35.5 us (4%)
  other arithmetic  33.1 us (4%)
  between operations  16.2 us (2%)
    reduce_scatter x3, waiting for transfers between devices, scatter_sum(): return lax.psum_scatter(x, 'dp', scatter_dimension=0, tiled=True)  214 us
    all_to_all x5, waiting for transfers between devices, swap_all(): return lax.all_to_all(x, 'dp', split_axis=0, concat_axis=0, tiled=True)  122 us
    all_gather x1, blocking collectives, gather_all(): return lax.all_gather(x, 'dp', axis=0, tiled=True)  75.5 us
    pallas_call x1, Pallas kernels, attend_back(): pl.pallas_call(attend_back_kernel, grid_spec=pltpu.PrefetchScalarGridSpec...  52 us
    pallas_call x1, Pallas kernels, feed_forward(): pl.pallas_call(feed_kernel, grid=(FF // width,), in_specs=[whole((rows, D...  50.1 us
    unnamed x1, blocking collectives  38 us
    dot_general x6, matrix products, dot(): return jnp.dot(left, right, preferred_element_type=single)  35.1 us
    all_to_all x5, starting transfers between devices, swap_all(): return lax.all_to_all(x, 'dp', split_axis=0, concat_axis=0, tiled=True)  33.1 us
  transfers between devices with their start and end apart: 17, of which 7 were waited for; matrix products, arithmetic and copies ran while one was open for 14% of the time, Pallas kernels for 24%

profile of v1, /device:TPU:0, one launch (start us, length us, event | category | flops | bytes accessed | tf_op | source)
XLA Modules:
  0.0 855.1 jit_solution(17228533940430460266)
XLA Ops:
  19.7 7.3 all-to-all-start.1
  28.6 75.5 %all-gather = bf16[32,1,312]{2,1,0:T(2,128)(2,1)S(1)} all-gather(bf16[1,1,312]{2,1,0:T(2,128)(2,1)S(1)} %bitcast.118), channel_id=1, replica_groups=mesh['dp'=32] {'dp'}, dimensions={0}, use_global_device_ids=true | all-gather | bytes 20592 | tf_op jit(solution)/shard_map/all_gather | solution.py:566
  112.1 10.5 %all-to-all-start = ((s32[32,1,96]{2,1,0:T(1,128)}), s32[32,1,96]{2,1,0:T(1,128)S(1)}, u32[]{:S(2)}, u32[]{:S(2)}) async-start(s32[32,1,96]{2,1,0:T(1,128)} %bitcast.3), calls=%async_computation | async-start | bytes 32768 | tf_op jit(solution)/shard_map/all_to_all | solution.py:665
  130.7 8.3 fusion.32
  139.0 6.2 all-to-all-start.3
  145.8 5.8 copy.134
  158.6 24.7 %front.1 = (bf16[3072,768]{1,0:T(8,128)(2,1)}, bf16[3072,384]{1,0:T(8,128)(2,1)S(1)}, bf16[3072,384]{1,0:T(8,128)(2,1)S(1)}, bf16[384,3072]{1,0:T(8,128)(2,1)S(1...) custom-call(s32[7,12]{1,0:T(8,128)S(1)} %stack.19.meta, s32[6,1,512]{2,1,0:T(1,128)S(1)} %reshape.667.places, ...), custom_call_target="tpu_custom_call" | custom-call | flops 10267656192 | bytes 25165824 | tf_op jit(solution)/shard_map/front/pallas_call | solution.py:218
  186.7 30.4 %attend.1 = (f32[3072,384]{1,0:T(8,128)S(1)}, f32[8,3072]{1,0:T(8,128)S(1)}) custom-call(s32[7,12]{1,0:T(8,128)S(1)} %stack.19.meta, bf16[3072,384]{1,0:T(8,128)(2,1)S(1)} %get-tuple-element.33.q, bf16[3072,384]{1,0:T(8,128)(2,1)S(1)} %get-tuple-element.34.k, bf16[384,3072]{1,0:T(8,128)(2,1)S(1)} %copy-done.17, s32[1,3072]{1,0:T(1,128)S(1)} %broadcast_select_fusion.2.start), custom_call_target="tpu_custom_call" | custom-call | flops 12884901888 | bytes 12582912 | tf_op jit(solution)/shard_map/attend/pallas_call | solution.py:412
  217.6 9.0 %unsettle.2 = bf16[6,512,384]{2,1,0:T(8,128)(2,1)S(1)} custom-call(s32[7,12]{1,0:T(8,128)S(1)} %stack.19.meta, s32[3072,128]{1,0:T(8,128)S(1)} %broadcast_in_dim.122.spots, f32[3072,384]{1,0:T(8,128)S(1)} %get-tuple-element.36.values.context), custom_call_target="tpu_custom_call" | custom-call | tf_op jit(solution)/shard_map/unsettle/pallas_call | solution.py:308
  242.6 8.1 settle.1.upper
  252.1 60.5 %all-to-all-done.2 = bf16[32,48,768]{2,1,0:T(8,128)(2,1)} async-done(((bf16[32,48,768]{2,1,0:T(8,128)(2,1)}), bf16[32,48,768]{2,1,0:T(8,128)(2,1)}, u32[]{:S(2)}, u32[]{:S(2)}) %all-to-all-start.2) | async-done | bytes 2359328 | tf_op jit(solution)/shard_map/all_to_all | solution.py:665
  312.5 5.4 fusion.30
  326.0 52.0 %attend_back.1 = (f32[3072,384]{1,0:T(8,128)}, f32[3072,384]{1,0:T(8,128)}, f32[3072,384]{1,0:T(8,128)}) custom-call(s32[7,12]{1,0:T(8,128)S(1)} %stack.19.meta, bf16[3072,384]{1,0:T(8,128)(2,1)S(1)} %copy-done.12, bf16[3072,384]{1,0:T(8,128)(2,1)S(1)} %copy-done.14, bf16[384,3072]{1,0:T(8,128)(2,1)} %copy-done.15, bf16[3072,384]{1,0:T(8,128)(2,1)} %copy-done.16, ...), custom_call_target="tpu_custom_call" | custom-call | flops 32212254720 | bytes 25165824 | tf_op jit(solution)/shard_map/attend_back/pallas_call | solution.py:487
  377.9 17.5 %back.1 = (bf16[3072,768]{1,0:T(8,128)(2,1)S(1)}, f32[768,1152]{1,0:T(8,128)S(1)}, f32[1,1152]{1,0:T(1,128)S(1)}) custom-call(s32[7,12]{1,0:T(8,128)S(1)} %stack.19.meta, f32[3072,384]{1,0:T(8,128)} %get-tuple-element.41.dq, f32[3072,384]{1,0:T(8,128)} %get-tuple-element.42.dk, f32[3072,384]{1,0:T(8,128)} %get-tuple-element.43.dv, ...), custom_call_target="tpu_custom_call" | custom-call | flops 10871635968 | bytes 33554432 | tf_op jit(solution)/shard_map/back/pallas_call | solution.py:536
  411.4 8.0 copy.151
  421.9 50.1 %feed_forward.1 = (f32[1280,768]{1,0:T(8,128)}, f32[1280,768]{1,0:T(8,128)}, f32[768,3072]{1,0:T(8,128)}, f32[1,3072]{1,0:T(1,128)}, f32[3072,768]{1,0:T(8,128)}) custom-call(bf16[1280,768]{1,0:T(8,128)(2,1)} %tok.1, bf16[1280,768]{1,0:T(8,128)(2,1)} %get-tuple-element.123.tan, f32[1,768]{1,0:T(1,128)} %reshape.634.gain, f32[1,768]{1,0:T(1,128)} %reshape.659.shift, ...), custom_call_target="tpu_custom_call" | custom-call | flops 36238786560 | bytes 52428800 | tf_op jit(solution)/shard_map/feed_forward/pallas_call | solution.py:124
  475.1 11.7 %unsettle.3 = bf16[6,512,768]{2,1,0:T(8,128)(2,1)S(1)} custom-call(s32[7,12]{1,0:T(8,128)S(1)} %stack.19.meta, s32[3072,128]{1,0:T(8,128)S(1)} %broadcast_in_dim.122.spots, bf16[3072,768]{1,0:T(8,128)(2,1)S(1)} %copy-done.3), custom_call_target="tpu_custom_call" | custom-call | tf_op jit(solution)/shard_map/unsettle/pallas_call | solution.py:308
  501.4 6.0 fusion.25
  507.4 61.7 %all-to-all-done.4 = bf16[32,48,768]{2,1,0:T(8,128)(2,1)} async-done(((bf16[32,48,768]{2,1,0:T(8,128)(2,1)}), bf16[32,48,768]{2,1,0:T(8,128)(2,1)}, u32[]{:S(2)}, u32[]{:S(2)}) %all-to-all-start.4) | async-done | bytes 2359328 | tf_op jit(solution)/shard_map/all_to_all | solution.py:665
  569.1 9.1 %fusion.21 = (f32[768]{0:T(1024)S(1)}, f32[1280]{0:T(1024)S(1)}, f32[1280]{0:T(1024)S(1)}, f32[768]{0:T(1024)S(1)}, f32[768]{0:T(1024)S(1)}, /*index=5*/f32[1280...) fusion(bf16[1280,768]{1,0:T(8,128)(2,1)S(1)} %copy-done.19, f32[1280]{0:T(1024)S(1)} %add_rsqrt_fusion, ...), kind=kOutput, calls=%fused_computation.32 | convolution fusion | flops 3038568448 | bytes 12243968 | tf_op jit(solution)/shard_map/dot_general | solution.py:31
  578.6 38.0 %all-reduce.5 = (f32[32,288]{1,0:T(8,128)S(1)}, f32[]{:T(128)}) all-reduce(f32[32,288]{1,0:T(8,128)S(1)} %concatenate.65, f32[]{:T(128)} %convert_reduce_fusion.2), channel_id=2, replica_groups=mesh['dp'=32] {'dp'}, use_global_device_ids=true, to_apply=%region_16.17.clone | all-reduce | flops 9217 | bytes 73736
  619.1 6.8 fusion.20
  629.9 74.3 %reduce-scatter.11.cloned.1.call-done = f32[96,768]{1,0:T(8,128)} async-done(((f32[3072,768]{1,0:T(8,128)}), f32[96,768]{1,0:T(8,128)}) %reduce-scatter.11.cloned.1.call-update) | async-done | bytes 294928 | tf_op jit(solution)/shard_map/reduce_scatter | solution.py:570
  705.9 139.9 %reduce-scatter.9.cloned.1.call-done = f32[24,3072]{1,0:T(8,128)} async-done(((f32[768,3072]{1,0:T(8,128)}), f32[24,3072]{1,0:T(8,128)}) %reduce-scatter.9.cloned.1.call-update) | async-done | bytes 294928 | tf_op jit(solution)/shard_map/reduce_scatter | solution.py:570
  (255 shorter events, 112.2 us)
Async XLA Ops:
  7.2 123.4 %all-gather.8.cloned.1.call-start = ((), (), s32[]{:S(2)}) async-start(), calls=%async_computation.10 | async-start | bytes 1216512 | tf_op jit(solution)/shard_map/all_gather | solution.py:566
  8.9 136.9 %all-gather.6.cloned.1.call-start = ((), (), s32[]{:S(2)}) async-start(), calls=%async_computation.9 | async-start | bytes 3649536 | tf_op jit(solution)/shard_map/all_gather | solution.py:566
  10.6 411.3 %all-gather.10.cloned.1.call-start = ((), (), s32[]{:S(2)}) async-start(), calls=%async_computation.11 | async-start | bytes 4866048 | tf_op jit(solution)/shard_map/all_gather | solution.py:566
  14.9 297.7 %copy-start.29 = (s32[1280]{0:T(1024)}, s32[1280]{0:T(1024)S(1)}, u32[]{:S(2)}) copy-start(s32[1280]{0:T(1024)S(1)} %get-tuple-element.141) | copy-start | bytes 15364
  19.7 85.4 %copy-start.31 = (s32[1280]{0:T(1024)S(1)}, s32[1280]{0:T(1024)}, u32[]{:S(2)}) copy-start(s32[1280]{0:T(1024)} %param.21) | copy-start | bytes 15364
  19.7 91.8 %all-to-all-start.1 = ((bf16[32,48,768]{2,1,0:T(8,128)(2,1)}), bf16[32,48,768]{2,1,0:T(8,128)(2,1)S(1)}, u32[]{:S(2)}, u32[]{:S(2)}) async-start(bf16[32,48,768]{2,1,0:T(8,128)(2,1)} %bitcast.108), calls=%async_computation.1 | async-start | bytes 4718592 | tf_op jit(solution)/shard_map/all_to_all | solution.py:665
  27.0 394.8 %all-gather.12.cloned.1.call-start = ((), (), s32[]{:S(2)}) async-start(), calls=%async_computation.12 | async-start | bytes 4866048 | tf_op jit(solution)/shard_map/all_gather | solution.py:566
  105.9 313.9 %copy-start.23 = (f32[32,24]{1,0:T(8,128)}, f32[32,24]{1,0:T(8,128)S(1)}, u32[]{:S(2)}) copy-start(f32[32,24]{1,0:T(8,128)S(1)} %get-tuple-element.135) | copy-start | bytes 9220
  112.1 26.9 %all-to-all-start = ((s32[32,1,96]{2,1,0:T(1,128)}), s32[32,1,96]{2,1,0:T(1,128)S(1)}, u32[]{:S(2)}, u32[]{:S(2)}) async-start(s32[32,1,96]{2,1,0:T(1,128)} %bitcast.3), calls=%async_computation | async-start | bytes 32768 | tf_op jit(solution)/shard_map/all_to_all | solution.py:665
  124.4 32.8 %collective-permute-start = (bf16[3,512,768]{2,1,0:T(8,128)(2,1)}, bf16[3,512,768]{2,1,0:T(8,128)(2,1)}, u32[]{:S(2)}, u32[]{:S(2)}) collective-permute-start(bf16[3,512,768]{2,1,0:T(8,128)(2,1)} %bitcast.9.own), channel_id=1, source_target_pairs={{0,1},{1,0},{2,3},{3,2},{4,5},{5,4},{6,7},{7,6},{8,9},{9,8},{10,11... | collective-permute-start | bytes 7077896 | tf_op jit(solution)/shard_map/ppermute | solution.py:605
  139.0 92.7 %all-to-all-start.3 = ((bf16[32,48,768]{2,1,0:T(8,128)(2,1)}), bf16[32,48,768]{2,1,0:T(8,128)(2,1)}, u32[]{:S(2)}, u32[]{:S(2)}) async-start(bf16[32,48,768]{2,1,0:T(8,128)(2,1)} %bitcast.109), calls=%async_computation.3 | async-start | bytes 4718592 | tf_op jit(solution)/shard_map/all_to_all | solution.py:665
  226.8 2.9 collective-permute-start.1
  231.7 80.8 %all-to-all-start.2 = ((bf16[32,48,768]{2,1,0:T(8,128)(2,1)}), bf16[32,48,768]{2,1,0:T(8,128)(2,1)}, u32[]{:S(2)}, u32[]{:S(2)}) async-start(bf16[32,48,768]{2,1,0:T(8,128)(2,1)} %bitcast.102), calls=%async_computation.2 | async-start | bytes 4718592 | tf_op jit(solution)/shard_map/all_to_all | solution.py:665
  236.8 389.1 %reduce-scatter.7.cloned.1.call-start = ((), (), s32[]{:S(2)}) async-start(), calls=%async_computation.13 | async-start | bytes 2433024 | tf_op jit(solution)/shard_map/reduce_scatter | solution.py:570
  239.7 2.9 collective-permute-start.2
  322.4 305.1 %reduce-scatter.13.cloned.1.call-start = ((), (), s32[]{:S(2)}) async-start(), calls=%async_computation.16 | async-start | bytes 7299072
  326.0 52.0 %copy-start.10 = (f32[3072,128]{1,0:T(8,128)S(1)}, f32[3072,128]{1,0:T(8,128)}, u32[]{:S(2)}) copy-start(f32[3072,128]{1,0:T(8,128)} %copy.139.sine) | copy-start | bytes 4718596
  419.5 284.7 %reduce-scatter.11.cloned.1.call-start = ((), (), s32[]{:S(2)}) async-start(), calls=%async_computation.15 | async-start | bytes 9732096 | tf_op jit(solution)/shard_map/reduce_scatter | solution.py:570
  472.0 373.8 %reduce-scatter.9.cloned.1.call-start = ((), (), s32[]{:S(2)}) async-start(), calls=%async_computation.14 | async-start | bytes 9732096 | tf_op jit(solution)/shard_map/reduce_scatter | solution.py:570
  486.9 4.6 collective-permute-start.3
  493.7 75.3 %all-to-all-start.4 = ((bf16[32,48,768]{2,1,0:T(8,128)(2,1)}), bf16[32,48,768]{2,1,0:T(8,128)(2,1)}, u32[]{:S(2)}, u32[]{:S(2)}) async-start(bf16[32,48,768]{2,1,0:T(8,128)(2,1)} %bitcast.101), calls=%async_computation.4 | async-start | bytes 4718592 | tf_op jit(solution)/shard_map/all_to_all | solution.py:665
  501.4 67.7 %copy-start.30 = (s32[1280]{0:T(1024)S(1)}, s32[1280]{0:T(1024)}, u32[]{:S(2)}) copy-start(s32[1280]{0:T(1024)} %copy-done.29) | copy-start | bytes 15364
  617.9 229.6 %copy-start.36 = (f32[24]{0:T(128)}, f32[24]{0:T(128)S(1)}, u32[]{:S(2)}) copy-start(f32[24]{0:T(128)S(1)} %get-tuple-element.188) | copy-start | bytes 292
  627.5 220.5 %copy-start.1 = (s32[24,3]{0,1:T(4,128)S(1)}, s32[24,3]{0,1:T(4,128)}, u32[]{:S(2)}) copy-start(s32[24,3]{0,1:T(4,128)} %param.23) | copy-start | bytes 868
  (39 other events, 426.5 us)
Sparse Core Ops, SparseCore 0:
  11.5 70.8 all-gather.7
  85.9 57.6 all-gather.5
  147.0 76.2 all-gather.9
  226.7 82.1 all-gather.11
  322.5 97.8 reduce-scatter.6
  426.9 136.9 reduce-scatter.12
  569.9 134.2 reduce-scatter.10
  711.1 134.6 reduce-scatter.8

commit v2 on v1

v2 whole, which is shorter than its diff:
```python
import functools
import math

import jax
import jax.numpy as jnp
from jax import lax
from jax.experimental import pallas as pl
from jax.experimental.pallas import tpu as pltpu
from jax.sharding import PartitionSpec as P

D = 768
HEADS = 12
HEAD_DIM = 64
ROT = 16
FF = 3072
LONG = 2048
SHORT_TOK = 1024
TOTAL = 3 * SHORT_TOK
BLK = 256
BLOCKS = TOTAL // BLK
NH = HEADS // 2
HW = NH * HEAD_DIM
PART = SHORT_TOK // 2
MIB = 2**20

epsilon = 1e-05
bfloat = jnp.bfloat16
single = jnp.float32


def dot(left, right):
    return jnp.dot(left, right, preferred_element_type=single)


def over_rows(left, right):
    return lax.dot_general(left, right, (((0,), (0,)), ((), ())), preferred_element_type=single)


def against(left, right):
    return lax.dot_general(left, right, (((1,), (1,)), ((), ())), preferred_element_type=single)


def norm_stats(values):
    mean = jnp.mean(values, -1, keepdims=True)
    centred = values - mean
    spread = jnp.mean(centred * centred, -1, keepdims=True)
    factor = lax.rsqrt(spread + epsilon)
    return (centred * factor, factor)


def params(mib):
    return pltpu.CompilerParams(vmem_limit_bytes=mib * MIB)


def whole(shape):
    return pl.BlockSpec(shape, lambda *_: (0,) * len(shape))


def feed_kernel(
    tok, tan, lines, up, up_add, down, feed, lower, grad, g_up_add, normed, act, slope
):
    step = pl.program_id(0)
    rows = tok.shape[0]
    chunk = rows // 2
    root = 1.0 / math.sqrt(2.0)
    dens = 1.0 / math.sqrt(2.0 * math.pi)

    @pl.when(step == 0)
    def _():
        def one(i, carry):
            r = pl.ds(pl.multiple_of(i * BLK, BLK), BLK)
            scaled, _ = norm_stats(tok[r, :].astype(single))
            normed[r, :] = (scaled * lines[2:3, :] + lines[3:4, :]).astype(bfloat)
            return carry

        lax.fori_loop(0, rows // BLK, one, 0)

    bias_sum = jnp.zeros((1, D), single)
    for i in range(2):
        r = pl.ds(i * chunk, chunk)
        hidden = dot(normed[r, :], up[...]) + up_add[0]
        above = against(tan[r, :], down[...])
        phi = 0.5 * (1.0 + lax.erf(hidden * root))
        active = (hidden * phi).astype(bfloat)
        sl = (above * (phi + hidden * (dens * jnp.exp(-0.5 * hidden * hidden)))).astype(bfloat)
        act[r, :] = active
        slope[r, :] = sl
        bias_sum = bias_sum + jnp.sum(sl.astype(single), 0, keepdims=True)
        part_feed = dot(active, down[...])
        part_lower = against(sl, up[...])

        @pl.when(step == 0)
        def _():
            feed[r, :] = part_feed
            lower[r, :] = part_lower

        @pl.when(step > 0)
        def _():
            feed[r, :] += part_feed
            lower[r, :] += part_lower

    g_up_add[0] = bias_sum
    grad[:, :D] = over_rows(normed[...], slope[...]).astype(bfloat)
    grad[:, D:] = over_rows(act[...], tan[...]).astype(bfloat)


def feed_forward(tok, tan, lines, weights, up_add):
    rows, count = tok.shape[0], FF // D
    wide = lambda where: pl.BlockSpec((D, D), lambda j: (0, where + j))
    one = lambda shape: pl.BlockSpec(shape, lambda j: (0, 0), pipeline_mode=pl.Buffered(1))
    line = pl.BlockSpec((1, 1, D), lambda j: (j, 0, 0))
    pair = pl.BlockSpec((D, 2 * D), lambda j: (0, j))
    return pl.pallas_call(
        feed_kernel,
        grid=(count,),
        in_specs=[one((rows, D)), one((rows, D)), one((16, D)), wide(0), line, wide(count)],
        out_specs=[one((rows, D)), one((rows, D)), pair, line],
        out_shape=[
            jax.ShapeDtypeStruct((rows, D), single),
            jax.ShapeDtypeStruct((rows, D), single),
            jax.ShapeDtypeStruct((D, 2 * count * D), bfloat),
            jax.ShapeDtypeStruct((count, 1, D), single),
        ],
        scratch_shapes=[
            pltpu.VMEM((rows, D), bfloat),
            pltpu.VMEM((rows, D), bfloat),
            pltpu.VMEM((rows, D), bfloat),
        ],
        compiler_params=params(60),
        cost_estimate=pl.CostEstimate(
            flops=12 * rows * D * D * count, bytes_accessed=count * 12 * MIB, transcendentals=2 * rows * D * count
        ),
        name="feed_forward",
    )(tok, tan, lines, weights, up_add, weights)


def gather_rows(meta, i, places, own, other, rows):
    spot = lax.broadcasted_iota(jnp.int32, (BLK, PART), 0) + i * BLK

    def part(k):
        mine = jnp.where(places[k] == spot, 1.0, 0.0).astype(bfloat)
        theirs = jnp.where(places[k + 3] == spot, 1.0, 0.0).astype(bfloat)
        return dot(mine, own[k]) + dot(theirs, other[k])

    low = meta[3, i]
    rows[...] = part(low)

    @pl.when(meta[4, i] > 1)
    def _():
        rows[...] += part(low + 1)


def column(line):
    return jnp.broadcast_to(line, (128, line.shape[1])).T[:, 0:1]


def return_rows(meta, at, places, values, mine, theirs, acc):
    b = lax.rem(at + 3, 6)
    acc[...] = jnp.zeros_like(acc)
    lane = lax.broadcasted_iota(jnp.int32, (PART, PART), 1)
    spots = column(places[b])

    def one(c, carry):
        hot = jnp.where(spots == lane + c * PART, 1.0, 0.0).astype(bfloat)
        r = pl.ds(pl.multiple_of(c * PART, PART), PART)
        acc[...] += dot(hot, values[r, :])
        return carry

    lax.fori_loop(meta[5, b], meta[6, b], one, 0)

    @pl.when(at < 3)
    def _():
        theirs[0] = acc[...].astype(bfloat)

    @pl.when(at >= 3)
    def _():
        mine[0] = acc[...].astype(bfloat)


def turn_lanes(values, cosine, sine):
    lane = lax.broadcasted_iota(jnp.int32, values.shape, 1)
    swapped = jnp.where(
        lax.rem(lane, ROT) < ROT // 2, pltpu.roll(values, 128 - ROT // 2, 1), pltpu.roll(values, ROT // 2, 1)
    )
    return values * cosine + swapped * sine


def of_head(values, h):
    lane = lax.broadcasted_iota(jnp.int32, values.shape, 1)
    return jnp.where((lane < HEAD_DIM) == (h % 2 == 0), values, jnp.zeros_like(values))


def lanes_of(h):
    return slice((h // 2) * 128, (h // 2) * 128 + 128)


def rows_of(h):
    return slice(h * HEAD_DIM, (h + 1) * HEAD_DIM)


def block_of(j):
    return pl.ds(pl.multiple_of(j * BLK, BLK), BLK)


def allowed_of(start, j, diagonal):
    row = lax.broadcasted_iota(jnp.int32, (BLK, BLK), 0)
    allowed = row + j * BLK >= start[...]
    if diagonal:
        allowed &= row <= lax.broadcasted_iota(jnp.int32, (BLK, BLK), 1)
    return allowed


def over_blocks(meta, i, step):
    def masked(j, carry):
        step(j, True, False)
        return carry

    def plain(j, carry):
        step(j, False, False)
        return carry

    lax.fori_loop(meta[0, i], meta[1, i], masked, 0)
    lax.fori_loop(meta[1, i], i, plain, 0)
    step(i, True, True)


def forward_kernel(
    meta,
    places,
    own,
    other,
    lines,
    weight_q,
    weight_k,
    weight_v,
    add,
    cosine,
    sine,
    start,
    kept,
    q,
    k,
    kt,
    v,
    context,
    logsum,
    mine,
    theirs,
    rows,
    keys,
    values,
    score,
    peak,
    total,
    acc,
    done,
    back_acc,
):
    step_at = pl.program_id(0)
    i = jnp.minimum(step_at, BLOCKS - 1)
    here = block_of(i)
    live = (step_at < BLOCKS) & (meta[2, i] > 0)

    @pl.when(live)
    def _():
        gather_rows(meta, i, places, own, other, rows)
        scaled, _ = norm_stats(rows[...])
        n = (scaled * lines[0:1, :] + lines[1:2, :]).astype(bfloat)
        kept[...] = rows[...].astype(bfloat)
        for s, weight in enumerate((weight_q, weight_k, weight_v)):
            mixed = dot(n, weight[...]) + add[:, s * HW : (s + 1) * HW]
            if s < 2:
                mixed = jnp.concatenate(
                    [
                        turn_lanes(mixed[:, p : p + 128], cosine[...], sine[...])
                        for p in range(0, HW, 128)
                    ],
                    1,
                )
            narrow = mixed.astype(bfloat)
            if s == 0:
                q[...] = narrow * HEAD_DIM ** (-0.5)
            elif s == 1:
                k[...] = narrow
                keys[here, :] = narrow
                kt[...] = narrow.T
            else:
                v[...] = narrow
                values[:, here] = narrow.T

        first = meta[0, i]
        queries = [of_head(q[:, lanes_of(h)], h) for h in range(NH)]
        peak[...] = jnp.full(peak.shape, -jnp.inf, single)

        def step(j, masked, diagonal):
            if masked:
                allowed = allowed_of(start, j, diagonal)
            for h in range(NH):
                s = against(keys[block_of(j), lanes_of(h)], queries[h])
                if masked:
                    s = jnp.where(allowed, s, -jnp.inf)
                score[h, block_of(j - first), :] = s
                peak[h] = jnp.maximum(peak[h], jnp.max(s.reshape(BLK // 8, 8, BLK), 0))

        over_blocks(meta, i, step)
        tops = [jnp.max(peak[h], 0, keepdims=True) for h in range(NH)]
        total[...] = jnp.zeros_like(total)
        acc[...] = jnp.zeros_like(acc)

        def gain(j, carry):
            for h in range(NH):
                p = jnp.exp(score[h, block_of(j - first), :] - tops[h])
                total[h] += jnp.sum(p.reshape(BLK // 8, 8, BLK), 0)
                acc[rows_of(h), :] += dot(values[rows_of(h), block_of(j)], p.astype(bfloat))
            return carry

        lax.fori_loop(first, i + 1, gain, 0)
        for h in range(NH):
            whole_sum = jnp.sum(total[h], 0, keepdims=True)
            acc[rows_of(h), :] = acc[rows_of(h), :] / whole_sum
            logsum[h : h + 1, :] = tops[h] + jnp.log(whole_sum)
        turned = acc[...].T
        context[...] = turned
        done[here, :] = turned.astype(bfloat)

    @pl.when((step_at < BLOCKS) & (meta[2, i] == 0))
    def _():
        for ref in (kept, q, k, kt, v, context, logsum):
            ref[...] = jnp.zeros_like(ref)

    @pl.when(step_at >= BLOCKS)
    def _():
        return_rows(meta, jnp.maximum(step_at - BLOCKS, 0), places, done, mine, theirs, back_acc)


def columns():
    return [
        pl.BlockSpec((D, HW), lambda i, m, s=s: (0, 2 * s + m[7, 0]), pipeline_mode=pl.Buffered(1))
        for s in range(3)
    ]


def held(*shape):
    return pl.BlockSpec(shape, lambda i, m: (0,) * len(shape), pipeline_mode=pl.Buffered(1))


def tall_at(width, first):
    return pl.BlockSpec((BLK, width), lambda i, m: (jnp.clip(i - first, 0, BLOCKS - 1), 0))


def flat_at(height, first):
    return pl.BlockSpec((height, BLK), lambda i, m: (0, jnp.clip(i - first, 0, BLOCKS - 1)))


def parts_at(first, width):
    return [
        pl.BlockSpec((1, PART, width), lambda i, m, f=f: (jnp.clip(i - f, 0, 2), 0, 0))
        for f in (first + 3, first)
    ]


def forward(meta, places, own, other, lines, weight, add, cosine, sine, start):
    out = lambda *shape: jax.ShapeDtypeStruct(shape, bfloat)
    return pl.pallas_call(
        forward_kernel,
        grid_spec=pltpu.PrefetchScalarGridSpec(
            num_scalar_prefetch=1,
            grid=(BLOCKS + 6,),
            in_specs=[
                held(6, 1, PART),
                held(3, PART, D),
                held(3, PART, D),
                held(16, D),
                *columns(),
                held(1, 3 * HW),
                tall_at(128, 0),
                tall_at(128, 0),
                flat_at(1, 0),
            ],
            out_specs=[
                tall_at(D, 0),
                tall_at(HW, 0),
                tall_at(HW, 0),
                flat_at(HW, 0),
                tall_at(HW, 0),
                tall_at(HW, 0),
                flat_at(8, 0),
                *parts_at(BLOCKS, HW),
            ],
            scratch_shapes=[
                pltpu.VMEM((BLK, D), single),
                pltpu.VMEM((TOTAL, HW), bfloat),
                pltpu.VMEM((HW, TOTAL), bfloat),
                pltpu.VMEM((NH, LONG, BLK), single),
                pltpu.VMEM((NH, 8, BLK), single),
                pltpu.VMEM((NH, 8, BLK), single),
                pltpu.VMEM((HW, BLK), single),
                pltpu.VMEM((TOTAL, HW), bfloat),
                pltpu.VMEM((PART, HW), single),
            ],
        ),
        out_shape=[
            out(TOTAL, D),
            out(TOTAL, HW),
            out(TOTAL, HW),
            out(HW, TOTAL),
            out(TOTAL, HW),
            jax.ShapeDtypeStruct((TOTAL, HW), single),
            jax.ShapeDtypeStruct((8, TOTAL), single),
            out(3, PART, HW),
            out(3, PART, HW),
        ],
        compiler_params=params(60),
        cost_estimate=pl.CostEstimate(
            flops=60 * 10**9, bytes_accessed=40 * MIB, transcendentals=NH * LONG * LONG // 2
        ),
        name="forward",
    )(meta, places, own, other, lines, weight, weight, weight, add, cosine, sine, start)


def backward_kernel(
    meta,
    places,
    own,
    other,
    weight_out,
    q,
    k,
    kt,
    v,
    start,
    context,
    logsum,
    kept,
    lines,
    weight_q,
    weight_k,
    weight_v,
    cosine,
    sine,
    mine,
    theirs,
    g_weight,
    g_add,
    g_gain,
    g_shift,
    rows,
    upper,
    dq,
    dk,
    dv,
    dqt,
    probs,
    slopes,
    g_acc,
    lower,
    back_acc,
):
    step_at = pl.program_id(0)
    i = jnp.minimum(step_at, BLOCKS - 1)
    b = jnp.clip(step_at - BLOCKS, 0, BLOCKS - 1)

    @pl.when(step_at == 0)
    def _():
        for ref in (g_acc, g_add, g_gain, g_shift):
            ref[...] = jnp.zeros_like(ref)

    @pl.when((step_at < BLOCKS) & (meta[2, i] > 0))
    def _():
        gather_rows(meta, i, places, own, other, rows)
        upper[...] = against(rows[...].astype(bfloat), weight_out[...]).astype(bfloat)
        queries = [of_head(q[:, lanes_of(h)], h) for h in range(NH)]
        uppers = [of_head(upper[:, lanes_of(h)], h) for h in range(NH)]
        both = (upper[...].astype(single) * context[...]).T
        delta = [jnp.sum(both[rows_of(h), :], 0, keepdims=True) for h in range(NH)]
        dqt[...] = jnp.zeros_like(dqt)

        def step(j, masked, diagonal):
            r = block_of(j)
            if masked:
                allowed = allowed_of(start, j, diagonal)
            for h in range(NH):
                s = against(k[r, lanes_of(h)], queries[h])
                p = jnp.exp(s - logsum[h : h + 1, :])
                if masked:
                    p = jnp.where(allowed, p, 0.0)
                dp = against(v[r, lanes_of(h)], uppers[h])
                c = slice((h % 2) * BLK, (h % 2) * BLK + BLK)
                probs[h // 2, :, c] = p.astype(bfloat)
                slopes[h // 2, :, c] = (p * (dp - delta[h])).astype(bfloat)
            for g in range(NH // 2):
                c = slice(g * 128, g * 128 + 128)
                part_v = dot(probs[g], jnp.concatenate(uppers[2 * g : 2 * g + 2], 0))
                part_k = dot(slopes[g], jnp.concatenate(queries[2 * g : 2 * g + 2], 0))
                if diagonal:
                    dv[r, c] = part_v
                    dk[r, c] = part_k
                else:
                    dv[r, c] += part_v
                    dk[r, c] += part_k
                for h in (2 * g, 2 * g + 1):
                    e = slice((h % 2) * BLK, (h % 2) * BLK + BLK)
                    dqt[rows_of(h), :] += dot(kt[rows_of(h), r], slopes[g, :, e])

        over_blocks(meta, i, step)
        dq[block_of(i), :] = dqt[...].T * HEAD_DIM ** (-0.5)

    @pl.when((step_at >= BLOCKS) & (step_at < 2 * BLOCKS) & (meta[2, b] > 0))
    def _():
        r = block_of(b)
        turned = []
        for ref in (dq, dk):
            for p in range(0, HW, 128):
                turned.append(turn_lanes(ref[r, p : p + 128], cosine[...], -sine[...]))
        turned.append(dv[r, :])
        mixed = jnp.concatenate(turned, 1).astype(bfloat)
        g_add[...] += jnp.sum(mixed.astype(single), 0, keepdims=True)
        up = (
            against(mixed[:, :HW], weight_q[...])
            + against(mixed[:, HW : 2 * HW], weight_k[...])
            + against(mixed[:, 2 * HW :], weight_v[...])
        )
        lower[r, :] = up.astype(bfloat)
        scaled, _ = norm_stats(kept[...].astype(single))
        g_gain[...] += jnp.sum(up * scaled, 0, keepdims=True)
        g_shift[...] += jnp.sum(up, 0, keepdims=True)
        normed = (scaled * lines[0:1, :] + lines[1:2, :]).astype(bfloat)
        g_acc[...] += over_rows(normed, mixed)

    @pl.when(step_at == 2 * BLOCKS)
    def _():
        for s in range(3):
            g_weight[s] = g_acc[:, s * HW : (s + 1) * HW].astype(bfloat)

    @pl.when(step_at >= 2 * BLOCKS)
    def _():
        return_rows(
            meta, jnp.maximum(step_at - 2 * BLOCKS, 0), places, lower, mine, theirs, back_acc
        )


def backward(
    meta, places, own, other, q, k, kt, v, start, context, logsum, kept, lines, weight, cosine, sine
):
    return pl.pallas_call(
        backward_kernel,
        grid_spec=pltpu.PrefetchScalarGridSpec(
            num_scalar_prefetch=1,
            grid=(2 * BLOCKS + 6,),
            in_specs=[
                held(6, 1, PART),
                held(3, PART, D),
                held(3, PART, D),
                pl.BlockSpec((HW, D), lambda i, m: (m[7, 0], 3), pipeline_mode=pl.Buffered(1)),
                tall_at(HW, 0),
                held(TOTAL, HW),
                held(HW, TOTAL),
                held(TOTAL, HW),
                flat_at(1, 0),
                tall_at(HW, 0),
                flat_at(8, 0),
                tall_at(D, BLOCKS),
                held(16, D),
                *columns(),
                tall_at(128, BLOCKS),
                tall_at(128, BLOCKS),
            ],
            out_specs=[
                *parts_at(2 * BLOCKS, D),
                held(3, D, HW),
                held(1, 3 * HW),
                held(1, D),
                held(1, D),
            ],
            scratch_shapes=[
                pltpu.VMEM((BLK, D), single),
                pltpu.VMEM((BLK, HW), bfloat),
                pltpu.VMEM((TOTAL, HW), single),
                pltpu.VMEM((TOTAL, HW), single),
                pltpu.VMEM((TOTAL, HW), single),
                pltpu.VMEM((HW, BLK), single),
                pltpu.VMEM((NH // 2, BLK, 2 * BLK), bfloat),
                pltpu.VMEM((NH // 2, BLK, 2 * BLK), bfloat),
                pltpu.VMEM((D, 3 * HW), single),
                pltpu.VMEM((TOTAL, D), bfloat),
                pltpu.VMEM((PART, D), single),
            ],
        ),
        out_shape=[
            jax.ShapeDtypeStruct((3, PART, D), bfloat),
            jax.ShapeDtypeStruct((3, PART, D), bfloat),
            jax.ShapeDtypeStruct((3, D, HW), bfloat),
            jax.ShapeDtypeStruct((1, 3 * HW), single),
            jax.ShapeDtypeStruct((1, D), single),
            jax.ShapeDtypeStruct((1, D), single),
        ],
        compiler_params=params(60),
        cost_estimate=pl.CostEstimate(
            flops=90 * 10**9, bytes_accessed=40 * MIB, transcendentals=NH * LONG * LONG // 2
        ),
        name="backward",
    )(
        meta,
        places,
        own,
        other,
        weight,
        q,
        k,
        kt,
        v,
        start,
        context,
        logsum,
        kept,
        lines,
        weight,
        weight,
        weight,
        cosine,
        sine,
    )


def placed_rows(place, moved):
    lane = lax.broadcasted_iota(jnp.int32, (BLK, moved.shape[0]), 1)
    return dot(jnp.where(column(place[...]) == lane, 1.0, 0.0).astype(bfloat), moved[...])


def lower_norm(upper, scaled, factor, gain):
    inner = upper * gain
    return factor * (
        inner
        - jnp.mean(inner, -1, keepdims=True)
        - scaled * jnp.mean(inner * scaled, -1, keepdims=True)
    )


def close_kernel(
    place, moved, weight, lines, tok, tan, feed, feed_back, out, lower, g_weight, sums, g_acc
):
    i = pl.program_id(0)

    @pl.when(i == 0)
    def _():
        g_acc[...] = jnp.zeros_like(g_acc)
        sums[...] = jnp.zeros_like(sums)

    rows = tok[...].astype(single)
    tangent = tan[...]
    context = placed_rows(place, moved).astype(bfloat)
    attended = dot(context, weight[...]) + lines[4:5, :]
    out[...] = (rows + attended + (feed[...] + lines[5:6, :])).astype(bfloat)
    g_acc[...] += over_rows(context, tangent)
    scaled, factor = norm_stats(rows)
    upper = feed_back[...]
    wide = tangent.astype(single)
    lower[...] = wide + lower_norm(upper, scaled, factor, lines[2:3, :])
    sums[0:1, :] += jnp.sum(upper * scaled, 0, keepdims=True)
    sums[1:2, :] += jnp.sum(upper, 0, keepdims=True)
    sums[2:3, :] += jnp.sum(wide, 0, keepdims=True)

    @pl.when(i == pl.num_programs(0) - 1)
    def _():
        g_weight[...] = g_acc[...].astype(bfloat)


def close(place, moved, weights, lines, tok, tan, feed, feed_back):
    rows = tok.shape[0]
    tall = lambda width: pl.BlockSpec((BLK, width), lambda i: (i, 0))
    return pl.pallas_call(
        close_kernel,
        grid=(rows // BLK,),
        in_specs=[
            pl.BlockSpec((1, BLK), lambda i: (0, i)),
            whole(moved.shape),
            pl.BlockSpec((D, D), lambda i: (0, 3)),
            whole((16, D)),
            tall(D),
            tall(D),
            tall(D),
            tall(D),
        ],
        out_specs=[tall(D), tall(D), whole((D, D)), whole((8, D))],
        out_shape=[
            jax.ShapeDtypeStruct((rows, D), bfloat),
            jax.ShapeDtypeStruct((rows, D), single),
            jax.ShapeDtypeStruct((D, D), bfloat),
            jax.ShapeDtypeStruct((8, D), single),
        ],
        scratch_shapes=[pltpu.VMEM((D, D), single)],
        compiler_params=params(60),
        cost_estimate=pl.CostEstimate(
            flops=2 * rows * D * (moved.shape[0] + 2 * D), bytes_accessed=20 * MIB, transcendentals=0
        ),
        name="close",
    )(place, moved, weights, lines, tok, tan, feed, feed_back)


def finish_kernel(place, moved, lines, tok, lower, out):
    scaled, factor = norm_stats(tok[...].astype(single))
    upper = placed_rows(place, moved)
    out[...] = (lower[...] + lower_norm(upper, scaled, factor, lines[0:1, :])).astype(bfloat)


def finish(place, moved, lines, tok, lower):
    rows = tok.shape[0]
    tall = lambda width: pl.BlockSpec((BLK, width), lambda i: (i, 0))
    return pl.pallas_call(
        finish_kernel,
        grid=(rows // BLK,),
        in_specs=[
            pl.BlockSpec((1, BLK), lambda i: (0, i)),
            whole(moved.shape),
            whole((16, D)),
            tall(D),
            tall(D),
        ],
        out_specs=tall(D),
        out_shape=jax.ShapeDtypeStruct((rows, D), bfloat),
        compiler_params=params(60),
        cost_estimate=pl.CostEstimate(
            flops=2 * rows * D * moved.shape[0], bytes_accessed=12 * MIB, transcendentals=0
        ),
        name="finish",
    )(place, moved, lines, tok, lower)


def gather_all(x):
    return lax.all_gather(x, "dp", axis=0, tiled=True)


def body(
    tokens,
    cotangent,
    loss_mask,
    bucket_perm,
    short_lengths,
    row_owner,
    row_slot,
    first_gain,
    first_shift,
    second_gain,
    second_shift,
    project_weight,
    project_bias,
    output_weight,
    output_bias,
    up_weight,
    up_bias,
    down_weight,
    down_bias,
):
    devices = lax.axis_size("dp")
    me = lax.axis_index("dp")
    core = me % 2
    chip = me // 2
    rows = tokens.shape[0]
    share = LONG // devices // 4
    room = 3 * share
    long_count = devices // 4
    swap = [(i, i ^ 1) for i in range(devices)]

    def exchange(x):
        return lax.ppermute(x, "dp", swap)

    chips = devices // 2
    across = math.isqrt(chips // 4)
    sizes = {"core": 2, "x": across, "y": across, "z": 4}
    strides = {"core": 1, "x": 2, "y": 2 * across, "z": 2 * across * across}

    def shifted(x, name, shift):
        n, stride = sizes[name], strides[name]
        hop = []
        for d in range(devices):
            c = (d // stride) % n
            hop.append((d, d + ((c + shift) % n - c) * stride))
        return lax.ppermute(x, "dp", hop)

    def reduce_along(x, name, dim, kind=bfloat):
        n = sizes[name]
        at = (me // strides[name]) % n
        total = lax.dynamic_index_in_dim(x, at, dim, keepdims=False).astype(single)
        for shift in range(1, n):
            sent = lax.dynamic_index_in_dim(x, (at + shift) % n, dim, keepdims=False)
            total = total + shifted(sent, name, shift).astype(single)
        return total.astype(kind)

    def after(x, *others):
        return lax.optimization_barrier((x, *others))[0]

    piece = D // devices
    fours = FF // D
    count = jnp.sum(loss_mask)
    count_column = jnp.where(
        jnp.arange(piece) == 0, count // 256, jnp.where(jnp.arange(piece) == 1, count % 256, 0)
    )
    small = jnp.concatenate(
        [
            jnp.stack([first_gain, first_shift, second_gain, second_shift, output_bias, down_bias], 1),
            project_bias.reshape(3, piece).T,
            up_bias.reshape(piece, fours),
            count_column[:, None].astype(single),
        ],
        1,
    )
    small = jnp.pad(small, ((0, 0), (0, 128 - small.shape[1])))
    spread = jnp.arange(devices, dtype=jnp.int32)
    bucket = jnp.sum(jnp.where(bucket_perm[None, :] == row_owner[:, None], spread[None, :], 0), -1)
    hot = (row_owner[:, None] == spread[None, :]).astype(bfloat)
    line = jnp.arange(rows, dtype=jnp.int32)
    before = (line[None, :] < line[:, None]).astype(bfloat)
    rank = jnp.sum(dot(before, hot) * hot.astype(single), -1).astype(jnp.int32)
    is_long = bucket < long_count
    short = bucket - long_count
    third = jnp.where(is_long, 0, short % 3)
    to_chip = jnp.where(is_long, 2 * bucket, 2 * (short // 3) + 1)
    held = jnp.where(is_long, 2 * share, share)
    to_core = rank // held
    place = (2 * to_chip + to_core) * room + third * share + rank % held
    slot = third * SHORT_TOK + row_slot
    spots = jnp.arange(devices * room, dtype=jnp.int32)
    slot_at = jnp.sum(
        jnp.where(place[None, :] == spots[:, None], slot[None, :] + 1, 0), -1
    ) - 1
    slot_code = jnp.concatenate([(slot_at + 1) // 256, (slot_at + 1) % 256])
    slot_code = slot_code.astype(single).reshape(piece, 2 * devices * room // piece)
    first_all = gather_all(
        jnp.concatenate([project_weight, output_weight, small, slot_code], 1).astype(bfloat)
    )
    lines = first_all[:, 4 * D : 4 * D + 16].astype(single).T
    project_add = lines[6:9].reshape(3, devices, piece).transpose(1, 0, 2).reshape(1, 3, 2, HW)
    project_add_half = lax.dynamic_index_in_dim(project_add, core, 2, keepdims=False).reshape(
        1, 3 * HW
    )
    up_add = lines[9:13].reshape(fours, 1, D)
    counts = lines[13].reshape(devices, piece)
    scale = lax.rsqrt(jnp.sum(counts[:, 0]) * 256.0 + jnp.sum(counts[:, 1]))

    sender = (place[None, :] == spots[:, None]).astype(bfloat)
    place_line = place[None]

    def swap_all(x):
        return lax.all_to_all(x, "dp", split_axis=0, concat_axis=0, tiled=True)

    def outgoing(x):
        return dot(sender, x).astype(bfloat).reshape(devices, room, D)

    def arrange(moved):
        return moved.reshape(devices, 3, share, D).transpose(1, 0, 2, 3).reshape(3, PART, D)

    def send_back(x):
        moved = x.reshape(3, devices, share, D).transpose(1, 0, 2, 3).reshape(devices, room, D)
        return swap_all(moved).reshape(devices * room, D)

    code = first_all[:, 4 * D + 128 :].reshape(devices, 2, chips, 2 * room)
    code = lax.dynamic_index_in_dim(code, chip, 2, keepdims=False).astype(jnp.int32)
    slot_recv = (code[:, 0] * 256 + code[:, 1] - 1).reshape(devices, 2, 3, share)
    slot_recv = slot_recv.transpose(1, 2, 0, 3).reshape(2, 3, PART)
    slot_recv = jnp.where(core == 0, slot_recv, slot_recv[::-1])
    places = slot_recv.reshape(6, 1, PART)

    self_long = chip % 2 == 0
    lengths = lax.dynamic_slice_in_dim(short_lengths, 3 * (chip // 2), 3, 0)
    ends = jnp.cumsum(lengths, -1)
    at = jnp.arange(TOTAL, dtype=jnp.int32).reshape(3, SHORT_TOK)
    inside = jnp.arange(SHORT_TOK, dtype=jnp.int32)
    begun = jnp.max(
        jnp.where(ends[:, None, :] <= inside[None, :, None], ends[:, None, :], 0), -1
    )
    start = jnp.where(self_long, 0, begun + at - inside[None, :]).reshape(TOTAL)
    position = jnp.arange(TOTAL, dtype=jnp.int32) - start
    blocks = jnp.arange(TOTAL // BLK, dtype=jnp.int32)
    low_start = start[::BLK] // BLK
    high_start = (start[BLK - 1 :: BLK] + BLK - 1) // BLK
    zero = jnp.zeros_like(blocks)
    meta = jnp.stack(
        [
            low_start,
            jnp.minimum(blocks, jnp.maximum(low_start, high_start)),
            jnp.where(self_long & (blocks >= LONG // BLK), 0, 1),
            jnp.where(self_long, 0, blocks // (SHORT_TOK // BLK)),
            jnp.where(self_long, 2, 1) + zero,
            jnp.where(self_long, 0, 2 * (blocks % 3)),
            jnp.where(self_long, jnp.where(blocks % 3 == 2, 0, 4), 2 * (blocks % 3) + 2),
            core + zero,
        ]
    ).astype(jnp.int32)
    lane = jnp.arange(128, dtype=jnp.int32) % HEAD_DIM
    freq = 10000.0 ** (-2.0 * (lane % (ROT // 2)).astype(single) / ROT)
    phase = position.astype(single)[:, None] * freq[None, :]
    turning = (lane < ROT)[None, :]
    cosine = jnp.where(turning, jnp.cos(phase), 1.0)
    sine = jnp.where(turning, jnp.sin(phase) * jnp.where(lane < ROT // 2, -1.0, 1.0)[None, :], 0.0)
    starts = start.reshape(1, TOTAL)

    tangent = cotangent * loss_mask.astype(bfloat)[:, None]
    tokens_out = outgoing(tokens)
    tangent_out = outgoing(tangent)
    tokens_out, late_up, late_down = lax.optimization_barrier((tokens_out, up_weight, down_weight))
    up_mixed = late_up.astype(bfloat).reshape(piece, D, fours).transpose(0, 2, 1)
    down_mixed = late_down.astype(bfloat).reshape(piece, fours, D)
    feed_weights = gather_all(
        jnp.concatenate([up_mixed.reshape(piece, FF), down_mixed.reshape(piece, FF)], 1)
    )
    tokens_in = swap_all(tokens_out)
    tokens_in, places, meta, cosine, sine, starts, tangent_out = lax.optimization_barrier(
        (tokens_in, places, meta, cosine, sine, starts, tangent_out)
    )
    own = arrange(tokens_in)
    other = exchange(own)
    kept, q, k, kt, v, context, logsum, context_mine, context_theirs = forward(
        meta,
        places,
        own,
        other,
        lines,
        first_all,
        project_add_half,
        cosine,
        sine,
        starts,
    )

    tangent_in = swap_all(after(tangent_out, context_mine))

    feed, feed_back, wide, up_add_grad = feed_forward(
        after(tokens, context_mine), tangent, lines, feed_weights, up_add
    )
    wide_sum = lax.psum_scatter(wide, "dp", scatter_dimension=0, tiled=True).astype(single)

    mine, theirs = context_mine, exchange(context_theirs)
    context_out = jnp.concatenate(
        [jnp.where(core == 0, mine, theirs), jnp.where(core == 0, theirs, mine)], -1
    )
    context_moved = send_back(context_out)

    upper_own = arrange(after(tangent_in, feed))
    upper_other = exchange(upper_own)
    lower_mine, lower_theirs, *project_parts = backward(
        meta,
        places,
        upper_own,
        upper_other,
        q,
        k,
        kt,
        v,
        starts,
        context,
        logsum,
        kept,
        lines,
        first_all,
        cosine,
        sine,
    )
    lower_sum = (
        lower_mine.astype(single) + exchange(lower_theirs).astype(single)
    ).astype(bfloat)
    upper_moved = send_back(lower_sum)
    project_grad_half, project_add_half_grad, gain_one_grad, shift_one_grad = project_parts

    block_out, lower_two, output_grad, sums = close(
        place_line,
        after(context_moved, lower_sum),
        first_all,
        lines,
        tokens,
        tangent,
        feed,
        feed_back,
    )

    def pair_up(one, two):
        return jnp.where(
            core == 0, jnp.concatenate([one, two], -1), jnp.concatenate([two, one], -1)
        )

    add_half = project_add_half_grad.reshape(3, HW)
    project_add_grad = pair_up(add_half, jnp.zeros_like(add_half)).reshape(devices, 3, piece)
    vectors = jnp.concatenate(
        [
            gain_one_grad,
            shift_one_grad,
            sums[:3],
            project_add_grad.transpose(1, 0, 2).reshape(3, D),
            up_add_grad.reshape(fours, D),
            jnp.zeros((4, D), single),
        ],
        0,
    )
    def over_chips(x):
        return x.reshape((4, across, across) + x.shape[1:])

    extra = vectors.reshape(16, devices, piece).transpose(1, 0, 2).reshape(devices, 1, 16 * piece)
    extra = jnp.pad(extra, ((0, 0), (0, 7), (0, D - 16 * piece))).astype(bfloat)
    output_part = jnp.concatenate([output_grad.reshape(devices, piece, D), extra], 1)
    output_half = reduce_along(output_part.reshape(chips, 2, piece + 8, D), "core", 1)
    projects = project_grad_half.reshape(3, chips, 2 * piece, HW)
    one = over_chips(jnp.concatenate([projects[0], projects[1]], 1))
    two = over_chips(
        jnp.concatenate([projects[2], output_half[..., :HW], output_half[..., HW:]], 1)
    )
    one = reduce_along(reduce_along(one, "x", 2), "y", 1)
    two = reduce_along(reduce_along(two, "y", 1), "x", 1)
    narrow = reduce_along(jnp.concatenate([one, two], 1), "z", 0, single)

    by_core = narrow[: 6 * piece].reshape(3, 2, piece, HW)
    for_me = lax.dynamic_index_in_dim(by_core, core, 1, keepdims=False)
    for_other = lax.dynamic_index_in_dim(by_core, 1 - core, 1, keepdims=False)
    project_grad = pair_up(for_me, exchange(for_other)).transpose(1, 0, 2).reshape(piece, 3 * D)
    low_half, high_half = narrow[6 * piece : 7 * piece + 8], narrow[7 * piece + 8 :]
    output_sum = jnp.concatenate([low_half[:piece], high_half[:piece]], -1)
    vector_sum = jnp.concatenate([low_half[piece], high_half[piece]])[: 16 * piece]
    vector_sum = vector_sum.reshape(16, piece) * scale
    wide_sum = wide_sum.reshape(piece, fours, 2, D)
    up_sum = wide_sum[:, :, 0].transpose(0, 2, 1).reshape(piece, FF)
    down_sum = wide_sum[:, :, 1].reshape(fours * piece, D)
    scaled = lax.optimization_barrier(
        (upper_moved, vector_sum, project_grad * scale, output_sum * scale, up_sum * scale, down_sum * scale)
    )
    tokens_grad = finish(place_line, scaled[0], lines, tokens, lower_two)
    vector_sum, project_sum, output_sum, up_sum, down_sum = scaled[1:]
    return (
        block_out,
        tokens_grad,
        vector_sum[0],
        vector_sum[1],
        vector_sum[2],
        vector_sum[3],
        project_sum,
        vector_sum[5:8].reshape(3 * piece),
        output_sum,
        vector_sum[4],
        up_sum,
        vector_sum[8:12].T.reshape(fours * piece),
        down_sum,
        vector_sum[4],
    )


def solution(mesh):
    tall, flat = P("dp", None), P("dp")
    return jax.shard_map(
        body,
        mesh=mesh,
        in_specs=(
            tall,
            tall,
            flat,
            P(),
            P(),
            flat,
            flat,
            flat,
            flat,
            flat,
            flat,
            tall,
            flat,
            tall,
            flat,
            tall,
            flat,
            tall,
            flat,
        ),
        out_specs=(
            tall,
            tall,
            flat,
            flat,
            flat,
            flat,
            tall,
            flat,
            tall,
            flat,
            tall,
            flat,
            tall,
            flat,
        ),
        check_vma=False,
    )
```

time: 863 us -> 496 us (0.57)
  waiting for transfers between devices: 347 us -> 121 us
  blocking collectives: 113 us -> 0 us
  Pallas kernels: 203 us -> 235 us
  local copies, waits for them, and re-layouts: 68.3 us -> 36.4 us
  matrix products: 38.3 us -> 12.7 us
    reduce_scatter x3 -> x1, waiting for transfers between devices: 214 us -> 0.01 us  [body(): lax.psum_scatter(wide, 'dp', scatter_dimension=0, tiled=True).astype(single)]
    all_to_all x5 -> x4, waiting for transfers between devices: 122 us -> 4.8 us  [swap_all(): return lax.all_to_all(x, 'dp', split_axis=0, concat_axis=0, tiled=True)]
    all_gather x1 -> x0, blocking collectives: 75.5 us -> none  [gather_all(): return lax.all_gather(x, 'dp', axis=0, tiled=True)]
    all_gather x4 -> x2, waiting for transfers between devices: 0.04 us -> 59.1 us  [gather_all(): return lax.all_gather(x, 'dp', axis=0, tiled=True)]
    ppermute x0 -> x8, waiting for transfers between devices: none -> 47.3 us  [shifted(): return lax.ppermute(x, 'dp', hop)]
    unnamed x1 -> x0, blocking collectives: 38 us -> none
    pallas_call x8 -> x5, Pallas kernels: 203 us -> 235 us  [the longest x1 93.7 us: backward(): pl.pallas_call(backward_kernel, grid_spec=pltpu.PrefetchScalarGridSpec(nu...]
    dot_general x6 -> x3, matrix products: 35.1 us -> 12.7 us  [dot(): return jnp.dot(left, right, preferred_element_type=single)]
  transfers between devices with their start and end apart: 17 -> 20, of which waited for: 7 -> 14; matrix products, arithmetic and copies ran while one was open for 14% -> 12% of each run, Pallas kernels for 24% -> 46%
where the time goes in v2:
time: 496 us; the launch traced here: 490 us
  Pallas kernels  235 us (47%)
  waiting for transfers between devices  121 us (24%)
  starting transfers between devices  38.6 us (8%)
  local copies, waits for them, and re-layouts  36.4 us (7%)
  other arithmetic  26.8 us (5%)
  between operations  19.2 us (4%)
  matrix products  12.7 us (3%)
    pallas_call x1, Pallas kernels, backward(): pl.pallas_call(backward_kernel, grid_spec=pltpu.PrefetchScalarGridSpec(nu...  93.7 us
    pallas_call x1, Pallas kernels, forward(): pl.pallas_call(forward_kernel, grid_spec=pltpu.PrefetchScalarGridSpec(num...  67.4 us
    all_gather x2, waiting for transfers between devices, gather_all(): return lax.all_gather(x, 'dp', axis=0, tiled=True)  59.1 us
    pallas_call x1, Pallas kernels, feed_forward(): pl.pallas_call(feed_kernel, grid=(count,), in_specs=[one((rows, D)), one(...  48.1 us
    ppermute x8, waiting for transfers between devices, shifted(): return lax.ppermute(x, 'dp', hop)  47.3 us
    all_to_all x4, starting transfers between devices, swap_all(): return lax.all_to_all(x, 'dp', split_axis=0, concat_axis=0, tiled=True)  21.6 us
    pallas_call x1, Pallas kernels, close(): pl.pallas_call(close_kernel, grid=(rows // BLK,), in_specs=[pl.BlockSpec(...  16.4 us
    ppermute x8, starting transfers between devices, shifted(): return lax.ppermute(x, 'dp', hop)  15.8 us
  transfers between devices with their start and end apart: 20, of which 14 were waited for; matrix products, arithmetic and copies ran while one was open for 12% of the time, Pallas kernels for 46%

profile of v2, /device:TPU:0, one launch (start us, length us, event | category | flops | bytes accessed | tf_op | source)
XLA Modules:
  0.0 490.4 jit_solution(11135036518407132639)
XLA Ops:
  16.0 6.3 %fusion.5 = bf16[1536,768]{1,0:T(8,128)(2,1)} fusion(bf16[1280,768]{1,0:T(8,128)(2,1)} %tok.4, s32[1280]{0:T(1024)S(1)} %get-tuple-element.213), kind=kOutput, calls=%fused_computation.9 | convolution fusion | flops 3023044608 | bytes 4330496 | tf_op jit(solution)/shard_map/dot_general | solution.py:32
  24.2 7.8 %all-to-all-start = ((bf16[32,48,768]{2,1,0:T(8,128)(2,1)}), bf16[32,48,768]{2,1,0:T(8,128)(2,1)S(1)}, u32[]{:S(2)}, u32[]{:S(2)}) async-start(bf16[32,48,768]{2,1,0:T(8,128)(2,1)} %bitcast.192), calls=%async_computation | async-start | bytes 4718592 | tf_op jit(solution)/shard_map/all_to_all | solution.py:844
  35.3 4.8 fusion.6
  40.8 7.2 %fusion.10 = (f32[3072,128]{1,0:T(8,128)}, f32[3072,128]{1,0:T(8,128)}) fusion(f32[128]{0:T(128)S(1)} %get-tuple-element.218, f32[128]{0:T(128)S(1)} %get-tuple-element.219, f32[3072]{0:T(1024)S(1)} %get-tuple-element.172, pred[128]{0:T(512)(128)(4,1)S(1)} %broadcast_compare_fusion.1), kind=kLoop, calls=%fused_computation.17 | loop fusion | flops 1572864 | bytes 3159168 | tf_op jit(solution)/shard_map/jit(_where)/select_n | solution.py:894
  47.9 57.3 %all-gather.3.cloned.1.call-done.weight_q.weight_k.weight_v.weight_out.weight = bf16[768,3328]{1,0:T(8,128)(2,1)} async-done(((bf16[24,3328]{1,0:T(8,128)(2,1)}), bf16[768,3328]{1,0:T(8,128)(2,1)}) %all-gather.3.cloned.1.call-update) | async-done | bytes 5111824 | tf_op jit(solution)/shard_map/all_gather | solution.py:730
  111.7 3.2 collective-permute-done.other
  115.0 67.4 %forward.1 = (bf16[3072,768]{1,0:T(8,128)(2,1)}, bf16[3072,384]{1,0:T(8,128)(2,1)}, bf16[3072,384]{1,0:T(8,128)(2,1)}, bf16[384,3072]{1,0:T(8,128)(2,1)}, bf16[3...) custom-call(s32[8,12]{1,0:T(8,128)} %stack.53.meta, ...), custom_call_target="tpu_custom_call" | custom-call | flops 60000002048 | bytes 41943040 | tf_op jit(solution)/shard_map/forward/pallas_call | solution.py:364
  182.4 3.2 all-to-all-start.2
  188.7 48.1 %feed_forward.1 = (f32[1280,768]{1,0:T(8,128)}, f32[1280,768]{1,0:T(8,128)}, bf16[768,6144]{1,0:T(8,128)(2,1)}, f32[4,1,768]{2,1,0:T(1,128)}) custom-call(bf16[1280,768]{1,0:T(8,128)(2,1)} %tok.4, bf16[1280,768]{1,0:T(8,128)(2,1)} %copy-done.5, f32[16,768]{1,0:T(8,128)} %copy-done.10, bf16[768,6144]{1,0:T(8,128)(2,1)} %all-gather.5.cloned.1.call-done.up.down, ...), custom_call_target="tpu_custom_call" | custom-call | flops 36238786560 | bytes 50331648 | tf_op jit(solution)/shard_map/feed_forward/pallas_call | solution.py:113
  236.8 3.3 all-to-all-done.2
  242.2 5.3 %collective-permute-done.1 = bf16[3,512,384]{2,1,0:T(8,128)(2,1)S(1)} collective-permute-done((bf16[3,512,384]{2,1,0:T(8,128)(2,1)S(1)}, bf16[3,512,384]{2,1,0:T(8,128)(2,1)S(1)}, u32[]{:S(2)}, u32[]{:S(2)}) %collective-permute-start.1) | collective-permute-done | bytes 1179680 | tf_op jit(solution)/shard_map/ppermute | solution.py:765
  249.6 4.2 all-to-all-start.1
  256.0 93.7 %backward.1 = (bf16[3,512,768]{2,1,0:T(8,128)(2,1)}, bf16[3,512,768]{2,1,0:T(8,128)(2,1)}, bf16[3,768,384]{2,1,0:T(8,128)(2,1)}, f32[1,1152]{1,0:T(1,128)}, f32[1,768]{1,0:T(1,128)}, /*index=5*/f32[1,768]{1,0:T(1,128)}) custom-call(s32[8,12]{1,0:T(8,128)} %stack.53.meta, s32[6,1,512]{2,1,0:T(1,128)} %copy.234.places, bf16[3,512,768]{2,1,0:T(8,128)(2,1)} %bitcast.31.own, ...), custom_call_target="tpu_custom_call" | custom-call | flops 89999998976 | bytes 41943040 | tf_op jit(solution)/shard_map/backward/pallas_call | solution.py:545
  356.0 2.9 add_convert_fusion
  358.9 16.4 %close.1 = (bf16[1280,768]{1,0:T(8,128)(2,1)}, f32[1280,768]{1,0:T(8,128)}, bf16[768,768]{1,0:T(8,128)(2,1)}, f32[8,768]{1,0:T(8,128)}) custom-call(s32[1,1280]{1,0:T(1,128)} %fusion.58.place, bf16[1536,768]{1,0:T(8,128)(2,1)} %bitcast.25.moved, bf16[768,3328]{1,0:T(8,128)(2,1)} %all-gather.3.cloned.1.call-done.weight_q.weight_k.weight_v.weight_out.weight, ...), custom_call_target="tpu_custom_call" | custom-call | flops 6039797760 | bytes 20971520 | tf_op jit(solution)/shard_map/close/pallas_call | solution.py:671
  384.8 6.4 %all-to-all-start.3 = ((bf16[32,48,768]{2,1,0:T(8,128)(2,1)}), bf16[32,48,768]{2,1,0:T(8,128)(2,1)}, u32[]{:S(2)}, u32[]{:S(2)}) async-start(bf16[32,48,768]{2,1,0:T(8,128)(2,1)} %bitcast.183), calls=%async_computation.3 | async-start | bytes 4718592 | tf_op jit(solution)/shard_map/all_to_all | solution.py:844
  394.8 6.9 %collective-permute-done.4 = bf16[4,2,96,384]{3,2,0,1:T(8,128)(2,1)} collective-permute-done((bf16[4,2,96,384]{3,2,0,1:T(8,128)(2,1)}, bf16[4,2,96,384]{3,2,0,1:T(8,128)(2,1)}, u32[]{:S(2)}, u32[]{:S(2)}) %collective-permute-start.4) | collective-permute-done | bytes 589856 | tf_op jit(solution)/shard_map/ppermute | solution.py:778
  403.1 6.3 %collective-permute-start.5 = (bf16[4,96,384]{2,1,0:T(8,128)(2,1)S(1)}, bf16[4,96,384]{2,1,0:T(8,128)(2,1)S(1)}, u32[]{:S(2)}, u32[]{:S(2)}) collective-permute-start(bf16[4,96,384]{2,1,0:T(8,128)(2,1)S(1)} %dynamic-slice_bitcast_fusion.2), channel_id=1, source_target_pairs={{0,4},{1,5},{2,6},{3,7},{4,0},{5,1},{6,2},{7,3},{8,12},{9,13},{10,... | collective-permute-start | bytes 884744 | tf_op jit(solution)/shard_map/ppermute | solution.py:778
  409.4 21.1 %collective-permute-done.7 = bf16[4,2,112,384]{3,2,0,1:T(8,128)(2,1)S(1)} collective-permute-done((bf16[4,2,112,384]{3,2,0,1:T(8,128)(2,1)S(1)}, bf16[4,2,112,384]{3,2,0,1:T(8,128)(2,1)S(1)}, u32[]{:S(2)}, u32[]{:S(2)}) %collective-permute-start.7) | collective-permute-done | bytes 688160 | tf_op jit(solution)/shard_map/ppermute | solution.py:778
  433.1 4.9 collective-permute-done.5
  438.0 5.5 %collective-permute-done.8 = bf16[4,112,384]{2,1,0:T(8,128)(2,1)S(1)} collective-permute-done((bf16[4,112,384]{2,1,0:T(8,128)(2,1)S(1)}, bf16[4,112,384]{2,1,0:T(8,128)(2,1)S(1)}, u32[]{:S(2)}, u32[]{:S(2)}) %collective-permute-start.8) | collective-permute-done | bytes 344096 | tf_op jit(solution)/shard_map/ppermute | solution.py:778
  443.7 4.6 collective-permute-start.11
  452.9 7.8 %collective-permute-done.10 = bf16[208,384]{1,0:T(8,128)(2,1)S(1)} collective-permute-done((bf16[208,384]{1,0:T(8,128)(2,1)S(1)}, bf16[208,384]{1,0:T(8,128)(2,1)S(1)}, u32[]{:S(2)}, u32[]{:S(2)}) %collective-permute-start.10) | collective-permute-done | bytes 159776 | tf_op jit(solution)/shard_map/ppermute | solution.py:778
  473.5 9.6 %finish.1 = bf16[1280,768]{1,0:T(8,128)(2,1)} custom-call(s32[1,1280]{1,0:T(1,128)} %fusion.58.place, bf16[1536,768]{1,0:T(8,128)(2,1)} %bitcast.35.moved, f32[16,768]{1,0:T(8,128)} %copy-done.10, bf16[1280,768]{1,0:T(8,128)(2,1)} %tok.4, f32[1280,768]{1,0:T(8,128)} %get-tuple-element.94.lower), custom_call_target="tpu_custom_call" | custom-call | flops 3019898880 | bytes 12582912 | tf_op jit(solution)/shard_map/finish/pallas_call | solution.py:709
  (263 shorter events, 66.7 us)
Async XLA Ops:
  7.3 97.9 %all-gather.3.cloned.1.call-start = ((), (), s32[]{:S(2)}) async-start(), calls=%async_computation.5 | async-start | bytes 5271552 | tf_op jit(solution)/shard_map/all_gather | solution.py:730
  16.0 172.7 %all-gather.5.cloned.1.call-start = ((), (), s32[]{:S(2)}) async-start(), calls=%async_computation.6 | async-start | bytes 9732096 | tf_op jit(solution)/shard_map/all_gather | solution.py:730
  24.2 84.4 %all-to-all-start = ((bf16[32,48,768]{2,1,0:T(8,128)(2,1)}), bf16[32,48,768]{2,1,0:T(8,128)(2,1)S(1)}, u32[]{:S(2)}, u32[]{:S(2)}) async-start(bf16[32,48,768]{2,1,0:T(8,128)(2,1)} %bitcast.192), calls=%async_computation | async-start | bytes 4718592 | tf_op jit(solution)/shard_map/all_to_all | solution.py:844
  110.1 4.9 collective-permute-start
  182.4 57.7 %all-to-all-start.2 = ((bf16[32,48,768]{2,1,0:T(8,128)(2,1)}), bf16[32,48,768]{2,1,0:T(8,128)(2,1)S(1)}, u32[]{:S(2)}, u32[]{:S(2)}) async-start(bf16[32,48,768]{2,1,0:T(8,128)(2,1)} %bitcast.193), calls=%async_computation.2 | async-start | bytes 4718592 | tf_op jit(solution)/shard_map/all_to_all | solution.py:844
  241.7 12.8 %collective-permute-start.2 = (bf16[3,512,768]{2,1,0:T(8,128)(2,1)}, bf16[3,512,768]{2,1,0:T(8,128)(2,1)S(1)}, u32[]{:S(2)}, u32[]{:S(2)}) collective-permute-start(bf16[3,512,768]{2,1,0:T(8,128)(2,1)} %bitcast.31.own), channel_id=1, source_target_pairs={{0,1},{1,0},{2,3},{3,2},{4,5},{5,4},{6,7},{7,6},{8,9},{9,8},{10,11... | collective-permute-start | bytes 7077896 | tf_op jit(solution)/shard_map/ppermute | solution.py:765
  241.7 5.8 %collective-permute-start.1 = (bf16[3,512,384]{2,1,0:T(8,128)(2,1)S(1)}, bf16[3,512,384]{2,1,0:T(8,128)(2,1)S(1)}, u32[]{:S(2)}, u32[]{:S(2)}) collective-permute-start(bf16[3,512,384]{2,1,0:T(8,128)(2,1)S(1)} %copy-done.27), channel_id=1, source_target_pairs={{0,1},{1,0},{2,3},{3,2},{4,5},{5,4},{6,7},{7,6},{8,9},{9,8},{10,11... | collective-permute-start | bytes 3538952 | tf_op jit(solution)/shard_map/ppermute | solution.py:765
  249.6 109.3 %all-to-all-start.1 = ((bf16[32,48,768]{2,1,0:T(8,128)(2,1)}), bf16[32,48,768]{2,1,0:T(8,128)(2,1)}, u32[]{:S(2)}, u32[]{:S(2)}) async-start(bf16[32,48,768]{2,1,0:T(8,128)(2,1)} %bitcast.24), calls=%async_computation.1 | async-start | bytes 4718592 | tf_op jit(solution)/shard_map/all_to_all | solution.py:844
  253.8 209.3 %reduce-scatter.2.cloned.1.call-start = ((), (), s32[]{:S(2)}) async-start(), calls=%async_computation.7 | async-start | bytes 9732096 | tf_op jit(solution)/shard_map/reduce_scatter | solution.py:930
  256.0 94.1 %copy-start.16 = (s32[1280]{0:T(1024)S(1)}, s32[1280]{0:T(1024)}, u32[]{:S(2)}) copy-start(s32[1280]{0:T(1024)} %get-tuple-element.215) | copy-start | bytes 15364
  256.0 94.1 %copy-start.18 = (pred[1280]{0:T(1024)(128)(4,1)S(1)}, pred[1280]{0:T(1024)(128)(4,1)}, u32[]{:S(2)}) copy-start(pred[1280]{0:T(1024)(128)(4,1)} %copy-done.17) | copy-start | bytes 3844
  256.0 94.1 %copy-start.23 = (pred[1280]{0:T(1024)(128)(4,1)S(1)}, pred[1280]{0:T(1024)(128)(4,1)}, u32[]{:S(2)}) copy-start(pred[1280]{0:T(1024)(128)(4,1)} %get-tuple-element.214) | copy-start | bytes 3844
  256.0 95.5 %copy-start.19 = (f32[4,1,768]{2,1,0:T(1,128)S(1)}, f32[4,1,768]{2,1,0:T(1,128)}, u32[]{:S(2)}) copy-start(f32[4,1,768]{2,1,0:T(1,128)} %get-tuple-element.91) | copy-start | bytes 36868
  349.8 4.8 collective-permute-start.3
  380.4 10.8 %collective-permute-start.6 = (bf16[16,32,768]{2,1,0:T(8,128)(2,1)}, bf16[16,32,768]{2,1,0:T(8,128)(2,1)}, u32[]{:S(2)}, u32[]{:S(2)}) collective-permute-start(bf16[16,32,768]{2,1,0:T(8,128)(2,1)} %dynamic-slice_bitcast_fusion), channel_id=1, source_target_pairs={{0,1},{1,0},{2,3},{3,2},{4,5},{5,4},{6,7},{7,6},{8,9},{9,8},{10,11... | collective-permute-start | bytes 2359304 | tf_op jit(solution)/shard_map/ppermute | solution.py:778
  383.2 18.6 %collective-permute-start.4 = (bf16[4,2,96,384]{3,2,0,1:T(8,128)(2,1)}, bf16[4,2,96,384]{3,2,0,1:T(8,128)(2,1)}, u32[]{:S(2)}, u32[]{:S(2)}) collective-permute-start(bf16[4,2,96,384]{3,2,0,1:T(8,128)(2,1)} %bitcast.177), channel_id=1, source_target_pairs={{0,2},{1,3},{2,0},{3,1},{4,6},{5,7},{6,4},{7,5},{8,10},{9,11},{10,... | collective-permute-start | bytes 1769480 | tf_op jit(solution)/shard_map/ppermute | solution.py:778
  384.8 85.6 %all-to-all-start.3 = ((bf16[32,48,768]{2,1,0:T(8,128)(2,1)}), bf16[32,48,768]{2,1,0:T(8,128)(2,1)}, u32[]{:S(2)}, u32[]{:S(2)}) async-start(bf16[32,48,768]{2,1,0:T(8,128)(2,1)} %bitcast.183), calls=%async_computation.3 | async-start | bytes 4718592 | tf_op jit(solution)/shard_map/all_to_all | solution.py:844
  393.1 37.4 %collective-permute-start.7 = (bf16[4,2,112,384]{3,2,0,1:T(8,128)(2,1)S(1)}, bf16[4,2,112,384]{3,2,0,1:T(8,128)(2,1)S(1)}, u32[]{:S(2)}, u32[]{:S(2)}) collective-permute-start(bf16[4,2,112,384]{3,2,0,1:T(8,128)(2,1)S(1)} %bitcast.201), channel_id=1, source_target_pairs={{0,4},{1,5},{2,6},{3,7},{4,0},{5,1},{6,2},{7,3},{8,12},{9,13},{10,... | collective-permute-start | bytes 2064392 | tf_op jit(solution)/shard_map/ppermute | solution.py:778
  403.1 34.9 %collective-permute-start.5 = (bf16[4,96,384]{2,1,0:T(8,128)(2,1)S(1)}, bf16[4,96,384]{2,1,0:T(8,128)(2,1)S(1)}, u32[]{:S(2)}, u32[]{:S(2)}) collective-permute-start(bf16[4,96,384]{2,1,0:T(8,128)(2,1)S(1)} %dynamic-slice_bitcast_fusion.2), channel_id=1, source_target_pairs={{0,4},{1,5},{2,6},{3,7},{4,0},{5,1},{6,2},{7,3},{8,12},{9,13},{10,... | collective-permute-start | bytes 884744 | tf_op jit(solution)/shard_map/ppermute | solution.py:778
  430.7 12.8 %collective-permute-start.8 = (bf16[4,112,384]{2,1,0:T(8,128)(2,1)S(1)}, bf16[4,112,384]{2,1,0:T(8,128)(2,1)S(1)}, u32[]{:S(2)}, u32[]{:S(2)}) collective-permute-start(bf16[4,112,384]{2,1,0:T(8,128)(2,1)S(1)} %dynamic-slice_bitcast_fusion.1), channel_id=1, source_target_pairs={{0,2},{1,3},{2,0},{3,1},{4,6},{5,7},{6,4},{7,5},{8,10},{9,11},{10,... | collective-permute-start | bytes 1032200 | tf_op jit(solution)/shard_map/ppermute | solution.py:778
  443.7 9.2 %collective-permute-start.11 = (bf16[208,384]{1,0:T(8,128)(2,1)S(1)}, bf16[208,384]{1,0:T(8,128)(2,1)S(1)}, u32[]{:S(2)}, u32[]{:S(2)}) collective-permute-start(bf16[208,384]{1,0:T(8,128)(2,1)S(1)} %get-tuple-element.193), channel_id=1, source_target_pairs={{0,24},{1,25},{2,26},{3,27},{4,28},{5,29},{6,30},{7,31},{8,0},{9,1... | collective-permute-start | bytes 479240 | tf_op jit(solution)/shard_map/ppermute | solution.py:778
  448.3 12.4 %collective-permute-start.10 = (bf16[208,384]{1,0:T(8,128)(2,1)S(1)}, bf16[208,384]{1,0:T(8,128)(2,1)S(1)}, u32[]{:S(2)}, u32[]{:S(2)}) collective-permute-start(bf16[208,384]{1,0:T(8,128)(2,1)S(1)} %get-tuple-element.192), channel_id=1, source_target_pairs={{0,16},{1,17},{2,18},{3,19},{4,20},{5,21},{6,22},{7,23},{8,24},{9,... | collective-permute-start | bytes 479240 | tf_op jit(solution)/shard_map/ppermute | solution.py:778
  448.3 12.4 %collective-permute-start.9 = (bf16[208,384]{1,0:T(8,128)(2,1)S(1)}, bf16[208,384]{1,0:T(8,128)(2,1)S(1)}, u32[]{:S(2)}, u32[]{:S(2)}) collective-permute-start(bf16[208,384]{1,0:T(8,128)(2,1)S(1)} %get-tuple-element.191), channel_id=1, source_target_pairs={{0,8},{1,9},{2,10},{3,11},{4,12},{5,13},{6,14},{7,15},{8,16},{9,17... | collective-permute-start | bytes 479240 | tf_op jit(solution)/shard_map/ppermute | solution.py:778
  461.0 1.4 collective-permute-start.12
  (33 other events, 450.7 us)
Sparse Core Ops, SparseCore 0:
  16.1 89.1 all-gather.2
  108.7 79.8 all-gather.4
  260.5 137.0 reduce-scatter.1

commit v3 on v2

--- a/solution.py
+++ b/solution.py
@@ -48,6 +48,15 @@
     return (centred * factor, factor)
 
 
+def lower_norm(upper, scaled, factor, gain):
+    inner = upper * gain
+    return factor * (
+        inner
+        - jnp.mean(inner, -1, keepdims=True)
+        - scaled * jnp.mean(inner * scaled, -1, keepdims=True)
+    )
+
+
 def params(mib):
     return pltpu.CompilerParams(vmem_limit_bytes=mib * MIB)
 
@@ -57,7 +66,7 @@
 
 
 def feed_kernel(
-    tok, tan, lines, up, up_add, down, feed, lower, grad, g_up_add, normed, act, slope
+    tok, tan, lines, up, up_add, down, feed, lower, grad, g_up_add, sums, normed, act, slope
 ):
     step = pl.program_id(0)
     rows = tok.shape[0]
@@ -103,6 +112,21 @@
     grad[:, :D] = over_rows(normed[...], slope[...]).astype(bfloat)
     grad[:, D:] = over_rows(act[...], tan[...]).astype(bfloat)
 
+    @pl.when(step == pl.num_programs(0) - 1)
+    def _():
+        def one(i, carry):
+            r = pl.ds(pl.multiple_of(i * BLK, BLK), BLK)
+            scaled, factor = norm_stats(tok[r, :].astype(single))
+            upper, wide = lower[r, :], tan[r, :].astype(single)
+            lower[r, :] = wide + lower_norm(upper, scaled, factor, lines[2:3, :])
+            terms = (upper * scaled, upper, wide)
+            return tuple(c + jnp.sum(t, 0, keepdims=True) for c, t in zip(carry, terms))
+
+        parts = lax.fori_loop(0, rows // BLK, one, (jnp.zeros((1, D), single),) * 3)
+        sums[...] = jnp.zeros_like(sums)
+        for i in range(3):
+            sums[i : i + 1, :] = parts[i]
+
 
 def feed_forward(tok, tan, lines, weights, up_add):
     rows, count = tok.shape[0], FF // D
@@ -114,12 +138,13 @@
         feed_kernel,
         grid=(count,),
         in_specs=[one((rows, D)), one((rows, D)), one((16, D)), wide(0), line, wide(count)],
-        out_specs=[one((rows, D)), one((rows, D)), pair, line],
+        out_specs=[one((rows, D)), one((rows, D)), pair, line, one((8, D))],
         out_shape=[
             jax.ShapeDtypeStruct((rows, D), single),
             jax.ShapeDtypeStruct((rows, D), single),
             jax.ShapeDtypeStruct((D, 2 * count * D), bfloat),
             jax.ShapeDtypeStruct((count, 1, D), single),
+            jax.ShapeDtypeStruct((8, D), single),
         ],
         scratch_shapes=[
             pltpu.VMEM((rows, D), bfloat),
@@ -180,7 +205,7 @@
 def turn_lanes(values, cosine, sine):
     lane = lax.broadcasted_iota(jnp.int32, values.shape, 1)
     swapped = jnp.where(
-        lax.rem(lane, ROT) < ROT // 2, pltpu.roll(values, 128 - ROT // 2, 1), pltpu.roll(values, ROT // 2, 1)
+        (lane & (ROT - 1)) < ROT // 2, pltpu.roll(values, 128 - ROT // 2, 1), pltpu.roll(values, ROT // 2, 1)
     )
     return values * cosine + swapped * sine
 
@@ -412,7 +437,7 @@
         ],
         compiler_params=params(60),
         cost_estimate=pl.CostEstimate(
-            flops=60 * 10**9, bytes_accessed=40 * MIB, transcendentals=NH * LONG * LONG // 2
+            flops=75 * 10**9, bytes_accessed=40 * MIB, transcendentals=NH * LONG * LONG // 2
         ),
         name="forward",
     )(meta, places, own, other, lines, weight, weight, weight, add, cosine, sine, start)
@@ -440,6 +465,7 @@
     sine,
     mine,
     theirs,
+    g_out,
     g_weight,
     g_add,
     g_gain,
@@ -452,6 +478,7 @@
     dqt,
     probs,
     slopes,
+    out_acc,
     g_acc,
     lower,
     back_acc,
@@ -462,13 +489,15 @@
 
     @pl.when(step_at == 0)
     def _():
-        for ref in (g_acc, g_add, g_gain, g_shift):
+        for ref in (out_acc, g_acc, g_add, g_gain, g_shift):
             ref[...] = jnp.zeros_like(ref)
 
     @pl.when((step_at < BLOCKS) & (meta[2, i] > 0))
     def _():
         gather_rows(meta, i, places, own, other, rows)
-        upper[...] = against(rows[...].astype(bfloat), weight_out[...]).astype(bfloat)
+        tangent = rows[...].astype(bfloat)
+        upper[...] = against(tangent, weight_out[...]).astype(bfloat)
+        out_acc[...] += over_rows(context[...].astype(bfloat), tangent)
         queries = [of_head(q[:, lanes_of(h)], h) for h in range(NH)]
         uppers = [of_head(upper[:, lanes_of(h)], h) for h in range(NH)]
         both = (upper[...].astype(single) * context[...]).T
@@ -529,6 +558,7 @@
 
     @pl.when(step_at == 2 * BLOCKS)
     def _():
+        g_out[...] = out_acc[...].astype(bfloat)
         for s in range(3):
             g_weight[s] = g_acc[:, s * HW : (s + 1) * HW].astype(bfloat)
 
@@ -567,6 +597,7 @@
             ],
             out_specs=[
                 *parts_at(2 * BLOCKS, D),
+                held(HW, D),
                 held(3, D, HW),
                 held(1, 3 * HW),
                 held(1, D),
@@ -581,6 +612,7 @@
                 pltpu.VMEM((HW, BLK), single),
                 pltpu.VMEM((NH // 2, BLK, 2 * BLK), bfloat),
                 pltpu.VMEM((NH // 2, BLK, 2 * BLK), bfloat),
+                pltpu.VMEM((HW, D), single),
                 pltpu.VMEM((D, 3 * HW), single),
                 pltpu.VMEM((TOTAL, D), bfloat),
                 pltpu.VMEM((PART, D), single),
@@ -589,6 +621,7 @@
         out_shape=[
             jax.ShapeDtypeStruct((3, PART, D), bfloat),
             jax.ShapeDtypeStruct((3, PART, D), bfloat),
+            jax.ShapeDtypeStruct((HW, D), bfloat),
             jax.ShapeDtypeStruct((3, D, HW), bfloat),
             jax.ShapeDtypeStruct((1, 3 * HW), single),
             jax.ShapeDtypeStruct((1, D), single),
@@ -627,45 +660,13 @@
     return dot(jnp.where(column(place[...]) == lane, 1.0, 0.0).astype(bfloat), moved[...])
 
 
-def lower_norm(upper, scaled, factor, gain):
-    inner = upper * gain
-    return factor * (
-        inner
-        - jnp.mean(inner, -1, keepdims=True)
-        - scaled * jnp.mean(inner * scaled, -1, keepdims=True)
-    )
-
-
-def close_kernel(
-    place, moved, weight, lines, tok, tan, feed, feed_back, out, lower, g_weight, sums, g_acc
-):
-    i = pl.program_id(0)
-
-    @pl.when(i == 0)
-    def _():
-        g_acc[...] = jnp.zeros_like(g_acc)
-        sums[...] = jnp.zeros_like(sums)
-
-    rows = tok[...].astype(single)
-    tangent = tan[...]
+def close_kernel(place, moved, weight, lines, tok, feed, out):
     context = placed_rows(place, moved).astype(bfloat)
     attended = dot(context, weight[...]) + lines[4:5, :]
-    out[...] = (rows + attended + (feed[...] + lines[5:6, :])).astype(bfloat)
-    g_acc[...] += over_rows(context, tangent)
-    scaled, factor = norm_stats(rows)
-    upper = feed_back[...]
-    wide = tangent.astype(single)
-    lower[...] = wide + lower_norm(upper, scaled, factor, lines[2:3, :])
-    sums[0:1, :] += jnp.sum(upper * scaled, 0, keepdims=True)
-    sums[1:2, :] += jnp.sum(upper, 0, keepdims=True)
-    sums[2:3, :] += jnp.sum(wide, 0, keepdims=True)
-
-    @pl.when(i == pl.num_programs(0) - 1)
-    def _():
-        g_weight[...] = g_acc[...].astype(bfloat)
-
-
-def close(place, moved, weights, lines, tok, tan, feed, feed_back):
+    out[...] = (tok[...].astype(single) + attended + (feed[...] + lines[5:6, :])).astype(bfloat)
+
+
+def close(place, moved, weights, lines, tok, feed):
     rows = tok.shape[0]
     tall = lambda width: pl.BlockSpec((BLK, width), lambda i: (i, 0))
     return pl.pallas_call(
@@ -678,23 +679,15 @@
             whole((16, D)),
             tall(D),
             tall(D),
-            tall(D),
-            tall(D),
         ],
-        out_specs=[tall(D), tall(D), whole((D, D)), whole((8, D))],
-        out_shape=[
-            jax.ShapeDtypeStruct((rows, D), bfloat),
-            jax.ShapeDtypeStruct((rows, D), single),
-            jax.ShapeDtypeStruct((D, D), bfloat),
-            jax.ShapeDtypeStruct((8, D), single),
-        ],
-        scratch_shapes=[pltpu.VMEM((D, D), single)],
+        out_specs=tall(D),
+        out_shape=jax.ShapeDtypeStruct((rows, D), bfloat),
         compiler_params=params(60),
         cost_estimate=pl.CostEstimate(
-            flops=2 * rows * D * (moved.shape[0] + 2 * D), bytes_accessed=20 * MIB, transcendentals=0
+            flops=12 * 10**9, bytes_accessed=12 * MIB, transcendentals=0
         ),
         name="close",
-    )(place, moved, weights, lines, tok, tan, feed, feed_back)
+    )(place, moved, weights, lines, tok, feed)
 
 
 def finish_kernel(place, moved, lines, tok, lower, out):
@@ -777,17 +770,18 @@
             hop.append((d, d + ((c + shift) % n - c) * stride))
         return lax.ppermute(x, "dp", hop)
 
-    def reduce_along(x, name, dim, kind=bfloat):
+    def after(x, *others):
+        return lax.optimization_barrier((x, *others))[0]
+
+    def reduce_along(x, name, dim, kind=bfloat, late=None):
         n = sizes[name]
         at = (me // strides[name]) % n
         total = lax.dynamic_index_in_dim(x, at, dim, keepdims=False).astype(single)
         for shift in range(1, n):
             sent = lax.dynamic_index_in_dim(x, (at + shift) % n, dim, keepdims=False)
-            total = total + shifted(sent, name, shift).astype(single)
+            got = shifted(sent, name, shift)
+            total = total + (got if late is None else after(got, late)).astype(single)
         return total.astype(kind)
-
-    def after(x, *others):
-        return lax.optimization_barrier((x, *others))[0]
 
     piece = D // devices
     fours = FF // D
@@ -924,15 +918,15 @@
 
     tangent_in = swap_all(after(tangent_out, context_mine))
 
-    feed, feed_back, wide, up_add_grad = feed_forward(
-        after(tokens, context_mine), tangent, lines, feed_weights, up_add
-    )
-    wide_sum = lax.psum_scatter(wide, "dp", scatter_dimension=0, tiled=True).astype(single)
-
     mine, theirs = context_mine, exchange(context_theirs)
     context_out = jnp.concatenate(
         [jnp.where(core == 0, mine, theirs), jnp.where(core == 0, theirs, mine)], -1
     )
+    feed, lower_two, wide, up_add_grad, sums = feed_forward(
+        after(tokens, context_out), tangent, lines, feed_weights, up_add
+    )
+    wide_sum = lax.psum_scatter(wide, "dp", scatter_dimension=0, tiled=True).astype(single)
+
     context_moved = send_back(context_out)
 
     upper_own = arrange(after(tangent_in, feed))
@@ -959,17 +953,12 @@
         lower_mine.astype(single) + exchange(lower_theirs).astype(single)
     ).astype(bfloat)
     upper_moved = send_back(lower_sum)
-    project_grad_half, project_add_half_grad, gain_one_grad, shift_one_grad = project_parts
-
-    block_out, lower_two, output_grad, sums = close(
-        place_line,
-        after(context_moved, lower_sum),
-        first_all,
-        lines,
-        tokens,
-        tangent,
-        feed,
-        feed_back,
+    output_half_grad, project_grad_half, project_add_half_grad, gain_one_grad, shift_one_grad = (
+        project_parts
+    )
+
+    block_out = close(
+        place_line, after(context_moved, lower_sum), first_all, lines, tokens, feed
     )
 
     def pair_up(one, two):
@@ -995,33 +984,37 @@
 
     extra = vectors.reshape(16, devices, piece).transpose(1, 0, 2).reshape(devices, 1, 16 * piece)
     extra = jnp.pad(extra, ((0, 0), (0, 7), (0, D - 16 * piece))).astype(bfloat)
+    empty = jnp.zeros_like(output_half_grad)
+    output_grad = jnp.where(
+        core == 0,
+        jnp.concatenate([output_half_grad, empty], 0),
+        jnp.concatenate([empty, output_half_grad], 0),
+    )
     output_part = jnp.concatenate([output_grad.reshape(devices, piece, D), extra], 1)
     output_half = reduce_along(output_part.reshape(chips, 2, piece + 8, D), "core", 1)
-    projects = project_grad_half.reshape(3, chips, 2 * piece, HW)
-    one = over_chips(jnp.concatenate([projects[0], projects[1]], 1))
-    two = over_chips(
-        jnp.concatenate([projects[2], output_half[..., :HW], output_half[..., HW:]], 1)
-    )
-    one = reduce_along(reduce_along(one, "x", 2), "y", 1)
-    two = reduce_along(reduce_along(two, "y", 1), "x", 1)
-    narrow = reduce_along(jnp.concatenate([one, two], 1), "z", 0, single)
-
-    by_core = narrow[: 6 * piece].reshape(3, 2, piece, HW)
-    for_me = lax.dynamic_index_in_dim(by_core, core, 1, keepdims=False)
-    for_other = lax.dynamic_index_in_dim(by_core, 1 - core, 1, keepdims=False)
-    project_grad = pair_up(for_me, exchange(for_other)).transpose(1, 0, 2).reshape(piece, 3 * D)
-    low_half, high_half = narrow[6 * piece : 7 * piece + 8], narrow[7 * piece + 8 :]
-    output_sum = jnp.concatenate([low_half[:piece], high_half[:piece]], -1)
-    vector_sum = jnp.concatenate([low_half[piece], high_half[piece]])[: 16 * piece]
-    vector_sum = vector_sum.reshape(16, piece) * scale
+    by_core = project_grad_half.reshape(3, chips, 2, piece, HW)
+    for_me = lax.dynamic_index_in_dim(by_core, core, 2, keepdims=False)
+    for_other = lax.dynamic_index_in_dim(by_core, 1 - core, 2, keepdims=False)
+    projects = pair_up(for_me, exchange(for_other))
+    narrow = over_chips(
+        jnp.concatenate([projects[0], projects[1], projects[2], output_half], 1)
+    )
+    cut = narrow.shape[3] // 16 * 8
+    one = reduce_along(narrow[..., :cut, :], "x", 2, late=block_out)
+    two = reduce_along(narrow[..., cut:, :], "y", 1, late=block_out)
+    one = reduce_along(one, "y", 1)
+    two = reduce_along(two, "x", 1)
     wide_sum = wide_sum.reshape(piece, fours, 2, D)
     up_sum = wide_sum[:, :, 0].transpose(0, 2, 1).reshape(piece, FF)
     down_sum = wide_sum[:, :, 1].reshape(fours * piece, D)
-    scaled = lax.optimization_barrier(
-        (upper_moved, vector_sum, project_grad * scale, output_sum * scale, up_sum * scale, down_sum * scale)
-    )
-    tokens_grad = finish(place_line, scaled[0], lines, tokens, lower_two)
-    vector_sum, project_sum, output_sum, up_sum, down_sum = scaled[1:]
+    upper_moved, up_sum, down_sum = lax.optimization_barrier(
+        (upper_moved, up_sum * scale, down_sum * scale)
+    )
+    tokens_grad = finish(place_line, upper_moved, lines, tokens, lower_two)
+    narrow = reduce_along(jnp.concatenate([one, two], 1), "z", 0, single, tokens_grad) * scale
+    project_sum = narrow[: 3 * piece].reshape(3, piece, D).transpose(1, 0, 2).reshape(piece, 3 * D)
+    output_sum = narrow[3 * piece : 4 * piece]
+    vector_sum = narrow[4 * piece, : 16 * piece].reshape(16, piece)
     return (
         block_out,
         tokens_grad,

time: 496 us -> 472 us (0.952)
  waiting for transfers between devices: 121 us -> 92.7 us
  other arithmetic: 26.8 us -> 33 us
    ppermute x8, waiting for transfers between devices: 47.3 us -> 25.5 us  [shifted(): return lax.ppermute(x, 'dp', hop)]
    ppermute x5, waiting for transfers between devices: 9.67 us -> 3.26 us  [exchange(): return lax.ppermute(x, 'dp', swap)]
    pallas_call x1, Pallas kernels: 16.4 us -> 10.1 us  [close(): pl.pallas_call(close_kernel, grid=(rows // BLK,), in_specs=[pl.BlockSpec(...]
    pallas_call x1, Pallas kernels: 48.1 us -> 54.1 us  [feed_forward(): pl.pallas_call(feed_kernel, grid=(count,), in_specs=[one((rows, D)), one(...]
  transfers between devices with their start and end apart: 20 -> 20, of which waited for: 14 -> 6; matrix products, arithmetic and copies ran while one was open for 12% -> 14% of each run, Pallas kernels for 46% -> 51%
where the time goes in v3:
time: 472 us; the launch traced here: 466 us
  Pallas kernels  236 us (50%)
  waiting for transfers between devices  92.7 us (20%)
  starting transfers between devices  37.4 us (8%)
  local copies, waits for them, and re-layouts  34.9 us (7%)
  other arithmetic  33 us (7%)
  between operations  19.2 us (4%)
  matrix products  12.6 us (3%)
    pallas_call x1, Pallas kernels, backward(): pl.pallas_call(backward_kernel, grid_spec=pltpu.PrefetchScalarGridSpec(nu...  94.6 us
    pallas_call x1, Pallas kernels, forward(): pl.pallas_call(forward_kernel, grid_spec=pltpu.PrefetchScalarGridSpec(num...  67.4 us
    all_gather x2, waiting for transfers between devices, gather_all(): return lax.all_gather(x, 'dp', axis=0, tiled=True)  57.5 us
    pallas_call x1, Pallas kernels, feed_forward(): pl.pallas_call(feed_kernel, grid=(count,), in_specs=[one((rows, D)), one(...  54.1 us
    ppermute x8, waiting for transfers between devices, shifted(): return lax.ppermute(x, 'dp', hop)  25.5 us
    all_to_all x4, starting transfers between devices, swap_all(): return lax.all_to_all(x, 'dp', split_axis=0, concat_axis=0, tiled=True)  22.3 us
    ppermute x8, starting transfers between devices, shifted(): return lax.ppermute(x, 'dp', hop)  13.7 us
    dot_general x3, matrix products, dot(): return jnp.dot(left, right, preferred_element_type=single)  12.6 us
  transfers between devices with their start and end apart: 20, of which 6 were waited for; matrix products, arithmetic and copies ran while one was open for 14% of the time, Pallas kernels for 51%

profile of v3, /device:TPU:0, one launch (start us, length us, event | category | flops | bytes accessed | tf_op | source)
XLA Modules:
  0.0 465.7 jit_solution(17361625087911244214)
XLA Ops:
  16.0 6.3 %fusion.5 = bf16[1536,768]{1,0:T(8,128)(2,1)} fusion(bf16[1280,768]{1,0:T(8,128)(2,1)} %tok.4, s32[1280]{0:T(1024)S(1)} %get-tuple-element.191), kind=kOutput, calls=%fused_computation.9 | convolution fusion | flops 3023044608 | bytes 4330496 | tf_op jit(solution)/shard_map/dot_general | solution.py:32
  24.1 7.8 %all-to-all-start = ((bf16[32,48,768]{2,1,0:T(8,128)(2,1)}), bf16[32,48,768]{2,1,0:T(8,128)(2,1)S(1)}, u32[]{:S(2)}, u32[]{:S(2)}) async-start(bf16[32,48,768]{2,1,0:T(8,128)(2,1)} %bitcast.198), calls=%async_computation | async-start | bytes 4718592 | tf_op jit(solution)/shard_map/all_to_all | solution.py:838
  33.5 1.8 broadcast_multiply_fusion.tan
  35.3 4.7 %fusion.6 = bf16[1536,768]{1,0:T(8,128)(2,1)} fusion(bf16[1280,768]{1,0:T(8,128)(2,1)S(1)} %broadcast_multiply_fusion.tan, s32[1280]{0:T(1024)S(1)} %get-tuple-element.191), kind=kOutput, calls=%fused_computation.10 | convolution fusion | flops 3023044608 | bytes 4330496 | tf_op jit(solution)/shard_map/dot_general | solution.py:32
  40.7 7.2 %fusion.10 = (f32[3072,128]{1,0:T(8,128)}, f32[3072,128]{1,0:T(8,128)}) fusion(f32[128]{0:T(128)S(1)} %get-tuple-element.196, f32[128]{0:T(128)S(1)} %get-tuple-element.197, f32[3072]{0:T(1024)S(1)} %get-tuple-element.158, pred[128]{0:T(512)(128)(4,1)S(1)} %broadcast_compare_fusion.1), kind=kLoop, calls=%fused_computation.20 | loop fusion | flops 1572864 | bytes 3159168 | tf_op jit(solution)/shard_map/jit(_where)/select_n | solution.py:888
  47.8 57.5 %all-gather.3.cloned.1.call-done.weight_q.weight_k.weight_v.weight_out.weight = bf16[768,3328]{1,0:T(8,128)(2,1)} async-done(((bf16[24,3328]{1,0:T(8,128)(2,1)}), bf16[768,3328]{1,0:T(8,128)(2,1)}) %all-gather.3.cloned.1.call-update) | async-done | bytes 5111824 | tf_op jit(solution)/shard_map/all_gather | solution.py:723
  111.8 3.2 collective-permute-done.other
  115.0 67.4 %forward.1 = (bf16[3072,768]{1,0:T(8,128)(2,1)}, bf16[3072,384]{1,0:T(8,128)(2,1)}, bf16[3072,384]{1,0:T(8,128)(2,1)}, bf16[384,3072]{1,0:T(8,128)(2,1)}, bf16[3...) custom-call(s32[8,12]{1,0:T(8,128)} %stack.53.meta, ...), custom_call_target="tpu_custom_call" | custom-call | flops 74999996416 | bytes 41943040 | tf_op jit(solution)/shard_map/forward/pallas_call | solution.py:389
  182.6 3.2 all-to-all-start.2
  190.4 54.1 %feed_forward.1 = (f32[1280,768]{1,0:T(8,128)}, f32[1280,768]{1,0:T(8,128)}, bf16[768,6144]{1,0:T(8,128)(2,1)}, f32[4,1,768]{2,1,0:T(1,128)}, f32[8,768]{1,0:T(8,128)}) custom-call(bf16[1280,768]{1,0:T(8,128)(2,1)} %tok.4, bf16[1280,768]{1,0:T(8,128)(2,1)} %copy-done.6, f32[16,768]{1,0:T(8,128)} %copy-done.13, ...), custom_call_target="tpu_custom_call" | custom-call | flops 36238786560 | bytes 50331648 | tf_op jit(solution)/shard_map/feed_forward/pallas_call | solution.py:137
  248.6 6.0 %all-to-all-start.1 = ((bf16[32,48,768]{2,1,0:T(8,128)(2,1)}), bf16[32,48,768]{2,1,0:T(8,128)(2,1)}, u32[]{:S(2)}, u32[]{:S(2)}) async-start(bf16[32,48,768]{2,1,0:T(8,128)(2,1)} %bitcast.24), calls=%async_computation.1 | async-start | bytes 4718592 | tf_op jit(solution)/shard_map/all_to_all | solution.py:838
  256.8 94.6 %backward.1 = (bf16[3,512,768]{2,1,0:T(8,128)(2,1)}, bf16[3,512,768]{2,1,0:T(8,128)(2,1)}, bf16[384,768]{1,0:T(8,128)(2,1)}, bf16[3,768,384]{2,1,0:T(8,128)(2,1)...) custom-call(s32[8,12]{1,0:T(8,128)} %stack.53.meta, s32[6,1,512]{2,1,0:T(1,128)} %copy.172.places, ...), custom_call_target="tpu_custom_call" | custom-call | flops 89999998976 | bytes 41943040 | tf_op jit(solution)/shard_map/backward/pallas_call | solution.py:575
  360.1 2.3 add_convert_fusion
  363.9 5.2 %all-to-all-start.3 = ((bf16[32,48,768]{2,1,0:T(8,128)(2,1)}), bf16[32,48,768]{2,1,0:T(8,128)(2,1)}, u32[]{:S(2)}, u32[]{:S(2)}) async-start(bf16[32,48,768]{2,1,0:T(8,128)(2,1)} %bitcast.34), calls=%async_computation.3 | async-start | bytes 4718592 | tf_op jit(solution)/shard_map/all_to_all | solution.py:838
  371.8 2.2 maximum_select_fusion
  375.0 1.9 collective-permute-start.8
  378.5 10.1 %close.1 = bf16[1280,768]{1,0:T(8,128)(2,1)} custom-call(s32[1,1280]{1,0:T(1,128)} %fusion.63.place, bf16[1536,768]{1,0:T(8,128)(2,1)} %bitcast.25.moved, bf16[768,3328]{1,0:T(8,128)(2,1)} %all-gather.3.cloned.1.call-done.weight_q.weight_k.weight_v.weight_out.weight, f32[16,768]{1,0:T(8,128)} %copy-done.13, bf16[1280,768]{1,0:T(8,128)(2,1)} %tok.4, ...), custom_call_target="tpu_custom_call" | custom-call | flops 12000000000 | bytes 12582912 | tf_op jit(solution)/shard_map/close/pallas_call | solution.py:672
  388.6 19.2 %collective-permute-done.8 = bf16[4,2,56,768]{3,2,1,0:T(8,128)(2,1)S(1)} collective-permute-done((bf16[4,2,56,768]{3,2,1,0:T(8,128)(2,1)}, bf16[4,2,56,768]{3,2,1,0:T(8,128)(2,1)S(1)}, u32[]{:S(2)}, u32[]{:S(2)}) %collective-permute-start.8) | collective-permute-done | bytes 688160 | tf_op jit(solution)/shard_map/ppermute | solution.py:771
  414.0 6.3 %collective-permute-done.6 = bf16[4,48,768]{2,1,0:T(8,128)(2,1)} collective-permute-done((bf16[4,48,768]{2,1,0:T(8,128)(2,1)S(1)}, bf16[4,48,768]{2,1,0:T(8,128)(2,1)}, u32[]{:S(2)}, u32[]{:S(2)}) %collective-permute-start.6) | collective-permute-done | bytes 294944 | tf_op jit(solution)/shard_map/ppermute | solution.py:771
  422.3 5.4 %collective-permute-start.12 = (bf16[104,768]{1,0:T(8,128)(2,1)}, bf16[104,768]{1,0:T(8,128)(2,1)}, u32[]{:S(2)}, u32[]{:S(2)}) collective-permute-start(bf16[104,768]{1,0:T(8,128)(2,1)} %get-tuple-element.175), channel_id=1, source_target_pairs={{0,24},{1,25},{2,26},{3,27},{4,28},{5,29},{6,30},{7,31},{8,0},{9,1... | collective-permute-start | bytes 479240 | tf_op jit(solution)/shard_map/ppermute | solution.py:771
  427.7 1.8 collective-permute-start.10
  435.8 1.7 copy.182
  438.4 4.4 all-to-all-done.3
  442.8 9.6 %finish.1 = bf16[1280,768]{1,0:T(8,128)(2,1)} custom-call(s32[1,1280]{1,0:T(1,128)} %fusion.63.place, bf16[1536,768]{1,0:T(8,128)(2,1)} %bitcast.35.moved, f32[16,768]{1,0:T(8,128)} %copy-done.13, bf16[1280,768]{1,0:T(8,128)(2,1)} %tok.4, f32[1280,768]{1,0:T(8,128)} %get-tuple-element.85.lower), custom_call_target="tpu_custom_call" | custom-call | flops 3019898880 | bytes 12582912 | tf_op jit(solution)/shard_map/finish/pallas_call | solution.py:702
  (262 shorter events, 62.4 us)
Async XLA Ops:
  7.2 24.9 %copy-start = (s32[24,3]{0,1:T(4,128)S(1)}, s32[24,3]{0,1:T(4,128)}, u32[]{:S(2)}) copy-start(s32[24,3]{0,1:T(4,128)} %param.23) | copy-start | bytes 868
  7.3 98.0 %all-gather.3.cloned.1.call-start = ((), (), s32[]{:S(2)}) async-start(), calls=%async_computation.5 | async-start | bytes 5271552 | tf_op jit(solution)/shard_map/all_gather | solution.py:723
  16.0 174.4 %all-gather.5.cloned.1.call-start = ((), (), s32[]{:S(2)}) async-start(), calls=%async_computation.6 | async-start | bytes 9732096 | tf_op jit(solution)/shard_map/all_gather | solution.py:723
  24.1 84.4 %all-to-all-start = ((bf16[32,48,768]{2,1,0:T(8,128)(2,1)}), bf16[32,48,768]{2,1,0:T(8,128)(2,1)S(1)}, u32[]{:S(2)}, u32[]{:S(2)}) async-start(bf16[32,48,768]{2,1,0:T(8,128)(2,1)} %bitcast.198), calls=%async_computation | async-start | bytes 4718592 | tf_op jit(solution)/shard_map/all_to_all | solution.py:838
  110.1 4.9 %collective-permute-start = (bf16[3,512,768]{2,1,0:T(8,128)(2,1)}, bf16[3,512,768]{2,1,0:T(8,128)(2,1)}, u32[]{:S(2)}, u32[]{:S(2)}) collective-permute-start(bf16[3,512,768]{2,1,0:T(8,128)(2,1)} %bitcast.18.own), channel_id=1, source_target_pairs={{0,1},{1,0},{2,3},{3,2},{4,5},{5,4},{6,7},{7,6},{8,9},{9,8},{10,11... | collective-permute-start | bytes 7077896 | tf_op jit(solution)/shard_map/ppermute | solution.py:758
  182.4 4.7 %collective-permute-start.1 = (bf16[3,512,384]{2,1,0:T(8,128)(2,1)}, bf16[3,512,384]{2,1,0:T(8,128)(2,1)}, u32[]{:S(2)}, u32[]{:S(2)}) collective-permute-start(bf16[3,512,384]{2,1,0:T(8,128)(2,1)} %get-tuple-element.65), channel_id=1, source_target_pairs={{0,1},{1,0},{2,3},{3,2},{4,5},{5,4},{6,7},{7,6},{8,9},{9,8},{10,11... | collective-permute-start | bytes 3538952 | tf_op jit(solution)/shard_map/ppermute | solution.py:758
  182.6 61.9 %all-to-all-start.2 = ((bf16[32,48,768]{2,1,0:T(8,128)(2,1)}), bf16[32,48,768]{2,1,0:T(8,128)(2,1)S(1)}, u32[]{:S(2)}, u32[]{:S(2)}) async-start(bf16[32,48,768]{2,1,0:T(8,128)(2,1)} %bitcast.199), calls=%async_computation.2 | async-start | bytes 4718592 | tf_op jit(solution)/shard_map/all_to_all | solution.py:838
  246.1 9.2 %collective-permute-start.2 = (bf16[3,512,768]{2,1,0:T(8,128)(2,1)}, bf16[3,512,768]{2,1,0:T(8,128)(2,1)S(1)}, u32[]{:S(2)}, u32[]{:S(2)}) collective-permute-start(bf16[3,512,768]{2,1,0:T(8,128)(2,1)} %bitcast.31.own), channel_id=1, source_target_pairs={{0,1},{1,0},{2,3},{3,2},{4,5},{5,4},{6,7},{7,6},{8,9},{9,8},{10,11... | collective-permute-start | bytes 7077896 | tf_op jit(solution)/shard_map/ppermute | solution.py:758
  248.6 115.3 %all-to-all-start.1 = ((bf16[32,48,768]{2,1,0:T(8,128)(2,1)}), bf16[32,48,768]{2,1,0:T(8,128)(2,1)}, u32[]{:S(2)}, u32[]{:S(2)}) async-start(bf16[32,48,768]{2,1,0:T(8,128)(2,1)} %bitcast.24), calls=%async_computation.1 | async-start | bytes 4718592 | tf_op jit(solution)/shard_map/all_to_all | solution.py:838
  254.6 174.9 %reduce-scatter.2.cloned.1.call-start = ((), (), s32[]{:S(2)}) async-start(), calls=%async_computation.7 | async-start | bytes 9732096 | tf_op jit(solution)/shard_map/reduce_scatter | solution.py:928
  256.8 94.9 %copy-start.16 = (f32[1280]{0:T(1024)S(1)}, f32[1280]{0:T(1024)}, u32[]{:S(2)}) copy-start(f32[1280]{0:T(1024)} %copy-done.15) | copy-start | bytes 15364
  256.8 95.7 %copy-start.22 = (f32[4,1,768]{2,1,0:T(1,128)S(1)}, f32[4,1,768]{2,1,0:T(1,128)}, u32[]{:S(2)}) copy-start(f32[4,1,768]{2,1,0:T(1,128)} %get-tuple-element.93) | copy-start | bytes 36868
  351.4 7.9 %collective-permute-start.3 = (bf16[3,512,768]{2,1,0:T(8,128)(2,1)}, bf16[3,512,768]{2,1,0:T(8,128)(2,1)}, u32[]{:S(2)}, u32[]{:S(2)}) collective-permute-start(bf16[3,512,768]{2,1,0:T(8,128)(2,1)} %get-tuple-element.81), channel_id=1, source_target_pairs={{0,1},{1,0},{2,3},{3,2},{4,5},{5,4},{6,7},{7,6},{8,9},{9,8},{10,11... | collective-permute-start | bytes 7077896 | tf_op jit(solution)/shard_map/ppermute | solution.py:758
  357.2 14.4 %collective-permute-start.7 = (bf16[16,32,768]{2,1,0:T(8,128)(2,1)}, bf16[16,32,768]{2,1,0:T(8,128)(2,1)S(1)}, u32[]{:S(2)}, u32[]{:S(2)}) collective-permute-start(bf16[16,32,768]{2,1,0:T(8,128)(2,1)} %dynamic-slice_bitcast_fusion.2), channel_id=1, source_target_pairs={{0,1},{1,0},{2,3},{3,2},{4,5},{5,4},{6,7},{7,6},{8,9},{9,8},{10,11... | collective-permute-start | bytes 2359304 | tf_op jit(solution)/shard_map/ppermute | solution.py:771
  358.9 12.9 %collective-permute-start.4 = (bf16[3,16,24,384]{3,2,1,0:T(8,128)(2,1)}, bf16[3,16,24,384]{3,2,1,0:T(8,128)(2,1)}, u32[]{:S(2)}, u32[]{:S(2)}) collective-permute-start(bf16[3,16,24,384]{3,2,1,0:T(8,128)(2,1)} %get-tuple-element.172), channel_id=1, source_target_pairs={{0,1},{1,0},{2,3},{3,2},{4,5},{5,4},{6,7},{7,6},{8,9},{9,8},{10,11... | collective-permute-start | bytes 2654216 | tf_op jit(solution)/shard_map/ppermute | solution.py:758
  363.9 78.9 %all-to-all-start.3 = ((bf16[32,48,768]{2,1,0:T(8,128)(2,1)}), bf16[32,48,768]{2,1,0:T(8,128)(2,1)}, u32[]{:S(2)}, u32[]{:S(2)}) async-start(bf16[32,48,768]{2,1,0:T(8,128)(2,1)} %bitcast.34), calls=%async_computation.3 | async-start | bytes 4718592 | tf_op jit(solution)/shard_map/all_to_all | solution.py:838
  375.0 32.8 %collective-permute-start.8 = (bf16[4,2,56,768]{3,2,1,0:T(8,128)(2,1)}, bf16[4,2,56,768]{3,2,1,0:T(8,128)(2,1)S(1)}, u32[]{:S(2)}, u32[]{:S(2)}) collective-permute-start(bf16[4,2,56,768]{3,2,1,0:T(8,128)(2,1)} %fusion.16), channel_id=1, source_target_pairs={{0,4},{1,5},{2,6},{3,7},{4,0},{5,1},{6,2},{7,3},{8,12},{9,13},{10,... | collective-permute-start | bytes 2064392 | tf_op jit(solution)/shard_map/ppermute | solution.py:771
  377.0 30.9 %collective-permute-start.5 = (bf16[4,2,48,768]{3,2,1,0:T(8,128)(2,1)S(1)}, bf16[4,2,48,768]{3,2,1,0:T(8,128)(2,1)}, u32[]{:S(2)}, u32[]{:S(2)}) collective-permute-start(bf16[4,2,48,768]{3,2,1,0:T(8,128)(2,1)S(1)} %fusion.21), channel_id=1, source_target_pairs={{0,2},{1,3},{2,0},{3,1},{4,6},{5,7},{6,4},{7,5},{8,10},{9,11},{10,... | collective-permute-start | bytes 1769480 | tf_op jit(solution)/shard_map/ppermute | solution.py:771
  409.1 11.2 %collective-permute-start.6 = (bf16[4,48,768]{2,1,0:T(8,128)(2,1)S(1)}, bf16[4,48,768]{2,1,0:T(8,128)(2,1)}, u32[]{:S(2)}, u32[]{:S(2)}) collective-permute-start(bf16[4,48,768]{2,1,0:T(8,128)(2,1)S(1)} %dynamic-slice_bitcast_fusion.4), channel_id=1, source_target_pairs={{0,4},{1,5},{2,6},{3,7},{4,0},{5,1},{6,2},{7,3},{8,12},{9,13},{10,... | collective-permute-start | bytes 884744 | tf_op jit(solution)/shard_map/ppermute | solution.py:771
  410.3 11.0 %collective-permute-start.9 = (bf16[4,56,768]{2,1,0:T(8,128)(2,1)S(1)}, bf16[4,56,768]{2,1,0:T(8,128)(2,1)S(1)}, u32[]{:S(2)}, u32[]{:S(2)}) collective-permute-start(bf16[4,56,768]{2,1,0:T(8,128)(2,1)S(1)} %dynamic-slice_bitcast_fusion.3), channel_id=1, source_target_pairs={{0,2},{1,3},{2,0},{3,1},{4,6},{5,7},{6,4},{7,5},{8,10},{9,11},{10,... | collective-permute-start | bytes 1032200 | tf_op jit(solution)/shard_map/ppermute | solution.py:771
  421.3 10.9 %copy-start.3 = (bf16[4,48,768]{2,1,0:T(8,128)(2,1)}, bf16[4,48,768]{2,1,0:T(8,128)(2,1)S(1)}, u32[]{:S(2)}) copy-start(bf16[4,48,768]{2,1,0:T(8,128)(2,1)S(1)} %fusion.24) | copy-start | bytes 884740
  422.3 30.2 %collective-permute-start.12 = (bf16[104,768]{1,0:T(8,128)(2,1)}, bf16[104,768]{1,0:T(8,128)(2,1)}, u32[]{:S(2)}, u32[]{:S(2)}) collective-permute-start(bf16[104,768]{1,0:T(8,128)(2,1)} %get-tuple-element.175), channel_id=1, source_target_pairs={{0,24},{1,25},{2,26},{3,27},{4,28},{5,29},{6,30},{7,31},{8,0},{9,1... | collective-permute-start | bytes 479240 | tf_op jit(solution)/shard_map/ppermute | solution.py:771
  427.7 24.8 %collective-permute-start.11 = (bf16[104,768]{1,0:T(8,128)(2,1)}, bf16[104,768]{1,0:T(8,128)(2,1)}, u32[]{:S(2)}, u32[]{:S(2)}) collective-permute-start(bf16[104,768]{1,0:T(8,128)(2,1)} %get-tuple-element.174), channel_id=1, source_target_pairs={{0,16},{1,17},{2,18},{3,19},{4,20},{5,21},{6,22},{7,23},{8,24},{9,... | collective-permute-start | bytes 479240 | tf_op jit(solution)/shard_map/ppermute | solution.py:771
  427.7 24.8 %collective-permute-start.10 = (bf16[104,768]{1,0:T(8,128)(2,1)}, bf16[104,768]{1,0:T(8,128)(2,1)}, u32[]{:S(2)}, u32[]{:S(2)}) collective-permute-start(bf16[104,768]{1,0:T(8,128)(2,1)} %get-tuple-element.173), channel_id=1, source_target_pairs={{0,8},{1,9},{2,10},{3,11},{4,12},{5,13},{6,14},{7,15},{8,16},{9,17... | collective-permute-start | bytes 479240 | tf_op jit(solution)/shard_map/ppermute | solution.py:771
  (35 other events, 164.1 us)
Sparse Core Ops, SparseCore 0:
  16.1 89.2 all-gather.2
  108.8 79.8 all-gather.4
  261.4 152.6 reduce-scatter.1

commit v4 on v3

--- a/solution.py
+++ b/solution.py
@@ -18,6 +18,8 @@
 TOTAL = 3 * SHORT_TOK
 BLK = 256
 BLOCKS = TOTAL // BLK
+WIDE = 512
+STEPS = TOTAL // WIDE
 NH = HEADS // 2
 HW = NH * HEAD_DIM
 PART = SHORT_TOK // 2
@@ -98,15 +100,8 @@
         part_feed = dot(active, down[...])
         part_lower = against(sl, up[...])
 
-        @pl.when(step == 0)
-        def _():
-            feed[r, :] = part_feed
-            lower[r, :] = part_lower
-
-        @pl.when(step > 0)
-        def _():
-            feed[r, :] += part_feed
-            lower[r, :] += part_lower
+        feed[r, :] = jnp.where(step > 0, feed[r, :], 0.0) + part_feed
+        lower[r, :] = jnp.where(step > 0, lower[r, :], 0.0) + part_lower
 
     g_up_add[0] = bias_sum
     grad[:, :D] = over_rows(normed[...], slope[...]).astype(bfloat)
@@ -348,11 +343,6 @@
         context[...] = turned
         done[here, :] = turned.astype(bfloat)
 
-    @pl.when((step_at < BLOCKS) & (meta[2, i] == 0))
-    def _():
-        for ref in (kept, q, k, kt, v, context, logsum):
-            ref[...] = jnp.zeros_like(ref)
-
     @pl.when(step_at >= BLOCKS)
     def _():
         return_rows(meta, jnp.maximum(step_at - BLOCKS, 0), places, done, mine, theirs, back_acc)
@@ -369,12 +359,16 @@
     return pl.BlockSpec(shape, lambda i, m: (0,) * len(shape), pipeline_mode=pl.Buffered(1))
 
 
-def tall_at(width, first):
-    return pl.BlockSpec((BLK, width), lambda i, m: (jnp.clip(i - first, 0, BLOCKS - 1), 0))
-
-
-def flat_at(height, first):
-    return pl.BlockSpec((height, BLK), lambda i, m: (0, jnp.clip(i - first, 0, BLOCKS - 1)))
+def tall_at(width):
+    return pl.BlockSpec((BLK, width), lambda i, m: (jnp.minimum(i, m[8, 0]), 0))
+
+
+def flat_at(height):
+    return pl.BlockSpec((height, BLK), lambda i, m: (0, jnp.minimum(i, m[8, 0])))
+
+
+def wide_at(width):
+    return pl.BlockSpec((WIDE, width), lambda i, m: (jnp.clip(i - BLOCKS, 0, m[8, 0] // 2), 0))
 
 
 def parts_at(first, width):
@@ -398,18 +392,18 @@
                 held(16, D),
                 *columns(),
                 held(1, 3 * HW),
-                tall_at(128, 0),
-                tall_at(128, 0),
-                flat_at(1, 0),
+                tall_at(128),
+                tall_at(128),
+                flat_at(1),
             ],
             out_specs=[
-                tall_at(D, 0),
-                tall_at(HW, 0),
-                tall_at(HW, 0),
-                flat_at(HW, 0),
-                tall_at(HW, 0),
-                tall_at(HW, 0),
-                flat_at(8, 0),
+                tall_at(D),
+                tall_at(HW),
+                tall_at(HW),
+                flat_at(HW),
+                tall_at(HW),
+                tall_at(HW),
+                flat_at(8),
                 *parts_at(BLOCKS, HW),
             ],
             scratch_shapes=[
@@ -485,7 +479,7 @@
 ):
     step_at = pl.program_id(0)
     i = jnp.minimum(step_at, BLOCKS - 1)
-    b = jnp.clip(step_at - BLOCKS, 0, BLOCKS - 1)
+    b = jnp.clip(step_at - BLOCKS, 0, STEPS - 1)
 
     @pl.when(step_at == 0)
     def _():
@@ -534,9 +528,9 @@
         over_blocks(meta, i, step)
         dq[block_of(i), :] = dqt[...].T * HEAD_DIM ** (-0.5)
 
-    @pl.when((step_at >= BLOCKS) & (step_at < 2 * BLOCKS) & (meta[2, b] > 0))
-    def _():
-        r = block_of(b)
+    @pl.when((step_at >= BLOCKS) & (step_at < BLOCKS + STEPS) & (meta[2, 2 * b] > 0))
+    def _():
+        r = pl.ds(pl.multiple_of(b * WIDE, WIDE), WIDE)
         turned = []
         for ref in (dq, dk):
             for p in range(0, HW, 128):
@@ -556,16 +550,16 @@
         normed = (scaled * lines[0:1, :] + lines[1:2, :]).astype(bfloat)
         g_acc[...] += over_rows(normed, mixed)
 
-    @pl.when(step_at == 2 * BLOCKS)
+    @pl.when(step_at == BLOCKS + STEPS)
     def _():
         g_out[...] = out_acc[...].astype(bfloat)
         for s in range(3):
             g_weight[s] = g_acc[:, s * HW : (s + 1) * HW].astype(bfloat)
 
-    @pl.when(step_at >= 2 * BLOCKS)
+    @pl.when(step_at >= BLOCKS + STEPS)
     def _():
         return_rows(
-            meta, jnp.maximum(step_at - 2 * BLOCKS, 0), places, lower, mine, theirs, back_acc
+            meta, jnp.maximum(step_at - BLOCKS - STEPS, 0), places, lower, mine, theirs, back_acc
         )
 
 
@@ -576,27 +570,27 @@
         backward_kernel,
         grid_spec=pltpu.PrefetchScalarGridSpec(
             num_scalar_prefetch=1,
-            grid=(2 * BLOCKS + 6,),
+            grid=(BLOCKS + STEPS + 6,),
             in_specs=[
                 held(6, 1, PART),
                 held(3, PART, D),
                 held(3, PART, D),
                 pl.BlockSpec((HW, D), lambda i, m: (m[7, 0], 3), pipeline_mode=pl.Buffered(1)),
-                tall_at(HW, 0),
+                tall_at(HW),
                 held(TOTAL, HW),
                 held(HW, TOTAL),
                 held(TOTAL, HW),
-                flat_at(1, 0),
-                tall_at(HW, 0),
-                flat_at(8, 0),
-                tall_at(D, BLOCKS),
+                flat_at(1),
+                tall_at(HW),
+                flat_at(8),
+                wide_at(D),
                 held(16, D),
                 *columns(),
-                tall_at(128, BLOCKS),
-                tall_at(128, BLOCKS),
+                wide_at(128),
+                wide_at(128),
             ],
             out_specs=[
-                *parts_at(2 * BLOCKS, D),
+                *parts_at(BLOCKS + STEPS, D),
                 held(HW, D),
                 held(3, D, HW),
                 held(1, 3 * HW),
@@ -878,6 +872,7 @@
             jnp.where(self_long, 0, 2 * (blocks % 3)),
             jnp.where(self_long, jnp.where(blocks % 3 == 2, 0, 4), 2 * (blocks % 3) + 2),
             core + zero,
+            jnp.where(self_long, LONG // BLK, BLOCKS) - 1 + zero,
         ]
     ).astype(jnp.int32)
     lane = jnp.arange(128, dtype=jnp.int32) % HEAD_DIM

time: 472 us -> 465 us (0.985)
  Pallas kernels: 236 us -> 229 us
  transfers between devices with their start and end apart: 20 -> 20, of which waited for: 6 -> 7; matrix products, arithmetic and copies ran while one was open for 14% -> 14% of each run, Pallas kernels for 51% -> 50%
where the time goes in v4:
time: 465 us; the launch traced here: 459 us
  Pallas kernels  229 us (49%)
  waiting for transfers between devices  93.2 us (20%)
  starting transfers between devices  37 us (8%)
  local copies, waits for them, and re-layouts  35.5 us (8%)
  other arithmetic  33.1 us (7%)
  between operations  19.1 us (4%)
  matrix products  12.6 us (3%)
    pallas_call x1, Pallas kernels, backward(): pl.pallas_call(backward_kernel, grid_spec=pltpu.PrefetchScalarGridSpec(nu...  92.1 us
    pallas_call x1, Pallas kernels, forward(): pl.pallas_call(forward_kernel, grid_spec=pltpu.PrefetchScalarGridSpec(num...  66.3 us
    all_gather x2, waiting for transfers between devices, gather_all(): return lax.all_gather(x, 'dp', axis=0, tiled=True)  57.1 us
    pallas_call x1, Pallas kernels, feed_forward(): pl.pallas_call(feed_kernel, grid=(count,), in_specs=[one((rows, D)), one(...  50.5 us
    ppermute x8, waiting for transfers between devices, shifted(): return lax.ppermute(x, 'dp', hop)  24.9 us
    all_to_all x4, starting transfers between devices, swap_all(): return lax.all_to_all(x, 'dp', split_axis=0, concat_axis=0, tiled=True)  21.6 us
    ppermute x8, starting transfers between devices, shifted(): return lax.ppermute(x, 'dp', hop)  13.9 us
    dot_general x3, matrix products, dot(): return jnp.dot(left, right, preferred_element_type=single)  12.6 us
  transfers between devices with their start and end apart: 20, of which 7 were waited for; matrix products, arithmetic and copies ran while one was open for 14% of the time, Pallas kernels for 50%

profile of v4, /device:TPU:0, one launch (start us, length us, event | category | flops | bytes accessed | tf_op | source)
XLA Modules:
  0.0 459.1 jit_solution(17301926860501766075)
XLA Ops:
  16.0 6.3 %fusion.5 = bf16[1536,768]{1,0:T(8,128)(2,1)} fusion(bf16[1280,768]{1,0:T(8,128)(2,1)} %tok.4, s32[1280]{0:T(1024)S(1)} %get-tuple-element.191), kind=kOutput, calls=%fused_computation.9 | convolution fusion | flops 3023044608 | bytes 4330496 | tf_op jit(solution)/shard_map/dot_general | solution.py:34
  24.1 7.5 %all-to-all-start = ((bf16[32,48,768]{2,1,0:T(8,128)(2,1)}), bf16[32,48,768]{2,1,0:T(8,128)(2,1)S(1)}, u32[]{:S(2)}, u32[]{:S(2)}) async-start(bf16[32,48,768]{2,1,0:T(8,128)(2,1)} %bitcast.198), calls=%async_computation | async-start | bytes 4718592 | tf_op jit(solution)/shard_map/all_to_all | solution.py:832
  33.8 1.8 broadcast_multiply_fusion.tan
  35.6 4.7 %fusion.6 = bf16[1536,768]{1,0:T(8,128)(2,1)} fusion(bf16[1280,768]{1,0:T(8,128)(2,1)S(1)} %broadcast_multiply_fusion.tan, s32[1280]{0:T(1024)S(1)} %get-tuple-element.191), kind=kOutput, calls=%fused_computation.10 | convolution fusion | flops 3023044608 | bytes 4330496 | tf_op jit(solution)/shard_map/dot_general | solution.py:34
  40.9 7.2 %fusion.10 = (f32[3072,128]{1,0:T(8,128)}, f32[3072,128]{1,0:T(8,128)}) fusion(f32[128]{0:T(128)S(1)} %get-tuple-element.196, f32[128]{0:T(128)S(1)} %get-tuple-element.197, f32[3072]{0:T(1024)S(1)} %get-tuple-element.158, pred[128]{0:T(512)(128)(4,1)S(1)} %broadcast_compare_fusion.1), kind=kLoop, calls=%fused_computation.20 | loop fusion | flops 1572864 | bytes 3159168 | tf_op jit(solution)/shard_map/jit(_where)/select_n | solution.py:883
  48.1 57.1 %all-gather.3.cloned.1.call-done.weight_q.weight_k.weight_v.weight_out.weight = bf16[768,3328]{1,0:T(8,128)(2,1)} async-done(((bf16[24,3328]{1,0:T(8,128)(2,1)}), bf16[768,3328]{1,0:T(8,128)(2,1)}) %all-gather.3.cloned.1.call-update) | async-done | bytes 5111824 | tf_op jit(solution)/shard_map/all_gather | solution.py:717
  111.5 3.2 collective-permute-done.other
  114.8 66.3 %forward.1 = (bf16[3072,768]{1,0:T(8,128)(2,1)}, bf16[3072,384]{1,0:T(8,128)(2,1)}, bf16[3072,384]{1,0:T(8,128)(2,1)}, bf16[384,3072]{1,0:T(8,128)(2,1)}, bf16[3...) custom-call(s32[9,12]{1,0:T(8,128)} %stack.57.meta, ...), custom_call_target="tpu_custom_call" | custom-call | flops 74999996416 | bytes 41943040 | tf_op jit(solution)/shard_map/forward/pallas_call | solution.py:383
  181.3 3.1 all-to-all-start.2
  185.8 1.8 broadcast_select_fusion.1
  189.1 50.5 %feed_forward.1 = (f32[1280,768]{1,0:T(8,128)}, f32[1280,768]{1,0:T(8,128)}, bf16[768,6144]{1,0:T(8,128)(2,1)}, f32[4,1,768]{2,1,0:T(1,128)}, f32[8,768]{1,0:T(8,128)}) custom-call(bf16[1280,768]{1,0:T(8,128)(2,1)} %tok.4, bf16[1280,768]{1,0:T(8,128)(2,1)} %copy-done.6, f32[16,768]{1,0:T(8,128)} %copy-done.13, ...), custom_call_target="tpu_custom_call" | custom-call | flops 36238786560 | bytes 50331648 | tf_op jit(solution)/shard_map/feed_forward/pallas_call | solution.py:132
  243.8 5.9 %all-to-all-start.1 = ((bf16[32,48,768]{2,1,0:T(8,128)(2,1)}), bf16[32,48,768]{2,1,0:T(8,128)(2,1)}, u32[]{:S(2)}, u32[]{:S(2)}) async-start(bf16[32,48,768]{2,1,0:T(8,128)(2,1)} %bitcast.24), calls=%async_computation.1 | async-start | bytes 4718592 | tf_op jit(solution)/shard_map/all_to_all | solution.py:832
  251.8 92.1 %backward.1 = (bf16[3,512,768]{2,1,0:T(8,128)(2,1)}, bf16[3,512,768]{2,1,0:T(8,128)(2,1)}, bf16[384,768]{1,0:T(8,128)(2,1)}, bf16[3,768,384]{2,1,0:T(8,128)(2,1)...) custom-call(s32[9,12]{1,0:T(8,128)} %stack.57.meta, s32[6,1,512]{2,1,0:T(1,128)} %copy.172.places, ...), custom_call_target="tpu_custom_call" | custom-call | flops 89999998976 | bytes 41943040 | tf_op jit(solution)/shard_map/backward/pallas_call | solution.py:569
  352.3 2.3 add_convert_fusion
  356.2 5.1 %all-to-all-start.3 = ((bf16[32,48,768]{2,1,0:T(8,128)(2,1)}), bf16[32,48,768]{2,1,0:T(8,128)(2,1)}, u32[]{:S(2)}, u32[]{:S(2)}) async-start(bf16[32,48,768]{2,1,0:T(8,128)(2,1)} %bitcast.34), calls=%async_computation.3 | async-start | bytes 4718592 | tf_op jit(solution)/shard_map/all_to_all | solution.py:832
  363.9 2.2 maximum_select_fusion
  367.1 1.9 collective-permute-start.8
  370.6 10.1 %close.1 = bf16[1280,768]{1,0:T(8,128)(2,1)} custom-call(s32[1,1280]{1,0:T(1,128)} %fusion.63.place, bf16[1536,768]{1,0:T(8,128)(2,1)} %bitcast.25.moved, bf16[768,3328]{1,0:T(8,128)(2,1)} %all-gather.3.cloned.1.call-done.weight_q.weight_k.weight_v.weight_out.weight, f32[16,768]{1,0:T(8,128)} %copy-done.13, bf16[1280,768]{1,0:T(8,128)(2,1)} %tok.4, ...), custom_call_target="tpu_custom_call" | custom-call | flops 12000000000 | bytes 12582912 | tf_op jit(solution)/shard_map/close/pallas_call | solution.py:666
  380.7 19.8 %collective-permute-done.8 = bf16[4,2,56,768]{3,2,1,0:T(8,128)(2,1)S(1)} collective-permute-done((bf16[4,2,56,768]{3,2,1,0:T(8,128)(2,1)}, bf16[4,2,56,768]{3,2,1,0:T(8,128)(2,1)S(1)}, u32[]{:S(2)}, u32[]{:S(2)}) %collective-permute-start.8) | collective-permute-done | bytes 688160 | tf_op jit(solution)/shard_map/ppermute | solution.py:765
  402.0 3.0 collective-permute-start.9
  407.0 4.2 collective-permute-done.6
  414.0 6.5 %collective-permute-start.12 = (bf16[104,768]{1,0:T(8,128)(2,1)}, bf16[104,768]{1,0:T(8,128)(2,1)}, u32[]{:S(2)}, u32[]{:S(2)}) collective-permute-start(bf16[104,768]{1,0:T(8,128)(2,1)} %get-tuple-element.175), channel_id=1, source_target_pairs={{0,24},{1,25},{2,26},{3,27},{4,28},{5,29},{6,30},{7,31},{8,0},{9,1... | collective-permute-start | bytes 479240 | tf_op jit(solution)/shard_map/ppermute | solution.py:765
  430.0 6.3 %all-to-all-done.3 = bf16[32,48,768]{2,1,0:T(8,128)(2,1)} async-done(((bf16[32,48,768]{2,1,0:T(8,128)(2,1)}), bf16[32,48,768]{2,1,0:T(8,128)(2,1)}, u32[]{:S(2)}, u32[]{:S(2)}) %all-to-all-start.3) | async-done | bytes 2359328 | tf_op jit(solution)/shard_map/all_to_all | solution.py:832
  436.3 9.6 %finish.1 = bf16[1280,768]{1,0:T(8,128)(2,1)} custom-call(s32[1,1280]{1,0:T(1,128)} %fusion.63.place, bf16[1536,768]{1,0:T(8,128)(2,1)} %bitcast.35.moved, f32[16,768]{1,0:T(8,128)} %copy-done.13, bf16[1280,768]{1,0:T(8,128)(2,1)} %tok.4, f32[1280,768]{1,0:T(8,128)} %get-tuple-element.85.lower), custom_call_target="tpu_custom_call" | custom-call | flops 3019898880 | bytes 12582912 | tf_op jit(solution)/shard_map/finish/pallas_call | solution.py:696
  (263 shorter events, 61.4 us)
Async XLA Ops:
  7.2 24.5 %copy-start = (s32[24,3]{0,1:T(4,128)S(1)}, s32[24,3]{0,1:T(4,128)}, u32[]{:S(2)}) copy-start(s32[24,3]{0,1:T(4,128)} %param.23) | copy-start | bytes 868
  7.3 97.9 %all-gather.3.cloned.1.call-start = ((), (), s32[]{:S(2)}) async-start(), calls=%async_computation.5 | async-start | bytes 5271552 | tf_op jit(solution)/shard_map/all_gather | solution.py:717
  16.0 173.2 %all-gather.5.cloned.1.call-start = ((), (), s32[]{:S(2)}) async-start(), calls=%async_computation.6 | async-start | bytes 9732096 | tf_op jit(solution)/shard_map/all_gather | solution.py:717
  24.1 84.1 %all-to-all-start = ((bf16[32,48,768]{2,1,0:T(8,128)(2,1)}), bf16[32,48,768]{2,1,0:T(8,128)(2,1)S(1)}, u32[]{:S(2)}, u32[]{:S(2)}) async-start(bf16[32,48,768]{2,1,0:T(8,128)(2,1)} %bitcast.198), calls=%async_computation | async-start | bytes 4718592 | tf_op jit(solution)/shard_map/all_to_all | solution.py:832
  109.9 4.9 %collective-permute-start = (bf16[3,512,768]{2,1,0:T(8,128)(2,1)}, bf16[3,512,768]{2,1,0:T(8,128)(2,1)}, u32[]{:S(2)}, u32[]{:S(2)}) collective-permute-start(bf16[3,512,768]{2,1,0:T(8,128)(2,1)} %bitcast.18.own), channel_id=1, source_target_pairs={{0,1},{1,0},{2,3},{3,2},{4,5},{5,4},{6,7},{7,6},{8,9},{9,8},{10,11... | collective-permute-start | bytes 7077896 | tf_op jit(solution)/shard_map/ppermute | solution.py:752
  181.1 4.7 %collective-permute-start.1 = (bf16[3,512,384]{2,1,0:T(8,128)(2,1)}, bf16[3,512,384]{2,1,0:T(8,128)(2,1)}, u32[]{:S(2)}, u32[]{:S(2)}) collective-permute-start(bf16[3,512,384]{2,1,0:T(8,128)(2,1)} %get-tuple-element.65), channel_id=1, source_target_pairs={{0,1},{1,0},{2,3},{3,2},{4,5},{5,4},{6,7},{7,6},{8,9},{9,8},{10,11... | collective-permute-start | bytes 3538952 | tf_op jit(solution)/shard_map/ppermute | solution.py:752
  181.3 58.4 %all-to-all-start.2 = ((bf16[32,48,768]{2,1,0:T(8,128)(2,1)}), bf16[32,48,768]{2,1,0:T(8,128)(2,1)S(1)}, u32[]{:S(2)}, u32[]{:S(2)}) async-start(bf16[32,48,768]{2,1,0:T(8,128)(2,1)} %bitcast.199), calls=%async_computation.2 | async-start | bytes 4718592 | tf_op jit(solution)/shard_map/all_to_all | solution.py:832
  241.3 9.1 %collective-permute-start.2 = (bf16[3,512,768]{2,1,0:T(8,128)(2,1)}, bf16[3,512,768]{2,1,0:T(8,128)(2,1)S(1)}, u32[]{:S(2)}, u32[]{:S(2)}) collective-permute-start(bf16[3,512,768]{2,1,0:T(8,128)(2,1)} %bitcast.31.own), channel_id=1, source_target_pairs={{0,1},{1,0},{2,3},{3,2},{4,5},{5,4},{6,7},{7,6},{8,9},{9,8},{10,11... | collective-permute-start | bytes 7077896 | tf_op jit(solution)/shard_map/ppermute | solution.py:752
  243.8 112.4 %all-to-all-start.1 = ((bf16[32,48,768]{2,1,0:T(8,128)(2,1)}), bf16[32,48,768]{2,1,0:T(8,128)(2,1)}, u32[]{:S(2)}, u32[]{:S(2)}) async-start(bf16[32,48,768]{2,1,0:T(8,128)(2,1)} %bitcast.24), calls=%async_computation.1 | async-start | bytes 4718592 | tf_op jit(solution)/shard_map/all_to_all | solution.py:832
  249.7 171.4 %reduce-scatter.2.cloned.1.call-start = ((), (), s32[]{:S(2)}) async-start(), calls=%async_computation.7 | async-start | bytes 9732096 | tf_op jit(solution)/shard_map/reduce_scatter | solution.py:923
  251.8 92.4 %copy-start.16 = (f32[1280]{0:T(1024)S(1)}, f32[1280]{0:T(1024)}, u32[]{:S(2)}) copy-start(f32[1280]{0:T(1024)} %copy-done.15) | copy-start | bytes 15364
  251.8 93.2 %copy-start.22 = (f32[4,1,768]{2,1,0:T(1,128)S(1)}, f32[4,1,768]{2,1,0:T(1,128)}, u32[]{:S(2)}) copy-start(f32[4,1,768]{2,1,0:T(1,128)} %get-tuple-element.93) | copy-start | bytes 36868
  343.9 7.9 %collective-permute-start.3 = (bf16[3,512,768]{2,1,0:T(8,128)(2,1)}, bf16[3,512,768]{2,1,0:T(8,128)(2,1)}, u32[]{:S(2)}, u32[]{:S(2)}) collective-permute-start(bf16[3,512,768]{2,1,0:T(8,128)(2,1)} %get-tuple-element.81), channel_id=1, source_target_pairs={{0,1},{1,0},{2,3},{3,2},{4,5},{5,4},{6,7},{7,6},{8,9},{9,8},{10,11... | collective-permute-start | bytes 7077896 | tf_op jit(solution)/shard_map/ppermute | solution.py:752
  349.8 13.9 %collective-permute-start.7 = (bf16[16,32,768]{2,1,0:T(8,128)(2,1)}, bf16[16,32,768]{2,1,0:T(8,128)(2,1)S(1)}, u32[]{:S(2)}, u32[]{:S(2)}) collective-permute-start(bf16[16,32,768]{2,1,0:T(8,128)(2,1)} %dynamic-slice_bitcast_fusion.2), channel_id=1, source_target_pairs={{0,1},{1,0},{2,3},{3,2},{4,5},{5,4},{6,7},{7,6},{8,9},{9,8},{10,11... | collective-permute-start | bytes 2359304 | tf_op jit(solution)/shard_map/ppermute | solution.py:765
  351.5 12.4 %collective-permute-start.4 = (bf16[3,16,24,384]{3,2,1,0:T(8,128)(2,1)}, bf16[3,16,24,384]{3,2,1,0:T(8,128)(2,1)}, u32[]{:S(2)}, u32[]{:S(2)}) collective-permute-start(bf16[3,16,24,384]{3,2,1,0:T(8,128)(2,1)} %get-tuple-element.172), channel_id=1, source_target_pairs={{0,1},{1,0},{2,3},{3,2},{4,5},{5,4},{6,7},{7,6},{8,9},{9,8},{10,11... | collective-permute-start | bytes 2654216 | tf_op jit(solution)/shard_map/ppermute | solution.py:752
  356.2 80.2 %all-to-all-start.3 = ((bf16[32,48,768]{2,1,0:T(8,128)(2,1)}), bf16[32,48,768]{2,1,0:T(8,128)(2,1)}, u32[]{:S(2)}, u32[]{:S(2)}) async-start(bf16[32,48,768]{2,1,0:T(8,128)(2,1)} %bitcast.34), calls=%async_computation.3 | async-start | bytes 4718592 | tf_op jit(solution)/shard_map/all_to_all | solution.py:832
  367.1 33.3 %collective-permute-start.8 = (bf16[4,2,56,768]{3,2,1,0:T(8,128)(2,1)}, bf16[4,2,56,768]{3,2,1,0:T(8,128)(2,1)S(1)}, u32[]{:S(2)}, u32[]{:S(2)}) collective-permute-start(bf16[4,2,56,768]{3,2,1,0:T(8,128)(2,1)} %fusion.16), channel_id=1, source_target_pairs={{0,4},{1,5},{2,6},{3,7},{4,0},{5,1},{6,2},{7,3},{8,12},{9,13},{10,... | collective-permute-start | bytes 2064392 | tf_op jit(solution)/shard_map/ppermute | solution.py:765
  369.1 31.4 %collective-permute-start.5 = (bf16[4,2,48,768]{3,2,1,0:T(8,128)(2,1)S(1)}, bf16[4,2,48,768]{3,2,1,0:T(8,128)(2,1)}, u32[]{:S(2)}, u32[]{:S(2)}) collective-permute-start(bf16[4,2,48,768]{3,2,1,0:T(8,128)(2,1)S(1)} %fusion.21), channel_id=1, source_target_pairs={{0,2},{1,3},{2,0},{3,1},{4,6},{5,7},{6,4},{7,5},{8,10},{9,11},{10,... | collective-permute-start | bytes 1769480 | tf_op jit(solution)/shard_map/ppermute | solution.py:765
  401.7 9.5 %collective-permute-start.6 = (bf16[4,48,768]{2,1,0:T(8,128)(2,1)S(1)}, bf16[4,48,768]{2,1,0:T(8,128)(2,1)}, u32[]{:S(2)}, u32[]{:S(2)}) collective-permute-start(bf16[4,48,768]{2,1,0:T(8,128)(2,1)S(1)} %dynamic-slice_bitcast_fusion.4), channel_id=1, source_target_pairs={{0,4},{1,5},{2,6},{3,7},{4,0},{5,1},{6,2},{7,3},{8,12},{9,13},{10,... | collective-permute-start | bytes 884744 | tf_op jit(solution)/shard_map/ppermute | solution.py:765
  402.0 11.2 %collective-permute-start.9 = (bf16[4,56,768]{2,1,0:T(8,128)(2,1)S(1)}, bf16[4,56,768]{2,1,0:T(8,128)(2,1)S(1)}, u32[]{:S(2)}, u32[]{:S(2)}) collective-permute-start(bf16[4,56,768]{2,1,0:T(8,128)(2,1)S(1)} %dynamic-slice_bitcast_fusion.3), channel_id=1, source_target_pairs={{0,2},{1,3},{2,0},{3,1},{4,6},{5,7},{6,4},{7,5},{8,10},{9,11},{10,... | collective-permute-start | bytes 1032200 | tf_op jit(solution)/shard_map/ppermute | solution.py:765
  412.2 11.6 %copy-start.3 = (bf16[4,48,768]{2,1,0:T(8,128)(2,1)}, bf16[4,48,768]{2,1,0:T(8,128)(2,1)S(1)}, u32[]{:S(2)}) copy-start(bf16[4,48,768]{2,1,0:T(8,128)(2,1)S(1)} %fusion.24) | copy-start | bytes 884740
  414.0 31.9 %collective-permute-start.12 = (bf16[104,768]{1,0:T(8,128)(2,1)}, bf16[104,768]{1,0:T(8,128)(2,1)}, u32[]{:S(2)}, u32[]{:S(2)}) collective-permute-start(bf16[104,768]{1,0:T(8,128)(2,1)} %get-tuple-element.175), channel_id=1, source_target_pairs={{0,24},{1,25},{2,26},{3,27},{4,28},{5,29},{6,30},{7,31},{8,0},{9,1... | collective-permute-start | bytes 479240 | tf_op jit(solution)/shard_map/ppermute | solution.py:765
  420.5 25.4 %collective-permute-start.11 = (bf16[104,768]{1,0:T(8,128)(2,1)}, bf16[104,768]{1,0:T(8,128)(2,1)}, u32[]{:S(2)}, u32[]{:S(2)}) collective-permute-start(bf16[104,768]{1,0:T(8,128)(2,1)} %get-tuple-element.174), channel_id=1, source_target_pairs={{0,16},{1,17},{2,18},{3,19},{4,20},{5,21},{6,22},{7,23},{8,24},{9,... | collective-permute-start | bytes 479240 | tf_op jit(solution)/shard_map/ppermute | solution.py:765
  420.5 25.4 %collective-permute-start.10 = (bf16[104,768]{1,0:T(8,128)(2,1)}, bf16[104,768]{1,0:T(8,128)(2,1)}, u32[]{:S(2)}, u32[]{:S(2)}) collective-permute-start(bf16[104,768]{1,0:T(8,128)(2,1)} %get-tuple-element.173), channel_id=1, source_target_pairs={{0,8},{1,9},{2,10},{3,11},{4,12},{5,13},{6,14},{7,15},{8,16},{9,17... | collective-permute-start | bytes 479240 | tf_op jit(solution)/shard_map/ppermute | solution.py:765
  (35 other events, 163.2 us)
Sparse Core Ops, SparseCore 0:
  16.1 89.1 all-gather.2
  108.7 79.5 all-gather.4
  256.4 162.0 reduce-scatter.1

commit v5 on v4

--- a/solution.py
+++ b/solution.py
@@ -111,9 +111,8 @@
     def _():
         def one(i, carry):
             r = pl.ds(pl.multiple_of(i * BLK, BLK), BLK)
-            scaled, factor = norm_stats(tok[r, :].astype(single))
+            scaled, _ = norm_stats(tok[r, :].astype(single))
             upper, wide = lower[r, :], tan[r, :].astype(single)
-            lower[r, :] = wide + lower_norm(upper, scaled, factor, lines[2:3, :])
             terms = (upper * scaled, upper, wide)
             return tuple(c + jnp.sum(t, 0, keepdims=True) for c, t in zip(carry, terms))
 
@@ -654,13 +653,17 @@
     return dot(jnp.where(column(place[...]) == lane, 1.0, 0.0).astype(bfloat), moved[...])
 
 
-def close_kernel(place, moved, weight, lines, tok, feed, out):
+def close_kernel(place, moved, weight, lines, tok, tan, feed, feed_back, out, lower):
     context = placed_rows(place, moved).astype(bfloat)
     attended = dot(context, weight[...]) + lines[4:5, :]
-    out[...] = (tok[...].astype(single) + attended + (feed[...] + lines[5:6, :])).astype(bfloat)
-
-
-def close(place, moved, weights, lines, tok, feed):
+    rows = tok[...].astype(single)
+    out[...] = (rows + attended + (feed[...] + lines[5:6, :])).astype(bfloat)
+    scaled, factor = norm_stats(rows)
+    second = lower_norm(feed_back[...], scaled, factor, lines[2:3, :])
+    lower[...] = tan[...].astype(single) + second
+
+
+def close(place, moved, weights, lines, tok, tan, feed, feed_back):
     rows = tok.shape[0]
     tall = lambda width: pl.BlockSpec((BLK, width), lambda i: (i, 0))
     return pl.pallas_call(
@@ -673,15 +676,20 @@
             whole((16, D)),
             tall(D),
             tall(D),
+            tall(D),
+            tall(D),
         ],
-        out_specs=tall(D),
-        out_shape=jax.ShapeDtypeStruct((rows, D), bfloat),
+        out_specs=[tall(D), tall(D)],
+        out_shape=[
+            jax.ShapeDtypeStruct((rows, D), bfloat),
+            jax.ShapeDtypeStruct((rows, D), single),
+        ],
         compiler_params=params(60),
         cost_estimate=pl.CostEstimate(
             flops=12 * 10**9, bytes_accessed=12 * MIB, transcendentals=0
         ),
         name="close",
-    )(place, moved, weights, lines, tok, feed)
+    )(place, moved, weights, lines, tok, tan, feed, feed_back)
 
 
 def finish_kernel(place, moved, lines, tok, lower, out):
@@ -917,7 +925,7 @@
     context_out = jnp.concatenate(
         [jnp.where(core == 0, mine, theirs), jnp.where(core == 0, theirs, mine)], -1
     )
-    feed, lower_two, wide, up_add_grad, sums = feed_forward(
+    feed, feed_back, wide, up_add_grad, sums = feed_forward(
         after(tokens, context_out), tangent, lines, feed_weights, up_add
     )
     wide_sum = lax.psum_scatter(wide, "dp", scatter_dimension=0, tiled=True).astype(single)
@@ -952,8 +960,15 @@
         project_parts
     )
 
-    block_out = close(
-        place_line, after(context_moved, lower_sum), first_all, lines, tokens, feed
+    block_out, lower_two = close(
+        place_line,
+        after(context_moved, lower_sum),
+        first_all,
+        lines,
+        tokens,
+        tangent,
+        feed,
+        feed_back,
     )
 
     def pair_up(one, two):

time: 465 us -> 464 us (level)
  transfers between devices with their start and end apart: 20 -> 20, of which waited for: 7 -> 8; matrix products, arithmetic and copies ran while one was open for 14% -> 14% of each run, Pallas kernels for 50% -> 50%
where the time goes in v5:
time: 464 us; the launch traced here: 458 us
  Pallas kernels  230 us (50%)
  waiting for transfers between devices  91.3 us (20%)
  starting transfers between devices  36.3 us (8%)
  local copies, waits for them, and re-layouts  35.6 us (8%)
  other arithmetic  32.9 us (7%)
  between operations  19.1 us (4%)
  matrix products  12.7 us (3%)
    pallas_call x1, Pallas kernels, backward(): pl.pallas_call(backward_kernel, grid_spec=pltpu.PrefetchScalarGridSpec(nu...  92.2 us
    pallas_call x1, Pallas kernels, forward(): pl.pallas_call(forward_kernel, grid_spec=pltpu.PrefetchScalarGridSpec(num...  66.3 us
    all_gather x2, waiting for transfers between devices, gather_all(): return lax.all_gather(x, 'dp', axis=0, tiled=True)  57 us
    pallas_call x1, Pallas kernels, feed_forward(): pl.pallas_call(feed_kernel, grid=(count,), in_specs=[one((rows, D)), one(...  49.2 us
    ppermute x8, waiting for transfers between devices, shifted(): return lax.ppermute(x, 'dp', hop)  22.7 us
    all_to_all x4, starting transfers between devices, swap_all(): return lax.all_to_all(x, 'dp', split_axis=0, concat_axis=0, tiled=True)  21.2 us
    ppermute x8, starting transfers between devices, shifted(): return lax.ppermute(x, 'dp', hop)  13.9 us
    dot_general x3, matrix products, dot(): return jnp.dot(left, right, preferred_element_type=single)  12.7 us
  transfers between devices with their start and end apart: 20, of which 8 were waited for; matrix products, arithmetic and copies ran while one was open for 14% of the time, Pallas kernels for 50%

profile of v5, /device:TPU:0, one launch (start us, length us, event | category | flops | bytes accessed | tf_op | source)
XLA Modules:
  0.0 457.8 jit_solution(8950671129849253985)
XLA Ops:
  16.0 6.3 %fusion.5 = bf16[1536,768]{1,0:T(8,128)(2,1)} fusion(bf16[1280,768]{1,0:T(8,128)(2,1)} %tok.4, s32[1280]{0:T(1024)S(1)} %get-tuple-element.195), kind=kOutput, calls=%fused_computation.9 | convolution fusion | flops 3023044608 | bytes 4330496 | tf_op jit(solution)/shard_map/dot_general | solution.py:34
  24.1 7.5 %all-to-all-start = ((bf16[32,48,768]{2,1,0:T(8,128)(2,1)}), bf16[32,48,768]{2,1,0:T(8,128)(2,1)S(1)}, u32[]{:S(2)}, u32[]{:S(2)}) async-start(bf16[32,48,768]{2,1,0:T(8,128)(2,1)} %bitcast.198), calls=%async_computation | async-start | bytes 4718592 | tf_op jit(solution)/shard_map/all_to_all | solution.py:840
  33.8 1.8 broadcast_multiply_fusion.tan
  35.6 4.8 %fusion.6 = bf16[1536,768]{1,0:T(8,128)(2,1)} fusion(bf16[1280,768]{1,0:T(8,128)(2,1)S(1)} %broadcast_multiply_fusion.tan, s32[1280]{0:T(1024)S(1)} %get-tuple-element.195), kind=kOutput, calls=%fused_computation.10 | convolution fusion | flops 3023044608 | bytes 4330496 | tf_op jit(solution)/shard_map/dot_general | solution.py:34
  41.0 7.2 %fusion.10 = (f32[3072,128]{1,0:T(8,128)}, f32[3072,128]{1,0:T(8,128)}) fusion(f32[128]{0:T(128)S(1)} %get-tuple-element.200, f32[128]{0:T(128)S(1)} %get-tuple-element.201, f32[3072]{0:T(1024)S(1)} %get-tuple-element.162, pred[128]{0:T(512)(128)(4,1)S(1)} %broadcast_compare_fusion.1), kind=kLoop, calls=%fused_computation.20 | loop fusion | flops 1572864 | bytes 3159168 | tf_op jit(solution)/shard_map/jit(_where)/select_n | solution.py:891
  48.2 57.0 %all-gather.3.cloned.1.call-done.weight_q.weight_k.weight_v.weight_out.weight = bf16[768,3328]{1,0:T(8,128)(2,1)} async-done(((bf16[24,3328]{1,0:T(8,128)(2,1)}), bf16[768,3328]{1,0:T(8,128)(2,1)}) %all-gather.3.cloned.1.call-update) | async-done | bytes 5111824 | tf_op jit(solution)/shard_map/all_gather | solution.py:725
  111.5 3.3 collective-permute-done.other
  114.7 66.3 %forward.1 = (bf16[3072,768]{1,0:T(8,128)(2,1)}, bf16[3072,384]{1,0:T(8,128)(2,1)}, bf16[3072,384]{1,0:T(8,128)(2,1)}, bf16[384,3072]{1,0:T(8,128)(2,1)}, bf16[3...) custom-call(s32[9,12]{1,0:T(8,128)} %stack.57.meta, ...), custom_call_target="tpu_custom_call" | custom-call | flops 74999996416 | bytes 41943040 | tf_op jit(solution)/shard_map/forward/pallas_call | solution.py:382
  181.3 3.1 all-to-all-start.2
  185.8 1.8 broadcast_select_fusion.1
  189.1 49.2 %feed_forward.1 = (f32[1280,768]{1,0:T(8,128)}, f32[1280,768]{1,0:T(8,128)}, bf16[768,6144]{1,0:T(8,128)(2,1)}, f32[4,1,768]{2,1,0:T(1,128)}, f32[8,768]{1,0:T(8,128)}) custom-call(bf16[1280,768]{1,0:T(8,128)(2,1)} %tok.4, bf16[1280,768]{1,0:T(8,128)(2,1)} %copy-done.6, f32[16,768]{1,0:T(8,128)} %copy-done.13, ...), custom_call_target="tpu_custom_call" | custom-call | flops 36238786560 | bytes 50331648 | tf_op jit(solution)/shard_map/feed_forward/pallas_call | solution.py:131
  242.9 5.4 %all-to-all-start.1 = ((bf16[32,48,768]{2,1,0:T(8,128)(2,1)}), bf16[32,48,768]{2,1,0:T(8,128)(2,1)}, u32[]{:S(2)}, u32[]{:S(2)}) async-start(bf16[32,48,768]{2,1,0:T(8,128)(2,1)} %bitcast.24), calls=%async_computation.1 | async-start | bytes 4718592 | tf_op jit(solution)/shard_map/all_to_all | solution.py:840
  250.5 92.2 %backward.1 = (bf16[3,512,768]{2,1,0:T(8,128)(2,1)}, bf16[3,512,768]{2,1,0:T(8,128)(2,1)}, bf16[384,768]{1,0:T(8,128)(2,1)}, bf16[3,768,384]{2,1,0:T(8,128)(2,1)...) custom-call(s32[9,12]{1,0:T(8,128)} %stack.57.meta, s32[6,1,512]{2,1,0:T(1,128)} %copy.172.places, ...), custom_call_target="tpu_custom_call" | custom-call | flops 89999998976 | bytes 41943040 | tf_op jit(solution)/shard_map/backward/pallas_call | solution.py:568
  351.0 2.3 add_convert_fusion
  354.9 5.1 %all-to-all-start.3 = ((bf16[32,48,768]{2,1,0:T(8,128)(2,1)}), bf16[32,48,768]{2,1,0:T(8,128)(2,1)}, u32[]{:S(2)}, u32[]{:S(2)}) async-start(bf16[32,48,768]{2,1,0:T(8,128)(2,1)} %bitcast.34), calls=%async_computation.3 | async-start | bytes 4718592 | tf_op jit(solution)/shard_map/all_to_all | solution.py:840
  362.6 2.0 maximum_select_fusion
  365.6 1.9 collective-permute-start.8
  369.1 12.4 %close.1 = (bf16[1280,768]{1,0:T(8,128)(2,1)}, f32[1280,768]{1,0:T(8,128)}) custom-call(s32[1,1280]{1,0:T(1,128)} %fusion.63.place, bf16[1536,768]{1,0:T(8,128)(2,1)} %bitcast.25.moved, bf16[768,3328]{1,0:T(8,128)(2,1)} %all-gather.3.cloned.1.call-done.weight_q.weight_k.weight_v.weight_out.weight, f32[16,768]{1,0:T(8,128)} %copy-done.13, ...), custom_call_target="tpu_custom_call" | custom-call | flops 12000000000 | bytes 12582912 | tf_op jit(solution)/shard_map/close/pallas_call | solution.py:669
  381.5 17.5 %collective-permute-done.8 = bf16[4,2,56,768]{3,2,1,0:T(8,128)(2,1)S(1)} collective-permute-done((bf16[4,2,56,768]{3,2,1,0:T(8,128)(2,1)}, bf16[4,2,56,768]{3,2,1,0:T(8,128)(2,1)S(1)}, u32[]{:S(2)}, u32[]{:S(2)}) %collective-permute-start.8) | collective-permute-done | bytes 688160 | tf_op jit(solution)/shard_map/ppermute | solution.py:773
  400.6 3.0 collective-permute-start.9
  405.6 4.2 collective-permute-done.6
  412.7 6.5 %collective-permute-start.12 = (bf16[104,768]{1,0:T(8,128)(2,1)}, bf16[104,768]{1,0:T(8,128)(2,1)}, u32[]{:S(2)}, u32[]{:S(2)}) collective-permute-start(bf16[104,768]{1,0:T(8,128)(2,1)} %get-tuple-element.179), channel_id=1, source_target_pairs={{0,24},{1,25},{2,26},{3,27},{4,28},{5,29},{6,30},{7,31},{8,0},{9,1... | collective-permute-start | bytes 479240 | tf_op jit(solution)/shard_map/ppermute | solution.py:773
  428.7 6.3 %all-to-all-done.3 = bf16[32,48,768]{2,1,0:T(8,128)(2,1)} async-done(((bf16[32,48,768]{2,1,0:T(8,128)(2,1)}), bf16[32,48,768]{2,1,0:T(8,128)(2,1)}, u32[]{:S(2)}, u32[]{:S(2)}) %all-to-all-start.3) | async-done | bytes 2359328 | tf_op jit(solution)/shard_map/all_to_all | solution.py:840
  435.0 9.6 %finish.1 = bf16[1280,768]{1,0:T(8,128)(2,1)} custom-call(s32[1,1280]{1,0:T(1,128)} %fusion.63.place, bf16[1536,768]{1,0:T(8,128)(2,1)} %bitcast.35.moved, f32[16,768]{1,0:T(8,128)} %copy-done.13, bf16[1280,768]{1,0:T(8,128)(2,1)} %tok.4, f32[1280,768]{1,0:T(8,128)} %get-tuple-element.89.lower), custom_call_target="tpu_custom_call" | custom-call | flops 3019898880 | bytes 12582912 | tf_op jit(solution)/shard_map/finish/pallas_call | solution.py:704
  (263 shorter events, 62.0 us)
Async XLA Ops:
  7.2 24.5 %copy-start = (s32[24,3]{0,1:T(4,128)S(1)}, s32[24,3]{0,1:T(4,128)}, u32[]{:S(2)}) copy-start(s32[24,3]{0,1:T(4,128)} %param.23) | copy-start | bytes 868
  7.3 97.9 %all-gather.3.cloned.1.call-start = ((), (), s32[]{:S(2)}) async-start(), calls=%async_computation.5 | async-start | bytes 5271552 | tf_op jit(solution)/shard_map/all_gather | solution.py:725
  15.9 173.2 %all-gather.5.cloned.1.call-start = ((), (), s32[]{:S(2)}) async-start(), calls=%async_computation.6 | async-start | bytes 9732096 | tf_op jit(solution)/shard_map/all_gather | solution.py:725
  24.1 84.1 %all-to-all-start = ((bf16[32,48,768]{2,1,0:T(8,128)(2,1)}), bf16[32,48,768]{2,1,0:T(8,128)(2,1)S(1)}, u32[]{:S(2)}, u32[]{:S(2)}) async-start(bf16[32,48,768]{2,1,0:T(8,128)(2,1)} %bitcast.198), calls=%async_computation | async-start | bytes 4718592 | tf_op jit(solution)/shard_map/all_to_all | solution.py:840
  109.8 4.9 %collective-permute-start = (bf16[3,512,768]{2,1,0:T(8,128)(2,1)}, bf16[3,512,768]{2,1,0:T(8,128)(2,1)}, u32[]{:S(2)}, u32[]{:S(2)}) collective-permute-start(bf16[3,512,768]{2,1,0:T(8,128)(2,1)} %bitcast.18.own), channel_id=1, source_target_pairs={{0,1},{1,0},{2,3},{3,2},{4,5},{5,4},{6,7},{7,6},{8,9},{9,8},{10,11... | collective-permute-start | bytes 7077896 | tf_op jit(solution)/shard_map/ppermute | solution.py:760
  181.1 4.7 %collective-permute-start.1 = (bf16[3,512,384]{2,1,0:T(8,128)(2,1)}, bf16[3,512,384]{2,1,0:T(8,128)(2,1)}, u32[]{:S(2)}, u32[]{:S(2)}) collective-permute-start(bf16[3,512,384]{2,1,0:T(8,128)(2,1)} %get-tuple-element.67), channel_id=1, source_target_pairs={{0,1},{1,0},{2,3},{3,2},{4,5},{5,4},{6,7},{7,6},{8,9},{9,8},{10,11... | collective-permute-start | bytes 3538952 | tf_op jit(solution)/shard_map/ppermute | solution.py:760
  181.3 57.5 %all-to-all-start.2 = ((bf16[32,48,768]{2,1,0:T(8,128)(2,1)}), bf16[32,48,768]{2,1,0:T(8,128)(2,1)S(1)}, u32[]{:S(2)}, u32[]{:S(2)}) async-start(bf16[32,48,768]{2,1,0:T(8,128)(2,1)} %bitcast.199), calls=%async_computation.2 | async-start | bytes 4718592 | tf_op jit(solution)/shard_map/all_to_all | solution.py:840
  240.4 8.6 %collective-permute-start.2 = (bf16[3,512,768]{2,1,0:T(8,128)(2,1)}, bf16[3,512,768]{2,1,0:T(8,128)(2,1)S(1)}, u32[]{:S(2)}, u32[]{:S(2)}) collective-permute-start(bf16[3,512,768]{2,1,0:T(8,128)(2,1)} %bitcast.31.own), channel_id=1, source_target_pairs={{0,1},{1,0},{2,3},{3,2},{4,5},{5,4},{6,7},{7,6},{8,9},{9,8},{10,11... | collective-permute-start | bytes 7077896 | tf_op jit(solution)/shard_map/ppermute | solution.py:760
  242.9 112.0 %all-to-all-start.1 = ((bf16[32,48,768]{2,1,0:T(8,128)(2,1)}), bf16[32,48,768]{2,1,0:T(8,128)(2,1)}, u32[]{:S(2)}, u32[]{:S(2)}) async-start(bf16[32,48,768]{2,1,0:T(8,128)(2,1)} %bitcast.24), calls=%async_computation.1 | async-start | bytes 4718592 | tf_op jit(solution)/shard_map/all_to_all | solution.py:840
  248.3 171.5 %reduce-scatter.2.cloned.1.call-start = ((), (), s32[]{:S(2)}) async-start(), calls=%async_computation.7 | async-start | bytes 9732096 | tf_op jit(solution)/shard_map/reduce_scatter | solution.py:931
  250.5 92.4 %copy-start.16 = (f32[1280]{0:T(1024)S(1)}, f32[1280]{0:T(1024)}, u32[]{:S(2)}) copy-start(f32[1280]{0:T(1024)} %copy-done.15) | copy-start | bytes 15364
  250.5 93.3 %copy-start.22 = (f32[4,1,768]{2,1,0:T(1,128)S(1)}, f32[4,1,768]{2,1,0:T(1,128)}, u32[]{:S(2)}) copy-start(f32[4,1,768]{2,1,0:T(1,128)} %get-tuple-element.97) | copy-start | bytes 36868
  342.6 7.9 %collective-permute-start.3 = (bf16[3,512,768]{2,1,0:T(8,128)(2,1)}, bf16[3,512,768]{2,1,0:T(8,128)(2,1)}, u32[]{:S(2)}, u32[]{:S(2)}) collective-permute-start(bf16[3,512,768]{2,1,0:T(8,128)(2,1)} %get-tuple-element.83), channel_id=1, source_target_pairs={{0,1},{1,0},{2,3},{3,2},{4,5},{5,4},{6,7},{7,6},{8,9},{9,8},{10,11... | collective-permute-start | bytes 7077896 | tf_op jit(solution)/shard_map/ppermute | solution.py:760
  348.5 13.9 %collective-permute-start.7 = (bf16[16,32,768]{2,1,0:T(8,128)(2,1)}, bf16[16,32,768]{2,1,0:T(8,128)(2,1)S(1)}, u32[]{:S(2)}, u32[]{:S(2)}) collective-permute-start(bf16[16,32,768]{2,1,0:T(8,128)(2,1)} %dynamic-slice_bitcast_fusion.2), channel_id=1, source_target_pairs={{0,1},{1,0},{2,3},{3,2},{4,5},{5,4},{6,7},{7,6},{8,9},{9,8},{10,11... | collective-permute-start | bytes 2359304 | tf_op jit(solution)/shard_map/ppermute | solution.py:773
  350.2 12.5 %collective-permute-start.4 = (bf16[3,16,24,384]{3,2,1,0:T(8,128)(2,1)}, bf16[3,16,24,384]{3,2,1,0:T(8,128)(2,1)}, u32[]{:S(2)}, u32[]{:S(2)}) collective-permute-start(bf16[3,16,24,384]{3,2,1,0:T(8,128)(2,1)} %get-tuple-element.176), channel_id=1, source_target_pairs={{0,1},{1,0},{2,3},{3,2},{4,5},{5,4},{6,7},{7,6},{8,9},{9,8},{10,11... | collective-permute-start | bytes 2654216 | tf_op jit(solution)/shard_map/ppermute | solution.py:760
  354.9 80.0 %all-to-all-start.3 = ((bf16[32,48,768]{2,1,0:T(8,128)(2,1)}), bf16[32,48,768]{2,1,0:T(8,128)(2,1)}, u32[]{:S(2)}, u32[]{:S(2)}) async-start(bf16[32,48,768]{2,1,0:T(8,128)(2,1)} %bitcast.34), calls=%async_computation.3 | async-start | bytes 4718592 | tf_op jit(solution)/shard_map/all_to_all | solution.py:840
  365.6 33.4 %collective-permute-start.8 = (bf16[4,2,56,768]{3,2,1,0:T(8,128)(2,1)}, bf16[4,2,56,768]{3,2,1,0:T(8,128)(2,1)S(1)}, u32[]{:S(2)}, u32[]{:S(2)}) collective-permute-start(bf16[4,2,56,768]{3,2,1,0:T(8,128)(2,1)} %fusion.16), channel_id=1, source_target_pairs={{0,4},{1,5},{2,6},{3,7},{4,0},{5,1},{6,2},{7,3},{8,12},{9,13},{10,... | collective-permute-start | bytes 2064392 | tf_op jit(solution)/shard_map/ppermute | solution.py:773
  367.6 31.5 %collective-permute-start.5 = (bf16[4,2,48,768]{3,2,1,0:T(8,128)(2,1)S(1)}, bf16[4,2,48,768]{3,2,1,0:T(8,128)(2,1)}, u32[]{:S(2)}, u32[]{:S(2)}) collective-permute-start(bf16[4,2,48,768]{3,2,1,0:T(8,128)(2,1)S(1)} %fusion.21), channel_id=1, source_target_pairs={{0,2},{1,3},{2,0},{3,1},{4,6},{5,7},{6,4},{7,5},{8,10},{9,11},{10,... | collective-permute-start | bytes 1769480 | tf_op jit(solution)/shard_map/ppermute | solution.py:773
  400.3 9.5 %collective-permute-start.6 = (bf16[4,48,768]{2,1,0:T(8,128)(2,1)S(1)}, bf16[4,48,768]{2,1,0:T(8,128)(2,1)}, u32[]{:S(2)}, u32[]{:S(2)}) collective-permute-start(bf16[4,48,768]{2,1,0:T(8,128)(2,1)S(1)} %dynamic-slice_bitcast_fusion.4), channel_id=1, source_target_pairs={{0,4},{1,5},{2,6},{3,7},{4,0},{5,1},{6,2},{7,3},{8,12},{9,13},{10,... | collective-permute-start | bytes 884744 | tf_op jit(solution)/shard_map/ppermute | solution.py:773
  400.6 11.2 %collective-permute-start.9 = (bf16[4,56,768]{2,1,0:T(8,128)(2,1)S(1)}, bf16[4,56,768]{2,1,0:T(8,128)(2,1)S(1)}, u32[]{:S(2)}, u32[]{:S(2)}) collective-permute-start(bf16[4,56,768]{2,1,0:T(8,128)(2,1)S(1)} %dynamic-slice_bitcast_fusion.3), channel_id=1, source_target_pairs={{0,2},{1,3},{2,0},{3,1},{4,6},{5,7},{6,4},{7,5},{8,10},{9,11},{10,... | collective-permute-start | bytes 1032200 | tf_op jit(solution)/shard_map/ppermute | solution.py:773
  410.9 11.6 %copy-start.3 = (bf16[4,48,768]{2,1,0:T(8,128)(2,1)}, bf16[4,48,768]{2,1,0:T(8,128)(2,1)S(1)}, u32[]{:S(2)}) copy-start(bf16[4,48,768]{2,1,0:T(8,128)(2,1)S(1)} %fusion.24) | copy-start | bytes 884740
  412.7 31.9 %collective-permute-start.12 = (bf16[104,768]{1,0:T(8,128)(2,1)}, bf16[104,768]{1,0:T(8,128)(2,1)}, u32[]{:S(2)}, u32[]{:S(2)}) collective-permute-start(bf16[104,768]{1,0:T(8,128)(2,1)} %get-tuple-element.179), channel_id=1, source_target_pairs={{0,24},{1,25},{2,26},{3,27},{4,28},{5,29},{6,30},{7,31},{8,0},{9,1... | collective-permute-start | bytes 479240 | tf_op jit(solution)/shard_map/ppermute | solution.py:773
  419.2 25.4 %collective-permute-start.11 = (bf16[104,768]{1,0:T(8,128)(2,1)}, bf16[104,768]{1,0:T(8,128)(2,1)}, u32[]{:S(2)}, u32[]{:S(2)}) collective-permute-start(bf16[104,768]{1,0:T(8,128)(2,1)} %get-tuple-element.178), channel_id=1, source_target_pairs={{0,16},{1,17},{2,18},{3,19},{4,20},{5,21},{6,22},{7,23},{8,24},{9,... | collective-permute-start | bytes 479240 | tf_op jit(solution)/shard_map/ppermute | solution.py:773
  419.2 25.4 %collective-permute-start.10 = (bf16[104,768]{1,0:T(8,128)(2,1)}, bf16[104,768]{1,0:T(8,128)(2,1)}, u32[]{:S(2)}, u32[]{:S(2)}) collective-permute-start(bf16[104,768]{1,0:T(8,128)(2,1)} %get-tuple-element.177), channel_id=1, source_target_pairs={{0,8},{1,9},{2,10},{3,11},{4,12},{5,13},{6,14},{7,15},{8,16},{9,17... | collective-permute-start | bytes 479240 | tf_op jit(solution)/shard_map/ppermute | solution.py:773
  (35 other events, 163.2 us)
Sparse Core Ops, SparseCore 0:
  16.0 89.1 all-gather.2
  108.7 79.5 all-gather.4
  255.0 162.1 reduce-scatter.1
